TPU v7x, 32 devices: a whole 2x2x4 slice. The times are simulated.
32 devices in a mesh: grp: 1, gx: 16 (over z, y, x), gy: 2 (over core).
Axes of the slice: x: 2, y: 2, z: 4, core: 2. Of those that a mesh axis runs over, the one named last changes fastest.
Arguments:
- log_conf: bfloat16 [6, 64, 512, 128], P(None, ('grp', 'gx'), 'gy'), may hold values from -3 to 3
- brownian: bfloat16 [6, 64, 512, 128], P(None, ('grp', 'gx'), 'gy'), may hold values from -6 to 6
- relax_rate: bfloat16 [64, 512, 128], P(('grp', 'gx'), 'gy'), may hold values from 0.5 to 5
- kernel: float32 [6, 5, 5, 5], replicated, may hold values from -0.5 to 0.5
Outputs:
- downsampled_stress: float32 [6, 32, 16, 128], P(None, ('gx', 'gy'), 'grp')
All inputs are finite; a program needn't handle non-finite values.
Results may differ from a plain program's by a relative error of at most 0.0003.
Values may be sent and summed in bfloat16 or wider, within the bound.
No kernel may reach another device: no remote copies, remote signals or barrier semaphores. Data moves between devices by JAX's collectives and lax.ppermute only.
A program may use at most 128 MiB of HBM per device.

v0:
```python
import jax
import jax.numpy as jnp
from jax import lax
from jax.sharding import PartitionSpec as P

DIFFUSE = 0.12
RELAX_STEP = 0.1
NOISE_AMP = 0.3


def padded_2(block, sides, width):
    for axis, dim in sides:
        count = lax.axis_size(axis)
        forward = [(i, i + 1) for i in range(count - 1)]
        backward = [(target, source) for source, target in forward]
        low = lax.ppermute(
            lax.slice_in_dim(block, block.shape[dim] - width, None, axis=dim), axis, forward
        )
        high = lax.ppermute(lax.slice_in_dim(block, 0, width, axis=dim), axis, backward)
        block = jnp.concatenate([low, block, high], axis=dim)
    return block


def shifted(block, axis, distance):
    devices = range(lax.axis_size(axis))
    route = [(i - distance, i) for i in devices if i - distance in devices]
    return lax.ppermute(block, axis, route)


def window(padded, axis, start):
    result = padded
    for dim in (1, 2, 3):
        length = padded.shape[dim] - 4
        begin = start if dim == axis else 2
        result = lax.slice_in_dim(result, begin, begin + length, axis=dim)
    return result


def diffusion_operator(padded):
    total = jnp.zeros_like(window(padded, 1, 2))
    for axis in (1, 2, 3):
        total = (
            total
            + (
                -window(padded, axis, 0)
                + 16.0 * window(padded, axis, 1)
                - 30.0 * window(padded, axis, 2)
                + 16.0 * window(padded, axis, 3)
                - window(padded, axis, 4)
            )
            / 12.0
        )
    return total


def second_order(field):
    comp_xx, comp_xy, comp_xz, comp_yy, comp_yz, comp_zz = [
        field[comp_index] for comp_index in range(6)
    ]
    squared_values = jnp.stack(
        [
            comp_xx * comp_xx + comp_xy * comp_xy + comp_xz * comp_xz,
            comp_xx * comp_xy + comp_xy * comp_yy + comp_xz * comp_yz,
            comp_xx * comp_xz + comp_xy * comp_yz + comp_xz * comp_zz,
            comp_xy * comp_xy + comp_yy * comp_yy + comp_yz * comp_yz,
            comp_xy * comp_xz + comp_yy * comp_yz + comp_yz * comp_zz,
            comp_xz * comp_xz + comp_yz * comp_yz + comp_zz * comp_zz,
        ]
    )
    return field + 0.5 * squared_values


def update(extended, forcing, rates):
    padded = jnp.pad(extended.astype(jnp.float32), ((0, 0), (0, 0), (0, 0), (2, 2)))
    center = window(padded, 1, 2)
    lap = diffusion_operator(padded)
    updated = (
        center
        + DIFFUSE * lap
        - RELAX_STEP * rates.astype(jnp.float32)[None] * center
        + NOISE_AMP * forcing.astype(jnp.float32)
    )
    return second_order(updated)


def restrict(stress_full, kernel, downsampled_xaxis, taps_x):
    comps = stress_full.shape[0]
    downsampled_yaxis = (stress_full.shape[2] - 2) // 4
    depth = stress_full.shape[3]
    coarse_z = depth // 4
    zpos = lax.broadcasted_iota(jnp.int32, (5, depth, coarse_z), 1)
    kpos = lax.broadcasted_iota(jnp.int32, (5, depth, coarse_z), 2)
    taps = lax.broadcasted_iota(jnp.int32, (5, depth, coarse_z), 0)
    selector = (zpos - 4 * kpos + 2 == taps).astype(jnp.float32)
    band = jnp.einsum("cabe,ezk->cabzk", kernel, selector, precision=lax.Precision.HIGHEST)
    total = jnp.zeros((comps, downsampled_xaxis, downsampled_yaxis, coarse_z), jnp.float32)
    for shift_x in taps_x:
        for shift_y in range(5):
            piece = lax.slice(
                stress_full,
                (0, shift_x, shift_y, 0),
                (
                    comps,
                    shift_x + 4 * (downsampled_xaxis - 1) + 1,
                    shift_y + 4 * (downsampled_yaxis - 1) + 1,
                    depth,
                ),
                (1, 4, 4, 1),
            )
            total = total + jnp.einsum(
                "cxyz,czk->cxyk", piece, band[:, shift_x, shift_y], precision=lax.Precision.HIGHEST
            )
    return total


def local(log_conf, brownian, relax_rate, kernel):
    comps = log_conf.shape[0]
    extended = padded_2(log_conf, (("gx", 1), ("gy", 2)), 2)
    stress = update(extended, brownian, relax_rate)
    lower_rows = shifted(stress[:, -2:], "gx", 1)
    stress_rows = jnp.concatenate([lower_rows, stress], axis=1)
    lower_cols = shifted(stress_rows[:, :, -2:], "gy", 1)
    stress_full = jnp.concatenate([lower_cols, stress_rows], axis=2)
    downsampled = restrict(stress_full, kernel, (stress_full.shape[1] - 2) // 4, range(5))
    slab_partitioned = jnp.transpose(downsampled, (0, 3, 1, 2))
    width_gx = lax.axis_size("gx")
    width_gy = lax.axis_size("gy")
    downsampled_xaxis = slab_partitioned.shape[2]
    downsampled_yaxis = slab_partitioned.shape[3]
    margin_extended = slab_partitioned[:, None]
    moved = lax.all_to_all(margin_extended, ("gx", "gy"), split_axis=2, concat_axis=1, tiled=True)
    planes = moved.shape[2]
    moved = moved.reshape(comps, width_gx, width_gy, planes, downsampled_xaxis, downsampled_yaxis)
    moved = jnp.transpose(moved, (0, 3, 1, 4, 2, 5))
    result = moved.reshape(
        comps, planes, width_gx * downsampled_xaxis, width_gy * downsampled_yaxis
    )
    return result


def solution(mesh):
    return jax.shard_map(
        local,
        mesh=mesh,
        in_specs=(
            P(None, ("grp", "gx"), "gy", None),
            P(None, ("grp", "gx"), "gy", None),
            P(("grp", "gx"), "gy", None),
            P(),
        ),
        out_specs=P(None, ("gx", "gy"), "grp", None),
        check_vma=False,
    )
```

profile of v0, /device:TPU:0, one launch (start us, length us, event | category | flops | bytes accessed | tf_op | source)
XLA Modules:
  0.0 161.0 jit_solution(15697098040735208995)
XLA Ops:
  0.0 1.5 fusion.109
  1.6 5.0 %collective-permute-start = (bf16[6,2,256,128]{3,2,0,1:T(8,128)(2,1)S(1)}, bf16[6,2,256,128]{3,2,0,1:T(8,128)(2,1)S(1)}, u32[]{:S(2)}, u32[]{:S(2)}) collective-permute-start(bf16[6,2,256,128]{3,2,0,1:T(8,128)(2,1)S(1)} %copy.182), channel_id=1, source_target_pairs={{0,2},{2,4},{4,6},{6,8},{8,10},{10,12},{12,14},{14,16},{16,18},{18... | collective-permute-start | bytes 2359304 | tf_op jit(solution)/shard_map/ppermute | solution.py:16
  6.7 1.4 collective-permute-start.1
  8.2 32.1 %collective-permute-done = bf16[6,2,256,128]{3,2,0,1:T(8,128)(2,1)S(1)} collective-permute-done((bf16[6,2,256,128]{3,2,0,1:T(8,128)(2,1)S(1)}, bf16[6,2,256,128]{3,2,0,1:T(8,128)(2,1)S(1)}, u32[]{:S(2)}, u32[]{:S(2)}) %collective-permute-start) | collective-permute-done | bytes 786464 | tf_op jit(solution)/shard_map/ppermute | solution.py:16
  40.5 1.7 %collective-permute-done.1 = bf16[6,2,256,128]{3,2,0,1:T(8,128)(2,1)S(1)} collective-permute-done((bf16[6,2,256,128]{3,2,0,1:T(8,128)(2,1)S(1)}, bf16[6,2,256,128]{3,2,0,1:T(8,128)(2,1)S(1)}, u32[]{:S(2)}, u32[]{:S(2)}) %collective-permute-start.1) | collective-permute-done | bytes 786464 | tf_op jit(solution)/shard_map/ppermute | solution.py:19
  42.4 1.3 collective-permute-start.2
  43.7 1.3 collective-permute-start.3
  47.8 6.9 %fusion.9 = f32[6,4,256,128]{3,2,0,1:T(8,128)S(1)} fusion(f32[6,8,260,128]{3,2,0,1:T(8,128)S(1)} %maximum_convert_fusion, bf16[6,4,256,128]{3,2,1,0:T(8,128)(2,1)} %param.5, f32[4,256,128]{2,1,0:T(8,128)} %convert_multiply_fusion), kind=kLoop, calls=%fused_computation.15 | loop fusion | flops 24379392 | bytes 40042496 | tf_op jit(solution)/shard_map/add | solution.py:78
  55.9 1.4 slice.410
  57.3 4.6 %collective-permute-start.4 = (f32[6,2,256,128]{3,2,0,1:T(8,128)}, f32[6,2,256,128]{3,2,0,1:T(8,128)}, u32[]{:S(2)}, u32[]{:S(2)}) collective-permute-start(f32[6,2,256,128]{3,2,0,1:T(8,128)} %slice.410), channel_id=1, source_target_pairs={{0,2},{2,4},{4,6},{6,8},{8,10},{10,12},{12,14},{14,16},{16,18},{18... | collective-permute-start | bytes 4718600 | tf_op jit(solution)/shard_map/ppermute | solution.py:27
  61.9 1.5 convolution_bitcast_fusion
  64.3 1.5 slice_bitcast_fusion
  65.9 1.2 copy-done.2
  73.4 2.0 %fusion.38 = f32[6,64,32]{1,2,0:T(8,128)} fusion(f32[6,1,64,128]{3,2,0,1:T(8,128)S(1)} %slice.385, f32[6,128,32]{1,0,2:T(8,128)} %get-tuple-element.7), kind=kOutput, calls=%fused_computation.70 | convolution fusion | flops 18874368 | bytes 344064 | tf_op jit(solution)/shard_map/cxyz,czk->cxyk/dot_general | solution.py:110
  75.3 2.1 %fusion.45 = f32[6,64,32]{1,2,0:T(8,128)} fusion(f32[6,1,64,128]{3,2,0,1:T(8,128)} %slice.375, f32[6,128,32]{1,0,2:T(8,128)} %get-tuple-element.12), kind=kOutput, calls=%fused_computation.77 | convolution fusion | flops 18874368 | bytes 344064 | tf_op jit(solution)/shard_map/cxyz,czk->cxyk/dot_general | solution.py:110
  77.4 1.4 fusion.52
  78.8 16.2 %collective-permute-done.4 = f32[6,2,256,128]{3,2,0,1:T(8,128)} collective-permute-done((f32[6,2,256,128]{3,2,0,1:T(8,128)}, f32[6,2,256,128]{3,2,0,1:T(8,128)}, u32[]{:S(2)}, u32[]{:S(2)}) %collective-permute-start.4) | collective-permute-done | bytes 1572896 | tf_op jit(solution)/shard_map/ppermute | solution.py:27
  95.0 1.4 pad_maximum_fusion
  96.5 1.9 %collective-permute-start.5 = (f32[6,6,2,128]{3,2,0,1:T(2,128)}, f32[6,6,2,128]{3,2,0,1:T(2,128)}, u32[]{:S(2)}, u32[]{:S(2)}) collective-permute-start(f32[6,6,2,128]{3,2,0,1:T(2,128)} %pad_maximum_fusion), channel_id=1, source_target_pairs={{0,1},{2,3},{4,5},{6,7},{8,9},{10,11},{12,13},{14,15},{16,17},{18,... | collective-permute-start | bytes 110600 | tf_op jit(solution)/shard_map/ppermute | solution.py:27
  99.5 2.0 %fusion.58 = f32[6,64,32]{1,2,0:T(8,128)} fusion(f32[6,1,64,128]{3,2,0,1:T(8,128)S(1)} %slice.359, f32[6,128,32]{1,0,2:T(8,128)} %get-tuple-element.20), kind=kOutput, calls=%fused_computation.90 | convolution fusion | flops 18874368 | bytes 344064 | tf_op jit(solution)/shard_map/cxyz,czk->cxyk/dot_general | solution.py:110
  102.7 2.0 %fusion.60 = f32[6,64,32]{1,2,0:T(8,128)} fusion(f32[6,1,64,128]{3,2,0,1:T(8,128)S(1)} %slice.357, f32[6,128,32]{1,0,2:T(8,128)} %get-tuple-element.21), kind=kOutput, calls=%fused_computation.92 | convolution fusion | flops 18874368 | bytes 344064 | tf_op jit(solution)/shard_map/cxyz,czk->cxyk/dot_general | solution.py:110
  105.8 2.0 %fusion.62 = f32[6,64,32]{1,2,0:T(8,128)} fusion(f32[6,1,64,128]{3,2,0,1:T(8,128)S(1)} %slice.355, f32[6,128,32]{1,0,2:T(8,128)} %get-tuple-element.22), kind=kOutput, calls=%fused_computation.94 | convolution fusion | flops 18874368 | bytes 344064 | tf_op jit(solution)/shard_map/cxyz,czk->cxyk/dot_general | solution.py:110
  108.9 2.0 %fusion.68 = f32[6,64,32]{1,2,0:T(8,128)} fusion(f32[6,1,64,128]{3,2,0,1:T(8,128)S(1)} %slice.349, f32[6,128,32]{1,0,2:T(8,128)} %get-tuple-element.26), kind=kOutput, calls=%fused_computation.100 | convolution fusion | flops 18874368 | bytes 344064 | tf_op jit(solution)/shard_map/cxyz,czk->cxyk/dot_general | solution.py:110
  112.0 2.0 %fusion.70 = f32[6,64,32]{1,2,0:T(8,128)} fusion(f32[6,1,64,128]{3,2,0,1:T(8,128)S(1)} %slice.347, f32[6,128,32]{1,0,2:T(8,128)} %get-tuple-element.27), kind=kOutput, calls=%fused_computation.102 | convolution fusion | flops 18874368 | bytes 344064 | tf_op jit(solution)/shard_map/cxyz,czk->cxyk/dot_general | solution.py:110
  115.2 2.0 %fusion.72 = f32[6,64,32]{1,2,0:T(8,128)} fusion(f32[6,1,64,128]{3,2,0,1:T(8,128)S(1)} %slice.345, f32[6,128,32]{1,0,2:T(8,128)} %get-tuple-element.28), kind=kOutput, calls=%fused_computation.104 | convolution fusion | flops 18874368 | bytes 344064 | tf_op jit(solution)/shard_map/cxyz,czk->cxyk/dot_general | solution.py:110
  117.1 4.0 %maximum_maximum_fusion = f32[6,6,258,128]{3,2,0,1:T(8,128)} fusion(f32[6,4,256,128]{3,2,0,1:T(8,128)S(1)} %copy-done.2, f32[6,2,256,128]{3,2,0,1:T(8,128)} %collective-permute-done.4, f32[6,6,2,128]{3,2,0,1:T(2,128)} %collective-permute-done.5), kind=kLoop, calls=%fused_computation.4 | loop fusion | flops 2377728 | bytes 9510912 | tf_op jit(solution)/shard_map/concatenate | solution.py:123
  121.1 1.2 slice.383
  127.1 1.2 slice.361
  133.1 1.4 fusion.40
  134.6 1.4 fusion.47
  138.2 1.6 fusion.34
  145.0 14.5 %all_to_all.4 = f32[32,1,384]{2,1,0:T(1,128)S(1)} all-to-all(f32[32,1,384]{2,1,0:T(1,128)S(1)} %reshape.157), channel_id=1, replica_groups=mesh['grp'=1,'gx'=16,'gy'=2] {'gx','gy'}, dimensions={0} | all-to-all | bytes 98304 | tf_op jit(solution)/shard_map/all_to_all | solution.py:131
  (117 shorter events, 36.6 us)
Async XLA Ops:
  0.0 61.9 %copy-start = (f32[6,5,5,5]{3,0,2,1:T(8,128)S(1)}, f32[6,5,5,5]{3,0,2,1:T(8,128)}, u32[]{:S(2)}) copy-start(f32[6,5,5,5]{3,0,2,1:T(8,128)} %param.7) | copy-start | bytes 9004
  1.6 38.8 %copy-start.3 = (bf16[6,4,256,128]{3,2,1,0:T(8,128)(2,1)S(1)}, bf16[6,4,256,128]{3,2,1,0:T(8,128)(2,1)}, u32[]{:S(2)}) copy-start(bf16[6,4,256,128]{3,2,1,0:T(8,128)(2,1)} %param.4) | copy-start | bytes 4718596
  1.6 38.6 %collective-permute-start = (bf16[6,2,256,128]{3,2,0,1:T(8,128)(2,1)S(1)}, bf16[6,2,256,128]{3,2,0,1:T(8,128)(2,1)S(1)}, u32[]{:S(2)}, u32[]{:S(2)}) collective-permute-start(bf16[6,2,256,128]{3,2,0,1:T(8,128)(2,1)S(1)} %copy.182), channel_id=1, source_target_pairs={{0,2},{2,4},{4,6},{6,8},{8,10},{10,12},{12,14},{14,16},{16,18},{18... | collective-permute-start | bytes 2359304 | tf_op jit(solution)/shard_map/ppermute | solution.py:16
  6.7 38.2 %copy-start.26 = (bf16[4,256,128]{2,1,0:T(8,128)(2,1)S(1)}, bf16[4,256,128]{2,1,0:T(8,128)(2,1)}, u32[]{:S(2)}) copy-start(bf16[4,256,128]{2,1,0:T(8,128)(2,1)} %param.6) | copy-start | bytes 786436
  6.7 35.5 %collective-permute-start.1 = (bf16[6,2,256,128]{3,2,0,1:T(8,128)(2,1)S(1)}, bf16[6,2,256,128]{3,2,0,1:T(8,128)(2,1)S(1)}, u32[]{:S(2)}, u32[]{:S(2)}) collective-permute-start(bf16[6,2,256,128]{3,2,0,1:T(8,128)(2,1)S(1)} %copy.183), channel_id=1, source_target_pairs={{2,0},{4,2},{6,4},{8,6},{10,8},{12,10},{14,12},{16,14},{18,16},{20... | collective-permute-start | bytes 2359304 | tf_op jit(solution)/shard_map/ppermute | solution.py:19
  42.4 3.5 %collective-permute-start.2 = (bf16[6,8,2,128]{3,2,0,1:T(2,128)(2,1)S(1)}, bf16[6,8,2,128]{3,2,0,1:T(2,128)(2,1)S(1)}, u32[]{:S(2)}, u32[]{:S(2)}) collective-permute-start(bf16[6,8,2,128]{3,2,0,1:T(2,128)(2,1)S(1)} %get-tuple-element.30), channel_id=1, source_target_pairs={{0,1},{2,3},{4,5},{6,7},{8,9},{10,11},{12,13},{14,15},{16,17},{18,... | collective-permute-start | bytes 73736 | tf_op jit(solution)/shard_map/ppermute | solution.py:16
  43.7 3.1 %collective-permute-start.3 = (bf16[6,8,2,128]{3,2,0,1:T(2,128)(2,1)S(1)}, bf16[6,8,2,128]{3,2,0,1:T(2,128)(2,1)S(1)}, u32[]{:S(2)}, u32[]{:S(2)}) collective-permute-start(bf16[6,8,2,128]{3,2,0,1:T(2,128)(2,1)S(1)} %get-tuple-element.31), channel_id=1, source_target_pairs={{1,0},{3,2},{5,4},{7,6},{9,8},{11,10},{13,12},{15,14},{17,16},{19,... | collective-permute-start | bytes 73736 | tf_op jit(solution)/shard_map/ppermute | solution.py:19
  55.9 7.5 %copy-start.1 = (f32[6,4,256,128]{3,2,0,1:T(8,128)}, f32[6,4,256,128]{3,2,0,1:T(8,128)S(1)}, u32[]{:S(2)}) copy-start(f32[6,4,256,128]{3,2,0,1:T(8,128)S(1)} %multiply_add_fusion) | copy-start | bytes 9437188
  57.3 37.7 %collective-permute-start.4 = (f32[6,2,256,128]{3,2,0,1:T(8,128)}, f32[6,2,256,128]{3,2,0,1:T(8,128)}, u32[]{:S(2)}, u32[]{:S(2)}) collective-permute-start(f32[6,2,256,128]{3,2,0,1:T(8,128)} %slice.410), channel_id=1, source_target_pairs={{0,2},{2,4},{4,6},{6,8},{8,10},{10,12},{12,14},{14,16},{16,18},{18... | collective-permute-start | bytes 4718600 | tf_op jit(solution)/shard_map/ppermute | solution.py:27
  96.5 20.7 %collective-permute-start.5 = (f32[6,6,2,128]{3,2,0,1:T(2,128)}, f32[6,6,2,128]{3,2,0,1:T(2,128)}, u32[]{:S(2)}, u32[]{:S(2)}) collective-permute-start(f32[6,6,2,128]{3,2,0,1:T(2,128)} %pad_maximum_fusion), channel_id=1, source_target_pairs={{0,1},{2,3},{4,5},{6,7},{8,9},{10,11},{12,13},{14,15},{16,17},{18,... | collective-permute-start | bytes 110600 | tf_op jit(solution)/shard_map/ppermute | solution.py:27
  121.1 14.8 %copy-start.15 = (f32[6,128,32]{1,0,2:T(8,128)S(1)}, f32[6,128,32]{1,0,2:T(8,128)}, u32[]{:S(2)}) copy-start(f32[6,128,32]{1,0,2:T(8,128)} %get-tuple-element.18) | copy-start | bytes 294916
  121.1 15.3 %copy-start.14 = (f32[6,128,32]{1,0,2:T(8,128)S(1)}, f32[6,128,32]{1,0,2:T(8,128)}, u32[]{:S(2)}) copy-start(f32[6,128,32]{1,0,2:T(8,128)} %get-tuple-element.19) | copy-start | bytes 294916
  121.1 15.7 %copy-start.13 = (f32[6,128,32]{1,0,2:T(8,128)S(1)}, f32[6,128,32]{1,0,2:T(8,128)}, u32[]{:S(2)}) copy-start(f32[6,128,32]{1,0,2:T(8,128)} %get-tuple-element.23) | copy-start | bytes 294916
  121.1 16.2 %copy-start.12 = (f32[6,128,32]{1,0,2:T(8,128)S(1)}, f32[6,128,32]{1,0,2:T(8,128)}, u32[]{:S(2)}) copy-start(f32[6,128,32]{1,0,2:T(8,128)} %get-tuple-element.25) | copy-start | bytes 294916
  121.1 16.6 %copy-start.11 = (f32[6,128,32]{1,0,2:T(8,128)S(1)}, f32[6,128,32]{1,0,2:T(8,128)}, u32[]{:S(2)}) copy-start(f32[6,128,32]{1,0,2:T(8,128)} %get-tuple-element.29) | copy-start | bytes 294916
  122.4 15.8 %copy-start.10 = (f32[6,128,32]{1,0,2:T(8,128)S(1)}, f32[6,128,32]{1,0,2:T(8,128)}, u32[]{:S(2)}) copy-start(f32[6,128,32]{1,0,2:T(8,128)} %get-tuple-element.24) | copy-start | bytes 294916
  127.1 12.6 %copy-start.9 = (f32[6,1,64,128]{3,2,0,1:T(8,128)S(1)}, f32[6,1,64,128]{3,2,0,1:T(8,128)}, u32[]{:S(2)}) copy-start(f32[6,1,64,128]{3,2,0,1:T(8,128)} %slice.367) | copy-start | bytes 589828
  128.3 11.9 %copy-start.8 = (f32[6,1,64,128]{3,2,0,1:T(8,128)S(1)}, f32[6,1,64,128]{3,2,0,1:T(8,128)}, u32[]{:S(2)}) copy-start(f32[6,1,64,128]{3,2,0,1:T(8,128)} %slice.369) | copy-start | bytes 589828
  131.9 9.2 %copy-start.7 = (f32[6,1,64,128]{3,2,0,1:T(8,128)S(1)}, f32[6,1,64,128]{3,2,0,1:T(8,128)}, u32[]{:S(2)}) copy-start(f32[6,1,64,128]{3,2,0,1:T(8,128)} %slice.377) | copy-start | bytes 589828
  133.1 6.7 %copy-start.23 = (f32[6,128,32]{1,0,2:T(8,128)S(1)}, f32[6,128,32]{1,0,2:T(8,128)}, u32[]{:S(2)}) copy-start(f32[6,128,32]{1,0,2:T(8,128)} %get-tuple-element.16) | copy-start | bytes 294916
  133.1 7.1 %copy-start.22 = (f32[6,128,32]{1,0,2:T(8,128)S(1)}, f32[6,128,32]{1,0,2:T(8,128)}, u32[]{:S(2)}) copy-start(f32[6,128,32]{1,0,2:T(8,128)} %get-tuple-element.15) | copy-start | bytes 294916
  133.1 7.5 %copy-start.21 = (f32[6,128,32]{1,0,2:T(8,128)S(1)}, f32[6,128,32]{1,0,2:T(8,128)}, u32[]{:S(2)}) copy-start(f32[6,128,32]{1,0,2:T(8,128)} %get-tuple-element.14) | copy-start | bytes 294916
  133.1 7.5 %copy-start.25 = (f32[6,64,32]{1,2,0:T(8,128)S(1)}, f32[6,64,32]{1,2,0:T(8,128)}, u32[]{:S(2)}) copy-start(f32[6,64,32]{1,2,0:T(8,128)} %fusion.45) | copy-start | bytes 147460
  133.1 8.0 %copy-start.20 = (f32[6,128,32]{1,0,2:T(8,128)S(1)}, f32[6,128,32]{1,0,2:T(8,128)}, u32[]{:S(2)}) copy-start(f32[6,128,32]{1,0,2:T(8,128)} %get-tuple-element.11) | copy-start | bytes 294916
  134.5 7.0 %copy-start.6 = (f32[6,1,64,128]{3,2,0,1:T(8,128)S(1)}, f32[6,1,64,128]{3,2,0,1:T(8,128)}, u32[]{:S(2)}) copy-start(f32[6,1,64,128]{3,2,0,1:T(8,128)} %slice.379) | copy-start | bytes 589828
  134.5 7.0 %copy-start.19 = (f32[6,128,32]{1,0,2:T(8,128)S(1)}, f32[6,128,32]{1,0,2:T(8,128)}, u32[]{:S(2)}) copy-start(f32[6,128,32]{1,0,2:T(8,128)} %get-tuple-element.10) | copy-start | bytes 294916
  135.9 6.0 %copy-start.18 = (f32[6,128,32]{1,0,2:T(8,128)S(1)}, f32[6,128,32]{1,0,2:T(8,128)}, u32[]{:S(2)}) copy-start(f32[6,128,32]{1,0,2:T(8,128)} %get-tuple-element.9) | copy-start | bytes 294916
  135.9 6.0 %copy-start.24 = (f32[6,64,32]{1,2,0:T(8,128)S(1)}, f32[6,64,32]{1,2,0:T(8,128)}, u32[]{:S(2)}) copy-start(f32[6,64,32]{1,2,0:T(8,128)} %fusion.38) | copy-start | bytes 147460
  136.8 5.6 %copy-start.5 = (f32[6,1,64,128]{3,2,0,1:T(8,128)S(1)}, f32[6,1,64,128]{3,2,0,1:T(8,128)}, u32[]{:S(2)}) copy-start(f32[6,1,64,128]{3,2,0,1:T(8,128)} %slice.387) | copy-start | bytes 589828
  136.8 5.6 %copy-start.17 = (f32[6,128,32]{1,0,2:T(8,128)S(1)}, f32[6,128,32]{1,0,2:T(8,128)}, u32[]{:S(2)}) copy-start(f32[6,128,32]{1,0,2:T(8,128)} %get-tuple-element.6) | copy-start | bytes 294916
  137.3 5.6 %copy-start.4 = (f32[6,1,64,128]{3,2,0,1:T(8,128)S(1)}, f32[6,1,64,128]{3,2,0,1:T(8,128)}, u32[]{:S(2)}) copy-start(f32[6,1,64,128]{3,2,0,1:T(8,128)} %slice.389) | copy-start | bytes 589828
  137.3 5.6 %copy-start.16 = (f32[6,128,32]{1,0,2:T(8,128)S(1)}, f32[6,128,32]{1,0,2:T(8,128)}, u32[]{:S(2)}) copy-start(f32[6,128,32]{1,0,2:T(8,128)} %get-tuple-element.5) | copy-start | bytes 294916
  (1 other events, 2.8 us)
where the time goes:
time: 162 us; the launch traced here: 161 us
  waiting for transfers between devices  50.9 us (31%)
  local copies, waits for them, and re-layouts  33.7 us (21%)
  matrix products  28.5 us (18%)
  other arithmetic  17 us (10%)
  starting transfers between devices  15.5 us (10%)
  blocking collectives  14.5 us (9%)
    ppermute x2, waiting for transfers between devices, padded_2(): lax.ppermute(lax.slice_in_dim(block, block.shape[dim] - width, None, axis...  32.1 us
    dot_general x25, matrix products, restrict(): jnp.einsum('cxyz,czk->cxyk', piece, band[:, shift_x, shift_y], precision=...  27 us
    slice x25, local copies, waits for them, and re-layouts, restrict(): lax.slice(stress_full, (0, shift_x, shift_y, 0), (comps, shift_x + 4 * (d...  24.9 us
    ppermute x2, waiting for transfers between devices, shifted(): return lax.ppermute(block, axis, route)  16.2 us
    all_to_all x1, blocking collectives, local(): lax.all_to_all(margin_extended, ('gx', 'gy'), split_axis=2, concat_axis=1...  14.5 us
    add x1, other arithmetic, update(): center + DIFFUSE * lap  6.95 us
    ppermute x2, starting transfers between devices, shifted(): return lax.ppermute(block, axis, route)  6.5 us
    ppermute x2, starting transfers between devices, padded_2(): lax.ppermute(lax.slice_in_dim(block, block.shape[dim] - width, None, axis...  6.31 us
  transfers between devices with their start and end apart: 6, of which 4 were waited for; matrix products, arithmetic and copies ran while one was open for 22% of the time, Pallas kernels for 0%

commit v1 on v0

v1 whole, which is shorter than its diff:
```python
import functools

import jax
import jax.numpy as jnp
from jax import lax
from jax.experimental import pallas as pl
from jax.experimental.pallas import tpu as pltpu
from jax.sharding import PartitionSpec as P

STENCIL = 0.12 / 12.0
RELAX_STEP = 0.1
NOISE_AMP = 0.3
NC = 6
LANES = 128
LEAD = 8
TAIL = 32


def band(size):
    row = lax.broadcasted_iota(jnp.int32, (size, size), 0)
    col = lax.broadcasted_iota(jnp.int32, (size, size), 1)
    gap = jnp.abs(row - col)
    value = jnp.where(gap == 0, -30.0, jnp.where(gap == 1, 16.0, jnp.where(gap == 2, -1.0, 0.0)))
    return value.astype(jnp.bfloat16)


def begin_kernel(idx_ref, f_ref, b_ref, r_ref, cols_ref, ty_ref, tz_ref, out_ref):
    rows, ny = f_ref.shape[1], f_ref.shape[2]
    odd, gy = idx_ref[0], idx_ref[1]
    step = 64
    for x in range(rows):
        side = jnp.where(odd == 1, x // 2, 1 - x // 2)
        plane = f_ref[0, x]
        for y in range(0, ny, step):
            ys = pl.ds(y, step)
            part = f_ref[0, x, ys]
            lap = jnp.dot(ty_ref[ys], plane, preferred_element_type=jnp.float32)
            lap += jnp.dot(part, tz_ref[...], preferred_element_type=jnp.float32)
            own = part.astype(jnp.float32)
            lap -= 30.0 * own
            for other in range(rows):
                if abs(other - x) == 1:
                    lap += 16.0 * f_ref[0, other, ys].astype(jnp.float32)
                elif abs(other - x) == 2:
                    lap -= f_ref[0, other, ys].astype(jnp.float32)
            rate = r_ref[x, ys].astype(jnp.float32)
            noise = b_ref[0, x, ys].astype(jnp.float32)
            out_ref[side, 0, x % 2, ys] = own - RELAX_STEP * rate * own + NOISE_AMP * noise + STENCIL * lap
        near_row = lax.broadcasted_iota(jnp.int32, (8, 1), 0)
        first = cols_ref[0, x, 0:1]
        second = cols_ref[0, x, 1:2]

        @pl.when(gy == 1)
        def _():
            extra = jnp.where(near_row == 0, 16.0 * second - first, jnp.where(near_row == 1, -second, 0.0))
            out_ref[side, 0, x % 2, 0:8] += STENCIL * extra

        @pl.when(gy == 0)
        def _():
            extra = jnp.where(near_row == 7, 16.0 * first - second, jnp.where(near_row == 6, -first, 0.0))
            out_ref[side, 0, x % 2, ny - 8 : ny] += STENCIL * extra


def begin(idx, log_conf, brownian, relax_rate, cols):
    comps, rows, ny, nz = log_conf.shape
    whole = lambda *shape: pl.BlockSpec(shape, lambda c: (0,) * len(shape))
    block = pl.BlockSpec((1, rows, ny, nz), lambda c: (c, 0, 0, 0))
    return pl.pallas_call(
        begin_kernel,
        grid=(comps,),
        in_specs=[
            pl.BlockSpec(memory_space=pltpu.SMEM),
            block,
            block,
            whole(rows, ny, nz),
            pl.BlockSpec((1, rows, 2, nz), lambda c: (c, 0, 0, 0)),
            whole(ny, ny),
            whole(nz, nz),
        ],
        out_specs=pl.BlockSpec((2, 1, 2, ny, nz), lambda c: (0, c, 0, 0, 0)),
        out_shape=jax.ShapeDtypeStruct((2, comps, 2, ny, nz), jnp.float32),
        compiler_params=pltpu.CompilerParams(vmem_limit_bytes=24 * 2**20),
        cost_estimate=pl.CostEstimate(
            flops=30 * comps * rows * ny * nz, bytes_accessed=10 * comps * rows * ny * nz, transcendentals=0
        ),
        name="begin",
    )(idx, log_conf, brownian, relax_rate, cols, band(ny), band(nz))


def finish_kernel(side, has_base, idx_ref, u_ref, halo_ref, w_ref, pick_ref, *refs):
    if has_base:
        base_ref, out_ref, stress, sums = refs
    else:
        out_ref, stress, sums = refs
    ny, nz = u_ref.shape[3], u_ref.shape[4]
    nj = ny // 4
    planes = out_ref.shape[0] // 8
    odd = idx_ref[0]
    upper = (odd == side).astype(jnp.int32)
    near, far = 1 - upper, upper
    edge, inner = upper, 1 - upper
    for c in range(NC):
        for r in range(2):
            for piece in range(nz // LANES):
                stress[c, r, piece, 0:LEAD] = jnp.zeros((LEAD, LANES), jnp.float32)
                stress[c, r, piece, LEAD + ny : LEAD + ny + TAIL] = jnp.zeros((TAIL, LANES), jnp.float32)

    def chunk(step, carry):
        y = pl.multiple_of(step * 16, 16)
        ys = pl.ds(y, 16)
        rows = ([], [])
        for c in range(NC):
            close = halo_ref[c, near, ys].astype(jnp.float32)
            distant = halo_ref[c, far, ys].astype(jnp.float32)
            rows[0].append(u_ref[0, c, inner, ys] - STENCIL * close)
            rows[1].append(u_ref[0, c, edge, ys] + (16.0 * STENCIL) * close - STENCIL * distant)
        for r in range(2):
            xx, xy, xz, yy, yz, zz = rows[r]
            xy2, xz2, yz2 = xy * xy, xz * xz, yz * yz
            values = (
                xx + 0.5 * (xx * xx + xy2 + xz2),
                xy + 0.5 * (xy * (xx + yy) + xz * yz),
                xz + 0.5 * (xz * (xx + zz) + xy * yz),
                yy + 0.5 * (xy2 + yy * yy + yz2),
                yz + 0.5 * (yz * (yy + zz) + xy * xz),
                zz + 0.5 * (xz2 + yz2 + zz * zz),
            )
            for c in range(NC):
                for piece in range(nz // LANES):
                    stress[c, r, piece, pl.ds(y + LEAD, 16)] = values[c][:, piece * LANES : (piece + 1) * LANES]
        return carry

    lax.fori_loop(0, ny // 16, chunk, 0)

    main_i = jnp.where(upper == 1, 0, 3)
    main_e = jnp.where(upper == 1, 1, 2)
    extra_i = jnp.where(upper == 1, 4, 5)
    height = nj + 8
    main_at = pl.multiple_of(upper * height, 8)
    extra_at = pl.multiple_of((1 - upper) * height, 8)
    for c in range(NC):
        weight = {}
        for b in range(5):
            for k in range(2):
                for name, a in (("mi", main_i), ("me", main_e), ("xi", extra_i)):
                    weight[name, b, k] = w_ref[c, a, 2 * b + k : 2 * b + k + 1]
        for jb in range(nj // 8 + 1):
            main = [None, None]
            extra = [None, None]
            for b in range(5 if jb < nj // 8 else 2):
                at = pl.ds(LEAD + 32 * jb + b - 2, 8, stride=4)
                inside = jnp.concatenate([stress[c, 0, piece, at] for piece in range(nz // LANES)], axis=1)
                outside = jnp.concatenate([stress[c, 1, piece, at] for piece in range(nz // LANES)], axis=1)
                for k in range(2):
                    term = inside * weight["mi", b, k] + outside * weight["me", b, k]
                    main[k] = term if main[k] is None else main[k] + term
                    term = inside * weight["xi", b, k]
                    extra[k] = term if extra[k] is None else extra[k] + term
            for k in range(2):
                sums[c, pl.ds(main_at + 8 * jb, 8), k * nz : (k + 1) * nz] = main[k]
                sums[c, pl.ds(extra_at + 8 * jb, 8), k * nz : (k + 1) * nz] = extra[k]

    def reduced(values):
        high = values.astype(jnp.bfloat16)
        low = (values - high.astype(jnp.float32)).astype(jnp.bfloat16)
        both = jnp.concatenate([high, low], axis=1)
        return lax.dot_general(
            pick_ref[...], both, (((1,), (1,)), ((), ())), preferred_element_type=jnp.float32
        )

    def put(place, value):
        rows = pl.ds(place, planes, stride=8)
        if has_base:
            value = value + base_ref[rows, :]
        out_ref[rows, :] = value

    for c in range(NC):
        put(c, reduced(jnp.concatenate([sums[c, 0:nj], sums[c, height : height + nj]], axis=0)))
    beyond = []
    for c in range(NC):
        for t in range(2):
            beyond.append(sums[c, t * height + nj : t * height + nj + 1])
    beyond.append(jnp.zeros((2 * nj - 2 * NC, 2 * nz), jnp.float32))
    put(NC, reduced(jnp.concatenate(beyond, axis=0)))
    out_ref[pl.ds(7, planes, stride=8), :] = jnp.zeros((planes, 2 * nj), jnp.float32)


def finish(side, idx, begun, halo, weights, pick, base):
    _, comps, _, ny, nz = begun.shape
    planes, nj = nz // 4, ny // 4
    vmem = pl.BlockSpec(memory_space=pltpu.VMEM)
    operands = [idx, begun, halo, weights, pick] + ([] if base is None else [base])
    specs = [
        pl.BlockSpec(memory_space=pltpu.SMEM),
        pl.BlockSpec((1, comps, 2, ny, nz), lambda i: (side, 0, 0, 0, 0)),
    ] + [pl.BlockSpec(x.shape, functools.partial(lambda n, i: (0,) * n, x.ndim)) for x in operands[2:]]
    return pl.pallas_call(
        functools.partial(finish_kernel, side, base is not None),
        grid=(1,),
        in_specs=specs,
        out_specs=pl.BlockSpec((planes * 8, 2 * nj), lambda i: (0, 0)),
        out_shape=jax.ShapeDtypeStruct((planes * 8, 2 * nj), jnp.float32),
        scratch_shapes=[
            pltpu.VMEM((comps, 2, nz // LANES, LEAD + ny + TAIL, LANES), jnp.float32),
            pltpu.VMEM((comps, 2 * (nj + 8), 2 * nz), jnp.float32),
        ],
        compiler_params=pltpu.CompilerParams(vmem_limit_bytes=32 * 2**20),
        cost_estimate=pl.CostEstimate(
            flops=40 * comps * ny * nz, bytes_accessed=16 * comps * ny * nz, transcendentals=0
        ),
        name="finish",
    )(*operands)


def gather_kernel(in_ref, out_ref):
    count, lanes = out_ref.shape[2], out_ref.shape[3]
    half = lanes // 2
    lane = lax.broadcasted_iota(jnp.int32, (count, lanes), 1)
    row = lax.broadcasted_iota(jnp.int32, (count, lanes), 0)
    low = lane < half
    beyond = in_ref[pl.ds(NC, count, stride=16), :]
    for c in range(NC):
        first = in_ref[pl.ds(c, count, stride=16), :]
        second = in_ref[pl.ds(8 + c, count, stride=16), :]
        own = jnp.where(low, first, pltpu.roll(second, half, 1))
        own += jnp.where(lane == half, pltpu.roll(beyond, half - 2 * c, 1), 0.0)
        after = jnp.where(low, pltpu.roll(first, half, 1), second)
        after += jnp.where(lane == half, pltpu.roll(beyond, half - 2 * c - 1, 1), 0.0)
        out_ref[c, 0] = own + jnp.where(row > 0, pltpu.roll(after, 1, 0), 0.0)


def local(log_conf, brownian, relax_rate, kernel):
    comps, rows, ny, nz = log_conf.shape
    width_gx, width_gy = lax.axis_size("gx"), lax.axis_size("gy")
    planes = nz // 4
    assert comps == NC and rows == 4 and width_gy == 2 and width_gx % 2 == 0
    assert planes == width_gx * width_gy
    odd = lax.axis_index("gx") % 2
    gy = lax.axis_index("gy")

    swap_first = [(i, i ^ 1) for i in range(width_gx)]
    swap_second = [(i, ((i + 1) ^ 1) - 1) for i in range(1, width_gx - 1)]
    halo_first = lax.ppermute(lax.dynamic_slice_in_dim(log_conf, 2 - 2 * odd, 2, axis=1), "gx", swap_first)
    halo_second = lax.ppermute(lax.dynamic_slice_in_dim(log_conf, 2 * odd, 2, axis=1), "gx", swap_second)
    edge_cols = jnp.where(gy == 0, log_conf[:, :, ny - 2 :], log_conf[:, :, :2])
    cols = lax.ppermute(edge_cols, "gy", [(0, 1), (1, 0)]).astype(jnp.float32)

    idx = jnp.stack([odd, gy]).astype(jnp.int32)
    begun = begin(idx, log_conf, brownian, relax_rate, cols)

    near = jnp.tile(jnp.roll(kernel[..., :4], -2, axis=-1), (1, 1, 1, nz // 4))
    last = jnp.broadcast_to(kernel[..., 4:], near.shape)
    weights = jnp.stack([near, last], axis=3).reshape(comps, 5, 10, nz)
    weights = jnp.pad(weights, ((0, 0), (0, 1), (0, 6), (0, 0)))
    z = lax.broadcasted_iota(jnp.int32, (planes, nz), 1)
    k = lax.broadcasted_iota(jnp.int32, (planes, nz), 0)
    pick = jnp.concatenate([(z + 2) // 4 == k, z == 4 * k + 2] * 2, axis=1).astype(jnp.bfloat16)

    part = finish(0, idx, begun, halo_first, weights, pick, None)
    part = finish(1, idx, begun, halo_second, weights, pick, part)
    moved = lax.all_to_all(part.reshape(planes, 8, ny // 2), ("gx", "gy"), 0, 0, tiled=True)
    return pl.pallas_call(
        gather_kernel,
        out_shape=jax.ShapeDtypeStruct((comps, 1, width_gx, ny // 2), jnp.float32),
        name="gather",
    )(moved.reshape(planes * 8, ny // 2))


def solution(mesh):
    return jax.shard_map(
        local,
        mesh=mesh,
        in_specs=(
            P(None, ("grp", "gx"), "gy", None),
            P(None, ("grp", "gx"), "gy", None),
            P(("grp", "gx"), "gy", None),
            P(),
        ),
        out_specs=P(None, ("gx", "gy"), "grp", None),
        check_vma=False,
    )
```

time: 162 us -> 61.1 us (0.38)
  waiting for transfers between devices: 50.9 us -> 20.1 us
  matrix products: 28.5 us -> 0 us
  local copies, waits for them, and re-layouts: 33.7 us -> 9.48 us
  other arithmetic: 17 us -> 1.26 us
  Pallas kernels: 0 us -> 12 us
  starting transfers between devices: 15.5 us -> 3.75 us
    ppermute x6 -> x3, waiting for transfers between devices: 50.9 us -> 20.1 us  [the longest x1 20.1 us: local(): lax.ppermute(lax.dynamic_slice_in_dim(log_conf, 2 - 2 * odd, 2, axis=1),...]
    dot_general x26 -> x0, matrix products: 28.5 us -> none  [the longest x25 27 us: restrict(): jnp.einsum('cxyz,czk->cxyk', piece, band[:, shift_x, shift_y], precision=...]
    slice x28 -> x3, local copies, waits for them, and re-layouts: 27.9 us -> 0.52 us  [the longest x2 0.43 us: local(): last = jnp.broadcast_to(kernel[..., 4:], near.shape)]
    pallas_call x0 -> x4, Pallas kernels: none -> 12 us  [the longest x1 6.4 us: begin(): pl.pallas_call(begin_kernel, grid=(comps,), in_specs=[pl.BlockSpec(memory...]
    ppermute x6 -> x3, starting transfers between devices: 15.5 us -> 3.75 us  [the longest x1 2.54 us: local(): lax.ppermute(lax.dynamic_slice_in_dim(log_conf, 2 - 2 * odd, 2, axis=1),...]
    add x2 -> x1, other arithmetic: 7.43 us -> 0.01 us  [local(): 4 * k + 2]
    concatenate x2 -> x1, other arithmetic: 5.43 us -> 0.1 us  [local(): near = jnp.tile(jnp.roll(kernel[..., :4], -2, axis=-1), (1, 1, 1, nz // 4))]
    another operation x1 -> x4, local copies, waits for them, and re-layouts: 0.7 us -> 5.23 us  [the longest x2 5.14 us: local(): near = jnp.tile(jnp.roll(kernel[..., :4], -2, axis=-1), (1, 1, 1, nz // 4))]
  transfers between devices with their start and end apart: 6 -> 3, of which waited for: 4 -> 1; matrix products, arithmetic and copies ran while one was open for 22% -> 15% of each run, Pallas kernels for 0% -> 14%
where the time goes in v1:
time: 61.1 us; the launch traced here: 60.8 us
  waiting for transfers between devices  20.1 us (33%)
  blocking collectives  13.9 us (23%)
  Pallas kernels  12 us (20%)
  local copies, waits for them, and re-layouts  9.48 us (16%)
  starting transfers between devices  3.75 us (6%)
  other arithmetic  1.26 us (2%)
    ppermute x1, waiting for transfers between devices, local(): lax.ppermute(lax.dynamic_slice_in_dim(log_conf, 2 - 2 * odd, 2, axis=1),...  20.1 us
    all_to_all x1, blocking collectives, local(): lax.all_to_all(part.reshape(planes, 8, ny // 2), ('gx', 'gy'), 0, 0, tile...  13.9 us
    pallas_call x1, Pallas kernels, begin(): pl.pallas_call(begin_kernel, grid=(comps,), in_specs=[pl.BlockSpec(memory...  6.4 us
    another operation x2, local copies, waits for them, and re-layouts, local(): near = jnp.tile(jnp.roll(kernel[..., :4], -2, axis=-1), (1, 1, 1, nz // 4))  5.14 us
    pallas_call x2, Pallas kernels, finish(): pl.pallas_call(functools.partial(finish_kernel, side, base is not None),...  3.98 us
    dynamic_slice x1, local copies, waits for them, and re-layouts, local(): lax.dynamic_slice_in_dim(log_conf, 2 - 2 * odd, 2, axis=1)  2.7 us
    ppermute x1, starting transfers between devices, local(): lax.ppermute(lax.dynamic_slice_in_dim(log_conf, 2 - 2 * odd, 2, axis=1),...  2.54 us
    pallas_call x1, Pallas kernels, local(): pl.pallas_call(gather_kernel, out_shape=jax.ShapeDtypeStruct((comps, 1, w...  1.65 us
  transfers between devices with their start and end apart: 3, of which 1 were waited for; matrix products, arithmetic and copies ran while one was open for 15% of the time, Pallas kernels for 14%

profile of v1, /device:TPU:0, one launch (start us, length us, event | category | flops | bytes accessed | tf_op | source)
XLA Modules:
  0.0 60.8 jit_solution(457828797118997355)
XLA Ops:
  0.0 0.8 %broadcast_select_fusion = bf16[6,4,2,128]{3,2,1,0:T(2,128)(2,1)S(1)} fusion(pred[]{:T(512)S(6)} %eq.51, bf16[6,4,256,128]{3,2,1,0:T(8,128)(2,1)} %f_ref.1), kind=kLoop, calls=%fused_computation.13 | loop fusion | flops 6144 | bytes 36865 | tf_op jit(solution)/shard_map/jit(_where)/select_n | solution.py:245
  0.9 0.5 collective-permute-start
  1.4 0.0 copy-start.3
  1.4 2.7 %constant_dynamic-slice_fusion = (bf16[6,2,256,128]{3,2,1,0:T(8,128)(2,1)}, bf16[6,2,256,128]{3,2,1,0:T(8,128)(2,1)}) fusion(bf16[6,4,256,128]{3,2,1,0:T(8,128)(2,1)} %f_ref.1, s32[]{:T(128)S(6)} %select_n.61, s32[]{:T(128)S(6)} %select_n.59), kind=kLoop, calls=%fused_computation.23 | loop fusion | bytes 3145736 | tf_op jit(solution)/shard_map/dynamic_slice | solution.py:243
  4.1 2.5 %collective-permute-start.2 = (bf16[6,2,256,128]{3,2,1,0:T(8,128)(2,1)}, bf16[6,2,256,128]{3,2,1,0:T(8,128)(2,1)S(1)}, u32[]{:S(2)}, u32[]{:S(2)}) collective-permute-start(bf16[6,2,256,128]{3,2,1,0:T(8,128)(2,1)} %get-tuple-element.5), channel_id=1, source_target_pairs={{0,2},{2,0},{4,6},{6,4},{8,10},{10,8},{12,14},{14,12},{16,18},{18,... | collective-permute-start | bytes 2359304 | tf_op jit(solution)/shard_map/ppermute | solution.py:243
  6.6 0.7 %collective-permute-start.1 = (bf16[6,2,256,128]{3,2,1,0:T(8,128)(2,1)}, bf16[6,2,256,128]{3,2,1,0:T(8,128)(2,1)S(1)}, u32[]{:S(2)}, u32[]{:S(2)}) collective-permute-start(bf16[6,2,256,128]{3,2,1,0:T(8,128)(2,1)} %get-tuple-element.6), channel_id=1, source_target_pairs={{2,4},{4,2},{6,8},{8,6},{10,12},{12,10},{14,16},{16,14},{18,20},{2... | collective-permute-start | bytes 2359304 | tf_op jit(solution)/shard_map/ppermute | solution.py:244
  7.4 0.0 copy-done.3
  7.4 0.1 slice.26
  7.5 0.1 fusion.6
  7.6 0.1 iota_compare_fusion
  7.6 0.3 copy.12
  8.0 0.1 pad_maximum_fusion.1
  8.1 1.6 %tile.8 = f32[6,5,5,32,4]{4,3,0,2,1:T(8,128)} broadcast(f32[6,5,5,4]{3,0,2,1:T(8,128)S(1)} %pad_maximum_fusion.1), dimensions={0,1,2,4} | broadcast | bytes 79200 | tf_op jit(solution)/shard_map/tile | solution.py:251
  9.7 0.0 copy-start.1
  9.7 3.5 %tile.9 = f32[6,5,5,1,128]{4,0,2,1,3:T(8,128)S(1)} reshape(f32[6,5,5,32,4]{4,3,0,2,1:T(8,128)} %tile.8) | data formatting | bytes 153600 | tf_op jit(solution)/shard_map/tile | solution.py:251
  13.2 0.0 copy-start
  13.3 0.0 copy-start.2
  13.3 0.1 select_convert_fusion.ty_ref
  13.4 0.1 stack_broadcast_in_dim.2
  13.5 0.1 pad_add_fusion.idx_ref
  13.7 0.0 collective-permute-done
  13.7 0.0 copy-done.1
  13.7 0.9 %copy-done = bf16[6,4,256,128]{3,2,1,0:T(8,128)(2,1)S(1)} copy-done((bf16[6,4,256,128]{3,2,1,0:T(8,128)(2,1)S(1)}, bf16[6,4,256,128]{3,2,1,0:T(8,128)(2,1)}, u32[]{:S(2)}) %copy-start) | copy-done | bytes 1572888
  14.7 0.0 copy-done.2
  14.7 6.4 %begin.1.u_ref = f32[2,6,2,256,128]{4,3,2,1,0:T(8,128)S(1)} custom-call(s32[2]{0:T(128)S(1)} %pad_add_fusion.idx_ref, bf16[6,4,256,128]{3,2,1,0:T(8,128)(2,1)S(1)} %copy-done, bf16[6,4,256,128]{3,2,1,0:T(8,128)(2,1)S(1)} %copy-done.1, bf16[4,256,128]{2,1,0:T(8,128)(2,1)S(1)} %copy-done.2, f32[6,4,2,128]{3,2,1,0:T(2,128)S(1)} %convert_element_type.14.cols_ref, ...), custom_call_target="tpu_custom_call" | custom-call | flops 23592960 | bytes 7864320 | tf_op jit(solution)/shard_map/begin/pallas_call | solution.py:68
  21.1 20.1 %collective-permute-done.2.halo_ref = bf16[6,2,256,128]{3,2,1,0:T(8,128)(2,1)S(1)} collective-permute-done((bf16[6,2,256,128]{3,2,1,0:T(8,128)(2,1)}, bf16[6,2,256,128]{3,2,1,0:T(8,128)(2,1)S(1)}, u32[]{:S(2)}, u32[]{:S(2)}) %collective-permute-start.2) | collective-permute-done | bytes 786464 | tf_op jit(solution)/shard_map/ppermute | solution.py:243
  41.2 2.0 %finish.2.refs_0_ = f32[256,128]{1,0:T(8,128)S(1)} custom-call(s32[2]{0:T(128)S(1)} %pad_add_fusion.idx_ref, f32[2,6,2,256,128]{4,3,2,1,0:T(8,128)S(1)} %begin.1.u_ref, bf16[6,2,256,128]{3,2,1,0:T(8,128)(2,1)S(1)} %collective-permute-done.2.halo_ref, f32[6,6,16,128]{3,2,1,0:T(8,128)S(1)} %pad.4.w_ref, bf16[32,512]{1,0:T(8,128)(2,1)S(1)} %add_convert_fusion.pick_ref), custom_call_target="tpu_custom_call" | custom-call | flops 7864320 | bytes 3145728 | tf_op jit(solution)/shard_map/finish/pallas_call | solution.py:197
  43.2 0.0 collective-permute-done.1.halo_ref
  43.2 2.0 %finish.3 = f32[256,128]{1,0:T(8,128)S(1)} custom-call(s32[2]{0:T(128)S(1)} %pad_add_fusion.idx_ref, f32[2,6,2,256,128]{4,3,2,1,0:T(8,128)S(1)} %begin.1.u_ref, bf16[6,2,256,128]{3,2,1,0:T(8,128)(2,1)S(1)} %collective-permute-done.1.halo_ref, f32[6,6,16,128]{3,2,1,0:T(8,128)S(1)} %pad.4.w_ref, bf16[32,512]{1,0:T(8,128)(2,1)S(1)} %add_convert_fusion.pick_ref, ...), custom_call_target="tpu_custom_call" | custom-call | flops 7864320 | bytes 3145728 | tf_op jit(solution)/shard_map/finish/pallas_call | solution.py:197
  45.2 13.9 %all_to_all.5 = f32[32,8,128]{2,1,0:T(8,128)} all-to-all(f32[32,8,128]{2,1,0:T(8,128)S(1)} %bitcast.11), channel_id=1, replica_groups=mesh['grp'=1,'gx'=16,'gy'=2] {'gx','gy'}, dimensions={0} | all-to-all | bytes 262144 | tf_op jit(solution)/shard_map/all_to_all | solution.py:261
  59.1 1.6 %gather.1 = f32[6,1,16,128]{3,2,1,0:T(8,128)} custom-call(f32[256,128]{1,0:T(8,128)} %bitcast.13), custom_call_target="tpu_custom_call" | custom-call | tf_op jit(solution)/shard_map/gather/pallas_call | solution.py:262
  (11 shorter events, 0.2 us)
Async XLA Ops:
  0.9 12.8 %collective-permute-start = (bf16[6,4,2,128]{3,2,1,0:T(2,128)(2,1)S(1)}, bf16[6,4,2,128]{3,2,1,0:T(2,128)(2,1)S(1)}, u32[]{:S(2)}, u32[]{:S(2)}) collective-permute-start(bf16[6,4,2,128]{3,2,1,0:T(2,128)(2,1)S(1)} %broadcast_select_fusion), channel_id=1, source_target_pairs={{0,1},{1,0},{2,3},{3,2},{4,5},{5,4},{6,7},{7,6},{8,9},{9,8},{10,11... | collective-permute-start | bytes 36872 | tf_op jit(solution)/shard_map/ppermute | solution.py:246
  1.4 6.0 %copy-start.3 = (f32[6,5,5,5]{3,0,2,1:T(8,128)S(1)}, f32[6,5,5,5]{3,0,2,1:T(8,128)}, u32[]{:S(2)}) copy-start(f32[6,5,5,5]{3,0,2,1:T(8,128)} %param.7) | copy-start | bytes 9004
  4.1 37.1 %collective-permute-start.2 = (bf16[6,2,256,128]{3,2,1,0:T(8,128)(2,1)}, bf16[6,2,256,128]{3,2,1,0:T(8,128)(2,1)S(1)}, u32[]{:S(2)}, u32[]{:S(2)}) collective-permute-start(bf16[6,2,256,128]{3,2,1,0:T(8,128)(2,1)} %get-tuple-element.5), channel_id=1, source_target_pairs={{0,2},{2,0},{4,6},{6,4},{8,10},{10,8},{12,14},{14,12},{16,18},{18,... | collective-permute-start | bytes 2359304 | tf_op jit(solution)/shard_map/ppermute | solution.py:243
  6.6 36.6 %collective-permute-start.1 = (bf16[6,2,256,128]{3,2,1,0:T(8,128)(2,1)}, bf16[6,2,256,128]{3,2,1,0:T(8,128)(2,1)S(1)}, u32[]{:S(2)}, u32[]{:S(2)}) collective-permute-start(bf16[6,2,256,128]{3,2,1,0:T(8,128)(2,1)} %get-tuple-element.6), channel_id=1, source_target_pairs={{2,4},{4,2},{6,8},{8,6},{10,12},{12,10},{14,16},{16,14},{18,20},{2... | collective-permute-start | bytes 2359304 | tf_op jit(solution)/shard_map/ppermute | solution.py:244
  9.7 4.0 %copy-start.1 = (bf16[6,4,256,128]{3,2,1,0:T(8,128)(2,1)S(1)}, bf16[6,4,256,128]{3,2,1,0:T(8,128)(2,1)}, u32[]{:S(2)}) copy-start(bf16[6,4,256,128]{3,2,1,0:T(8,128)(2,1)} %b_ref.1) | copy-start | bytes 4718596
  13.2 1.4 %copy-start = (bf16[6,4,256,128]{3,2,1,0:T(8,128)(2,1)S(1)}, bf16[6,4,256,128]{3,2,1,0:T(8,128)(2,1)}, u32[]{:S(2)}) copy-start(bf16[6,4,256,128]{3,2,1,0:T(8,128)(2,1)} %f_ref.1) | copy-start | bytes 4718596
  13.3 1.4 %copy-start.2 = (bf16[4,256,128]{2,1,0:T(8,128)(2,1)S(1)}, bf16[4,256,128]{2,1,0:T(8,128)(2,1)}, u32[]{:S(2)}) copy-start(bf16[4,256,128]{2,1,0:T(8,128)(2,1)} %r_ref.1) | copy-start | bytes 786436

commit v2 on v1

v2 whole, which is shorter than its diff:
```python
import functools

import jax
import jax.numpy as jnp
from jax import lax
from jax.experimental import pallas as pl
from jax.experimental.pallas import tpu as pltpu
from jax.sharding import PartitionSpec as P

STENCIL = 0.12 / 12.0
RELAX_STEP = 0.1
NOISE_AMP = 0.3
NC = 6
LANES = 128
LEAD = 8
TAIL = 32


def band(size):
    row = lax.broadcasted_iota(jnp.int32, (size, size), 0)
    col = lax.broadcasted_iota(jnp.int32, (size, size), 1)
    gap = jnp.abs(row - col)
    value = jnp.where(gap == 0, -30.0, jnp.where(gap == 1, 16.0, jnp.where(gap == 2, -1.0, 0.0)))
    return value.astype(jnp.bfloat16)


def position():
    return lax.rem(lax.axis_index("gx"), 2), lax.axis_index("gy")


def pack_kernel(f_ref, first_ref, second_ref, cols_ref, edges, sems):
    odd, gy = position()
    comps, rows, ny, nz = f_ref.shape
    stop = first_ref.shape[2]
    copies = []
    for c in range(comps):
        for s, (out_ref, row) in enumerate(((first_ref, 2 - 2 * odd), (second_ref, 2 * odd))):
            source = f_ref.at[c, pl.ds(row, 2), pl.ds(0, stop)]
            copies.append(pltpu.make_async_copy(source, out_ref.at[c], sems.at[2 * c + s]))
    at = pl.multiple_of((1 - gy) * (ny - 16), 16)
    copies.append(pltpu.make_async_copy(f_ref.at[:, :, pl.ds(at, 16)], edges, sems.at[2 * comps]))
    for copy in copies:
        copy.start()
    for copy in copies:
        copy.wait()
    for c in range(comps):
        for x in range(rows):
            values = edges[c, x].astype(jnp.float32)
            cols_ref[c, x] = jnp.where(gy == 0, values[14:16], values[0:2])


def pack(log_conf, stop):
    comps, rows, ny, nz = log_conf.shape
    sent = jax.ShapeDtypeStruct((comps, 2, stop, nz), log_conf.dtype)
    anywhere = pl.BlockSpec(memory_space=pl.ANY)
    return pl.pallas_call(
        pack_kernel,
        in_specs=[pl.BlockSpec(memory_space=pltpu.HBM)],
        out_specs=[anywhere, anywhere, pl.BlockSpec(memory_space=pltpu.VMEM)],
        out_shape=[sent, sent, jax.ShapeDtypeStruct((comps, rows, 2, nz), jnp.float32)],
        scratch_shapes=[
            pltpu.VMEM((comps, rows, 16, nz), log_conf.dtype),
            pltpu.SemaphoreType.DMA((2 * comps + 1,)),
        ],
        compiler_params=pltpu.CompilerParams(vmem_limit_bytes=8 * 2**20),
        name="pack",
    )(pltpu.with_memory_space_constraint(log_conf, pltpu.HBM))


def begin_kernel(f_ref, b_ref, r_ref, cols_ref, ty_ref, tz_ref, out_ref, first_ref, second_ref):
    rows, ny = f_ref.shape[1], f_ref.shape[2]
    odd, gy = position()
    step = 64
    late = first_ref.shape[2]
    first_ref[0] = f_ref[0, pl.ds(2 - 2 * odd, 2), ny - late : ny]
    second_ref[0] = f_ref[0, pl.ds(2 * odd, 2), ny - late : ny]
    for x in range(rows):
        plane = f_ref[0, x]
        for y in range(0, ny, step):
            ys = pl.ds(y, step)
            part = f_ref[0, x, ys]
            lap = jnp.dot(ty_ref[ys], plane, preferred_element_type=jnp.float32)
            lap += jnp.dot(part, tz_ref[...], preferred_element_type=jnp.float32)
            own = part.astype(jnp.float32)
            lap -= 30.0 * own
            for other in range(rows):
                if abs(other - x) == 1:
                    lap += 16.0 * f_ref[0, other, ys].astype(jnp.float32)
                elif abs(other - x) == 2:
                    lap -= f_ref[0, other, ys].astype(jnp.float32)
            rate = r_ref[x, ys].astype(jnp.float32)
            noise = b_ref[0, x, ys].astype(jnp.float32)
            out_ref[0, x, ys] = own - RELAX_STEP * rate * own + NOISE_AMP * noise + STENCIL * lap
        near_row = lax.broadcasted_iota(jnp.int32, (8, 1), 0)
        first = cols_ref[0, x, 0:1]
        second = cols_ref[0, x, 1:2]

        @pl.when(gy == 1)
        def _():
            extra = jnp.where(near_row == 0, 16.0 * second - first, jnp.where(near_row == 1, -second, 0.0))
            out_ref[0, x, 0:8] += STENCIL * extra

        @pl.when(gy == 0)
        def _():
            extra = jnp.where(near_row == 7, 16.0 * first - second, jnp.where(near_row == 6, -first, 0.0))
            out_ref[0, x, ny - 8 : ny] += STENCIL * extra


def begin(log_conf, brownian, relax_rate, cols, late):
    comps, rows, ny, nz = log_conf.shape
    whole = lambda *shape: pl.BlockSpec(shape, lambda c: (0,) * len(shape))
    block = pl.BlockSpec((1, rows, ny, nz), lambda c: (c, 0, 0, 0))
    sent = pl.BlockSpec((1, 2, late, nz), lambda c: (c, 0, 0, 0))
    return pl.pallas_call(
        begin_kernel,
        grid=(comps,),
        in_specs=[
            block,
            block,
            whole(rows, ny, nz),
            pl.BlockSpec((1, rows, 2, nz), lambda c: (c, 0, 0, 0)),
            whole(ny, ny),
            whole(nz, nz),
        ],
        out_specs=[block, sent, sent],
        out_shape=[
            jax.ShapeDtypeStruct((comps, rows, ny, nz), jnp.float32),
            jax.ShapeDtypeStruct((comps, 2, late, nz), log_conf.dtype),
            jax.ShapeDtypeStruct((comps, 2, late, nz), log_conf.dtype),
        ],
        compiler_params=pltpu.CompilerParams(vmem_limit_bytes=16 * 2**20),
        cost_estimate=pl.CostEstimate(
            flops=30 * comps * rows * ny * nz, bytes_accessed=10 * comps * rows * ny * nz, transcendentals=0
        ),
        name="begin",
    )(log_conf, brownian, relax_rate, cols, band(ny), band(nz))


def finish_kernel(start, stop, has_base, u_ref, first_ref, second_ref, w_ref, pick_ref, *refs):
    if has_base:
        base_ref, out_ref, stress, sums = refs
    else:
        out_ref, stress, sums = refs
    rows, ny, nz = u_ref.shape[1:]
    width, nj = stop - start, ny // 4
    own_j, planes, pieces = width // 4, out_ref.shape[0] // 8, nz // LANES
    odd, _ = position()
    for c in range(NC):
        for r in range(rows):
            for piece in range(pieces):
                stress[c, r, piece, 0:LEAD] = jnp.zeros((LEAD, LANES), jnp.float32)
                stress[c, r, piece, LEAD + width :] = jnp.zeros((TAIL, LANES), jnp.float32)

    for side, halo_ref in enumerate((first_ref, second_ref)):
        upper = (odd == side).astype(jnp.int32)
        near, far = 1 - upper, upper
        edge, inner = 3 * upper, 1 + upper

        def chunk(step, carry, halo_ref=halo_ref, near=near, far=far, edge=edge, inner=inner):
            y = pl.multiple_of(step * 16, 16)
            ys, us = pl.ds(y, 16), pl.ds(start + y, 16)
            updated = ([], [])
            for c in range(NC):
                close = halo_ref[c, near, ys].astype(jnp.float32)
                distant = halo_ref[c, far, ys].astype(jnp.float32)
                updated[0].append(u_ref[c, inner, us] - STENCIL * close)
                updated[1].append(u_ref[c, edge, us] + (16.0 * STENCIL) * close - STENCIL * distant)
            for row, (xx, xy, xz, yy, yz, zz) in zip((inner, edge), updated):
                xy2, xz2, yz2 = xy * xy, xz * xz, yz * yz
                values = (
                    xx + 0.5 * (xx * xx + xy2 + xz2),
                    xy + 0.5 * (xy * (xx + yy) + xz * yz),
                    xz + 0.5 * (xz * (xx + zz) + xy * yz),
                    yy + 0.5 * (xy2 + yy * yy + yz2),
                    yz + 0.5 * (yz * (yy + zz) + xy * xz),
                    zz + 0.5 * (xz2 + yz2 + zz * zz),
                )
                for c in range(NC):
                    for piece in range(pieces):
                        lanes = slice(piece * LANES, (piece + 1) * LANES)
                        stress[c, row, piece, pl.ds(y + LEAD, 16)] = values[c][:, lanes]
            return carry

        lax.fori_loop(0, width // 16, chunk, 0)

    taps = {0: ((0, 2), (1, 3), (2, 4)), 1: ((2, 0), (3, 1))}
    for c in range(NC):
        for t in range(2):
            weight = {}
            for row, a in taps[t]:
                for b in range(5):
                    for k in range(2):
                        weight[row, b, k] = w_ref[c, a, 2 * b + k : 2 * b + k + 1]
            for jb in range(own_j // 8 + 1):
                total = [None, None]
                for b in range(5 if jb < own_j // 8 else 2):
                    at = pl.ds(LEAD + 32 * jb + b - 2, 8, stride=4)
                    for row, _ in taps[t]:
                        value = jnp.concatenate([stress[c, row, piece, at] for piece in range(pieces)], axis=1)
                        for k in range(2):
                            term = value * weight[row, b, k]
                            total[k] = term if total[k] is None else total[k] + term
                for k in range(2):
                    sums[c, t, 8 * jb : 8 * jb + 8, k * nz : (k + 1) * nz] = total[k]

    def reduced(values):
        high = values.astype(jnp.bfloat16)
        low = (values - high.astype(jnp.float32)).astype(jnp.bfloat16)
        both = jnp.concatenate([high, low], axis=1)
        return lax.dot_general(
            pick_ref[...], both, (((1,), (1,)), ((), ())), preferred_element_type=jnp.float32
        )

    def put(place, value):
        at = pl.ds(place, planes, stride=8)
        if has_base:
            value = value + base_ref[at, :]
        out_ref[at, :] = value

    first_j = start // 4
    held = min(own_j + 8, nj - first_j)
    for c in range(NC):
        parts = []
        for t in range(2):
            if first_j:
                parts.append(jnp.zeros((first_j, 2 * nz), jnp.float32))
            parts.append(sums[c, t, 0:held])
            if first_j + held < nj:
                parts.append(jnp.zeros((nj - first_j - held, 2 * nz), jnp.float32))
        put(c, reduced(jnp.concatenate(parts, axis=0)))
    if stop == ny:
        beyond = [sums[c, t, own_j : own_j + 1] for c in range(NC) for t in range(2)]
        beyond.append(jnp.zeros((2 * nj - 2 * NC, 2 * nz), jnp.float32))
        put(NC, reduced(jnp.concatenate(beyond, axis=0)))
    else:
        out_ref[pl.ds(NC, planes, stride=8), :] = jnp.zeros((planes, 2 * nj), jnp.float32)
    out_ref[pl.ds(7, planes, stride=8), :] = jnp.zeros((planes, 2 * nj), jnp.float32)


def finish(start, stop, begun, halos, weights, pick, base):
    comps, rows, ny, nz = begun.shape
    planes, nj = nz // 4, ny // 4
    operands = [begun, *halos, weights, pick] + ([] if base is None else [base])
    operands = [pltpu.with_memory_space_constraint(x, pltpu.VMEM) for x in operands]
    return pl.pallas_call(
        functools.partial(finish_kernel, start, stop, base is not None),
        in_specs=[pl.BlockSpec(memory_space=pltpu.VMEM)] * len(operands),
        out_specs=pl.BlockSpec(memory_space=pltpu.VMEM),
        out_shape=jax.ShapeDtypeStruct((planes * 8, 2 * nj), jnp.float32),
        scratch_shapes=[
            pltpu.VMEM((comps, rows, nz // LANES, LEAD + stop - start + TAIL, LANES), jnp.float32),
            pltpu.VMEM((comps, 2, (stop - start) // 4 + 8, 2 * nz), jnp.float32),
        ],
        compiler_params=pltpu.CompilerParams(vmem_limit_bytes=16 * 2**20),
        cost_estimate=pl.CostEstimate(
            flops=80 * comps * (stop - start) * nz, bytes_accessed=32 * comps * (stop - start) * nz, transcendentals=0
        ),
        name="finish",
    )(*operands)


def gather_kernel(in_ref, out_ref):
    count, lanes = out_ref.shape[2], out_ref.shape[3]
    half = lanes // 2
    lane = lax.broadcasted_iota(jnp.int32, (count, lanes), 1)
    row = lax.broadcasted_iota(jnp.int32, (count, lanes), 0)
    low = lane < half
    beyond = in_ref[pl.ds(NC, count, stride=16), :]
    for c in range(NC):
        first = in_ref[pl.ds(c, count, stride=16), :]
        second = in_ref[pl.ds(8 + c, count, stride=16), :]
        own = jnp.where(low, first, pltpu.roll(second, half, 1))
        own += jnp.where(lane == half, pltpu.roll(beyond, half - 2 * c, 1), 0.0)
        after = jnp.where(low, pltpu.roll(first, half, 1), second)
        after += jnp.where(lane == half, pltpu.roll(beyond, half - 2 * c - 1, 1), 0.0)
        out_ref[c, 0] = own + jnp.where(row > 0, pltpu.roll(after, 1, 0), 0.0)


def local(log_conf, brownian, relax_rate, kernel):
    comps, rows, ny, nz = log_conf.shape
    width_gx, width_gy = lax.axis_size("gx"), lax.axis_size("gy")
    planes = nz // 4
    assert comps == NC and rows == 4 and width_gy == 2 and width_gx % 2 == 0
    assert planes == width_gx * width_gy

    swap_first = [(i, i ^ 1) for i in range(width_gx)]
    swap_second = [(i, ((i + 1) ^ 1) - 1) for i in range(1, width_gx - 1)]
    early = 3 * ny // 4
    first, second, cols = pack(log_conf, early)
    halo_early = [lax.ppermute(first, "gx", swap_first), lax.ppermute(second, "gx", swap_second)]
    cols = lax.ppermute(cols, "gy", [(0, 1), (1, 0)])
    begun, first, second = begin(log_conf, brownian, relax_rate, cols, ny - early)
    halo_late = [lax.ppermute(first, "gx", swap_first), lax.ppermute(second, "gx", swap_second)]

    near = jnp.tile(jnp.roll(kernel[..., :4], -2, axis=-1), (1, 1, 1, nz // 4))
    last = jnp.broadcast_to(kernel[..., 4:], near.shape)
    weights = jnp.stack([near, last], axis=3).reshape(comps, 5, 10, nz)
    weights = jnp.pad(weights, ((0, 0), (0, 1), (0, 6), (0, 0)))
    z = lax.broadcasted_iota(jnp.int32, (planes, nz), 1)
    k = lax.broadcasted_iota(jnp.int32, (planes, nz), 0)
    pick = jnp.concatenate([(z + 2) // 4 == k, z == 4 * k + 2] * 2, axis=1).astype(jnp.bfloat16)

    part = finish(0, early, begun, halo_early, weights, pick, None)
    part = finish(early, ny, begun, halo_late, weights, pick, part)
    moved = lax.all_to_all(part.reshape(planes, 8, ny // 2), ("gx", "gy"), 0, 0, tiled=True)
    return pl.pallas_call(
        gather_kernel,
        out_shape=jax.ShapeDtypeStruct((comps, 1, width_gx, ny // 2), jnp.float32),
        in_specs=[pl.BlockSpec(memory_space=pltpu.VMEM)],
        compiler_params=pltpu.CompilerParams(vmem_limit_bytes=4 * 2**20),
        name="gather",
    )(pltpu.with_memory_space_constraint(moved.reshape(planes * 8, ny // 2), pltpu.VMEM))


def solution(mesh):
    return jax.shard_map(
        local,
        mesh=mesh,
        in_specs=(
            P(None, ("grp", "gx"), "gy", None),
            P(None, ("grp", "gx"), "gy", None),
            P(("grp", "gx"), "gy", None),
            P(),
        ),
        out_specs=P(None, ("gx", "gy"), "grp", None),
        check_vma=False,
    )
```

time: 61.1 us -> 91.8 us (1.50)
  Pallas kernels: 12 us -> 48.5 us
  waiting for transfers between devices: 20.1 us -> 8.03 us
  starting transfers between devices: 3.75 us -> 8.71 us
  blocking collectives: 13.9 us -> 14.9 us
    pallas_call x3 -> x4, Pallas kernels: 10.4 us -> 47.7 us  [the longest x1 37.6 us: pack(): pl.pallas_call(pack_kernel, in_specs=[pl.BlockSpec(memory_space=pltpu.HBM...]
    ppermute x3 -> x5, waiting for transfers between devices: 20.1 us -> 8.03 us  [the longest x2 8.02 us: local(): lax.ppermute(first, 'gx', swap_first)]
    ppermute x3 -> x5, starting transfers between devices: 3.75 us -> 8.71 us  [the longest x2 6.06 us: local(): lax.ppermute(first, 'gx', swap_first)]
    dynamic_slice x1 -> x0, local copies, waits for them, and re-layouts: 2.7 us -> none  [local(): lax.dynamic_slice_in_dim(log_conf, 2 - 2 * odd, 2, axis=1)]
    another operation x2, local copies, waits for them, and re-layouts: 5.14 us -> 6.67 us  [local(): near = jnp.tile(jnp.roll(kernel[..., :4], -2, axis=-1), (1, 1, 1, nz // 4))]
    slice x1, local copies, waits for them, and re-layouts: 0.09 us -> 1.06 us  [local(): near = jnp.tile(jnp.roll(kernel[..., :4], -2, axis=-1), (1, 1, 1, nz // 4))]
    all_to_all x1, blocking collectives: 13.9 us -> 14.9 us  [local(): lax.all_to_all(part.reshape(planes, 8, ny // 2), ('gx', 'gy'), 0, 0, tile...]
  transfers between devices with their start and end apart: 3 -> 5, of which waited for: 1 -> 2; matrix products, arithmetic and copies ran while one was open for 15% -> 11% of each run, Pallas kernels for 14% -> 10%
where the time goes in v2:
time: 91.8 us; the launch traced here: 91.5 us
  Pallas kernels  48.5 us (53%)
  blocking collectives  14.9 us (16%)
  local copies, waits for them, and re-layouts  9.69 us (11%)
  starting transfers between devices  8.71 us (9%)
  waiting for transfers between devices  8.03 us (9%)
  other arithmetic  1.57 us (2%)
    pallas_call x1, Pallas kernels, pack(): pl.pallas_call(pack_kernel, in_specs=[pl.BlockSpec(memory_space=pltpu.HBM...  37.6 us
    all_to_all x1, blocking collectives, local(): lax.all_to_all(part.reshape(planes, 8, ny // 2), ('gx', 'gy'), 0, 0, tile...  14.9 us
    ppermute x2, waiting for transfers between devices, local(): lax.ppermute(first, 'gx', swap_first)  8.02 us
    another operation x2, local copies, waits for them, and re-layouts, local(): near = jnp.tile(jnp.roll(kernel[..., :4], -2, axis=-1), (1, 1, 1, nz // 4))  6.67 us
    pallas_call x1, Pallas kernels, begin(): pl.pallas_call(begin_kernel, grid=(comps,), in_specs=[block, block, whole...  6.32 us
    ppermute x2, starting transfers between devices, local(): lax.ppermute(first, 'gx', swap_first)  6.06 us
    pallas_call x2, Pallas kernels, finish(): pl.pallas_call(functools.partial(finish_kernel, start, stop, base is not...  3.87 us
    ppermute x2, starting transfers between devices, local(): lax.ppermute(second, 'gx', swap_second)  2.14 us
  transfers between devices with their start and end apart: 5, of which 2 were waited for; matrix products, arithmetic and copies ran while one was open for 11% of the time, Pallas kernels for 10%

profile of v2, /device:TPU:0, one launch (start us, length us, event | category | flops | bytes accessed | tf_op | source)
XLA Modules:
  0.0 91.5 jit_solution(15246265769620232046)
XLA Ops:
  0.0 37.6 %pack.1 = (bf16[6,2,192,128]{3,2,1,0:T(8,128)(2,1)}, bf16[6,2,192,128]{3,2,1,0:T(8,128)(2,1)}, f32[6,4,2,128]{3,2,1,0:T(2,128)}) custom-call(bf16[6,4,256,128]{3,2,1,0:T(8,128)(2,1)} %f_ref.3), custom_call_target="tpu_custom_call" | custom-call | tf_op jit(solution)/shard_map/pack/pallas_call | solution.py:56
  37.6 0.5 collective-permute-start
  38.1 2.6 %collective-permute-start.3 = (bf16[6,2,192,128]{3,2,1,0:T(8,128)(2,1)}, bf16[6,2,192,128]{3,2,1,0:T(8,128)(2,1)}, u32[]{:S(2)}, u32[]{:S(2)}) collective-permute-start(bf16[6,2,192,128]{3,2,1,0:T(8,128)(2,1)} %get-tuple-element.15), channel_id=1, source_target_pairs={{0,2},{2,0},{4,6},{6,4},{8,10},{10,8},{12,14},{14,12},{16,18},{18,... | collective-permute-start | bytes 1769480 | tf_op jit(solution)/shard_map/ppermute | solution.py:290
  40.7 1.5 %collective-permute-start.4 = (bf16[6,2,192,128]{3,2,1,0:T(8,128)(2,1)}, bf16[6,2,192,128]{3,2,1,0:T(8,128)(2,1)}, u32[]{:S(2)}, u32[]{:S(2)}) collective-permute-start(bf16[6,2,192,128]{3,2,1,0:T(8,128)(2,1)} %get-tuple-element.16), channel_id=1, source_target_pairs={{2,4},{4,2},{6,8},{8,6},{10,12},{12,10},{14,16},{16,14},{18,20},{2... | collective-permute-start | bytes 1769480 | tf_op jit(solution)/shard_map/ppermute | solution.py:290
  42.1 0.1 select_convert_fusion.ty_ref
  42.2 0.1 iota_compare_fusion
  42.3 1.1 %fusion.6 = (f32[6,5,5,2]{3,0,2,1:T(8,128)S(1)}, f32[6,5,5,2]{3,0,2,1:T(8,128)S(1)}) fusion(f32[6,5,5,5]{3,0,2,1:T(8,128)} %param.7), kind=kLoop, calls=%fused_computation.22 | loop fusion | bytes 4800 | tf_op jit(solution)/shard_map/jit(_roll_static)/slice | solution.py:295
  43.3 0.7 pad_maximum_fusion.1
  44.1 0.6 select_convert_fusion.1.tz_ref
  44.7 0.0 copy-done.4
  44.7 0.1 slice.18
  44.8 1.0 %copy.12 = f32[6,5,5,1]{0,2,1,3:T(8,128)} copy(f32[6,5,5,1]{3,0,2,1:T(8,128)S(1)} %slice.18) | data formatting | bytes 1200 | tf_op jit(solution)/shard_map/slice | solution.py:296
  45.8 2.7 %tile.8 = f32[6,5,5,32,4]{4,3,0,2,1:T(8,128)} broadcast(f32[6,5,5,4]{3,0,2,1:T(8,128)} %pad_maximum_fusion.1), dimensions={0,1,2,4} | broadcast | bytes 79200 | tf_op jit(solution)/shard_map/tile | solution.py:295
  48.5 4.0 %tile.9 = f32[6,5,5,1,128]{4,0,2,1,3:T(8,128)} reshape(f32[6,5,5,32,4]{4,3,0,2,1:T(8,128)} %tile.8) | data formatting | bytes 153600 | tf_op jit(solution)/shard_map/tile | solution.py:295
  52.5 0.0 collective-permute-done.cols_ref
  52.5 0.0 copy-done
  52.5 0.0 copy-done.1
  52.5 0.0 copy-done.2
  52.5 0.0 copy-start.3
  52.5 0.7 copy-done.3
  53.2 6.3 %begin.1 = (f32[6,4,256,128]{3,2,1,0:T(8,128)S(1)}, bf16[6,2,64,128]{3,2,1,0:T(8,128)(2,1)S(1)}, bf16[6,2,64,128]{3,2,1,0:T(8,128)(2,1)S(1)}) custom-call(bf16[6,4,256,128]{3,2,1,0:T(8,128)(2,1)S(1)} %copy-done, bf16[6,4,256,128]{3,2,1,0:T(8,128)(2,1)S(1)} %copy-done.1, bf16[4,256,128]{2,1,0:T(8,128)(2,1)S(1)} %copy-done.2, ...), custom_call_target="tpu_custom_call" | custom-call | flops 23592960 | bytes 7864320 | tf_op jit(solution)/shard_map/begin/pallas_call | solution.py:114
  59.6 3.5 %collective-permute-start.1 = (bf16[6,2,64,128]{3,2,1,0:T(8,128)(2,1)S(1)}, bf16[6,2,64,128]{3,2,1,0:T(8,128)(2,1)S(1)}, u32[]{:S(2)}, u32[]{:S(2)}) collective-permute-start(bf16[6,2,64,128]{3,2,1,0:T(8,128)(2,1)S(1)} %get-tuple-element.13), channel_id=1, source_target_pairs={{0,2},{2,0},{4,6},{6,4},{8,10},{10,8},{12,14},{14,12},{16,18},{18,... | collective-permute-start | bytes 589832 | tf_op jit(solution)/shard_map/ppermute | solution.py:293
  63.1 0.7 collective-permute-start.2
  63.7 0.1 stack_broadcast_in_dim.2
  64.0 7.3 %collective-permute-done.3.first_ref = bf16[6,2,192,128]{3,2,1,0:T(8,128)(2,1)} collective-permute-done((bf16[6,2,192,128]{3,2,1,0:T(8,128)(2,1)}, bf16[6,2,192,128]{3,2,1,0:T(8,128)(2,1)}, u32[]{:S(2)}, u32[]{:S(2)}) %collective-permute-start.3) | collective-permute-done | bytes 589856 | tf_op jit(solution)/shard_map/ppermute | solution.py:290
  71.3 0.0 collective-permute-done.4.second_ref
  71.3 3.1 %finish.2.refs_0_ = f32[256,128]{1,0:T(8,128)S(1)} custom-call(f32[6,4,256,128]{3,2,1,0:T(8,128)S(1)} %get-tuple-element.12.u_ref, bf16[6,2,192,128]{3,2,1,0:T(8,128)(2,1)} %collective-permute-done.3.first_ref, bf16[6,2,192,128]{3,2,1,0:T(8,128)(2,1)} %collective-permute-done.4.second_ref, f32[6,6,16,128]{3,2,1,0:T(8,128)S(1)} %pad.4.w_ref, ...), custom_call_target="tpu_custom_call" | custom-call | flops 11796480 | bytes 4718592 | tf_op jit(solution)/shard_map/finish/pallas_call | solution.py:245
  74.4 0.7 collective-permute-done.1.first_ref
  75.1 0.0 collective-permute-done.2.second_ref
  75.1 0.8 finish.3
  75.9 14.9 %all_to_all.5 = f32[32,8,128]{2,1,0:T(8,128)S(1)} all-to-all(f32[32,8,128]{2,1,0:T(8,128)S(1)} %bitcast.9), channel_id=1, replica_groups=mesh['grp'=1,'gx'=16,'gy'=2] {'gx','gy'}, dimensions={0} | all-to-all | bytes 262144 | tf_op jit(solution)/shard_map/all_to_all | solution.py:305
  90.8 0.7 gather.1
  (17 shorter events, 0.1 us)
Async XLA Ops:
  0.0 44.7 %copy-start.4 = (f32[6,5,5,5]{3,0,2,1:T(8,128)S(1)}, f32[6,5,5,5]{3,0,2,1:T(8,128)}, u32[]{:S(2)}) copy-start(f32[6,5,5,5]{3,0,2,1:T(8,128)} %param.7) | copy-start | bytes 9004
  37.6 14.9 %collective-permute-start = (f32[6,4,2,128]{3,2,1,0:T(2,128)}, f32[6,4,2,128]{3,2,1,0:T(2,128)}, u32[]{:S(2)}, u32[]{:S(2)}) collective-permute-start(f32[6,4,2,128]{3,2,1,0:T(2,128)} %get-tuple-element.11), channel_id=1, source_target_pairs={{0,1},{1,0},{2,3},{3,2},{4,5},{5,4},{6,7},{7,6},{8,9},{9,8},{10,11... | collective-permute-start | bytes 73736 | tf_op jit(solution)/shard_map/ppermute | solution.py:291
  38.1 33.2 %collective-permute-start.3 = (bf16[6,2,192,128]{3,2,1,0:T(8,128)(2,1)}, bf16[6,2,192,128]{3,2,1,0:T(8,128)(2,1)}, u32[]{:S(2)}, u32[]{:S(2)}) collective-permute-start(bf16[6,2,192,128]{3,2,1,0:T(8,128)(2,1)} %get-tuple-element.15), channel_id=1, source_target_pairs={{0,2},{2,0},{4,6},{6,4},{8,10},{10,8},{12,14},{14,12},{16,18},{18,... | collective-permute-start | bytes 1769480 | tf_op jit(solution)/shard_map/ppermute | solution.py:290
  40.7 30.7 %collective-permute-start.4 = (bf16[6,2,192,128]{3,2,1,0:T(8,128)(2,1)}, bf16[6,2,192,128]{3,2,1,0:T(8,128)(2,1)}, u32[]{:S(2)}, u32[]{:S(2)}) collective-permute-start(bf16[6,2,192,128]{3,2,1,0:T(8,128)(2,1)} %get-tuple-element.16), channel_id=1, source_target_pairs={{2,4},{4,2},{6,8},{8,6},{10,12},{12,10},{14,16},{16,14},{18,20},{2... | collective-permute-start | bytes 1769480 | tf_op jit(solution)/shard_map/ppermute | solution.py:290
  45.8 6.7 %copy-start = (bf16[6,4,256,128]{3,2,1,0:T(8,128)(2,1)S(1)}, bf16[6,4,256,128]{3,2,1,0:T(8,128)(2,1)}, u32[]{:S(2)}) copy-start(bf16[6,4,256,128]{3,2,1,0:T(8,128)(2,1)} %f_ref.3) | copy-start | bytes 4718596
  45.8 6.7 %copy-start.1 = (bf16[6,4,256,128]{3,2,1,0:T(8,128)(2,1)S(1)}, bf16[6,4,256,128]{3,2,1,0:T(8,128)(2,1)}, u32[]{:S(2)}) copy-start(bf16[6,4,256,128]{3,2,1,0:T(8,128)(2,1)} %b_ref.1) | copy-start | bytes 4718596
  45.8 6.7 %copy-start.2 = (bf16[4,256,128]{2,1,0:T(8,128)(2,1)S(1)}, bf16[4,256,128]{2,1,0:T(8,128)(2,1)}, u32[]{:S(2)}) copy-start(bf16[4,256,128]{2,1,0:T(8,128)(2,1)} %r_ref.1) | copy-start | bytes 786436
  52.5 0.8 copy-start.3
  53.2 10.5 %copy-start.6 = (f32[6,5,5,1]{0,2,1,3:T(8,128)S(1)}, f32[6,5,5,1]{0,2,1,3:T(8,128)}, u32[]{:S(2)}) copy-start(f32[6,5,5,1]{0,2,1,3:T(8,128)} %copy.12) | copy-start | bytes 1804
  53.2 10.6 %copy-start.5 = (f32[6,5,5,1,128]{4,0,2,1,3:T(8,128)S(1)}, f32[6,5,5,1,128]{4,0,2,1,3:T(8,128)}, u32[]{:S(2)}) copy-start(f32[6,5,5,1,128]{4,0,2,1,3:T(8,128)} %tile.9) | copy-start | bytes 230404
  59.6 15.6 %collective-permute-start.1 = (bf16[6,2,64,128]{3,2,1,0:T(8,128)(2,1)S(1)}, bf16[6,2,64,128]{3,2,1,0:T(8,128)(2,1)S(1)}, u32[]{:S(2)}, u32[]{:S(2)}) collective-permute-start(bf16[6,2,64,128]{3,2,1,0:T(8,128)(2,1)S(1)} %get-tuple-element.13), channel_id=1, source_target_pairs={{0,2},{2,0},{4,6},{6,4},{8,10},{10,8},{12,14},{14,12},{16,18},{18,... | collective-permute-start | bytes 589832 | tf_op jit(solution)/shard_map/ppermute | solution.py:293
  63.1 12.1 %collective-permute-start.2 = (bf16[6,2,64,128]{3,2,1,0:T(8,128)(2,1)S(1)}, bf16[6,2,64,128]{3,2,1,0:T(8,128)(2,1)S(1)}, u32[]{:S(2)}, u32[]{:S(2)}) collective-permute-start(bf16[6,2,64,128]{3,2,1,0:T(8,128)(2,1)S(1)} %get-tuple-element.14), channel_id=1, source_target_pairs={{2,4},{4,2},{6,8},{8,6},{10,12},{12,10},{14,16},{16,14},{18,20},{2... | collective-permute-start | bytes 589832 | tf_op jit(solution)/shard_map/ppermute | solution.py:293

commit v3 on v2

--- a/solution.py
+++ b/solution.py
@@ -28,49 +28,79 @@
     return lax.rem(lax.axis_index("gx"), 2), lax.axis_index("gy")
 
 
-def pack_kernel(f_ref, first_ref, second_ref, cols_ref, edges, sems):
+def pack_kernel(second, f_ref, *refs):
     odd, gy = position()
     comps, rows, ny, nz = f_ref.shape
-    stop = first_ref.shape[2]
+    if second:
+        out_ref, cols_ref, sems, edges, edge_sem = refs
+    else:
+        out_ref, sems = refs
+    row = 2 * odd if second else 2 - 2 * odd
     copies = []
     for c in range(comps):
-        for s, (out_ref, row) in enumerate(((first_ref, 2 - 2 * odd), (second_ref, 2 * odd))):
-            source = f_ref.at[c, pl.ds(row, 2), pl.ds(0, stop)]
-            copies.append(pltpu.make_async_copy(source, out_ref.at[c], sems.at[2 * c + s]))
-    at = pl.multiple_of((1 - gy) * (ny - 16), 16)
-    copies.append(pltpu.make_async_copy(f_ref.at[:, :, pl.ds(at, 16)], edges, sems.at[2 * comps]))
+        source = f_ref.at[c, pl.ds(row, 2), pl.ds(0, out_ref.shape[2])]
+        copies.append(pltpu.make_async_copy(source, out_ref.at[c], sems.at[c]))
+    if second:
+        at = pl.multiple_of((1 - gy) * (ny - 16), 16)
+        copies.append(pltpu.make_async_copy(f_ref.at[:, :, pl.ds(at, 16)], edges, edge_sem))
     for copy in copies:
         copy.start()
     for copy in copies:
         copy.wait()
-    for c in range(comps):
-        for x in range(rows):
-            values = edges[c, x].astype(jnp.float32)
-            cols_ref[c, x] = jnp.where(gy == 0, values[14:16], values[0:2])
-
-
-def pack(log_conf, stop):
+    if second:
+        for c in range(comps):
+            for x in range(rows):
+                values = edges[c, x].astype(jnp.float32)
+                cols_ref[c, x] = jnp.where(gy == 0, values[14:16], values[0:2])
+
+
+def pack(log_conf, stop, second):
     comps, rows, ny, nz = log_conf.shape
-    sent = jax.ShapeDtypeStruct((comps, 2, stop, nz), log_conf.dtype)
-    anywhere = pl.BlockSpec(memory_space=pl.ANY)
+    shapes = [jax.ShapeDtypeStruct((comps, 2, stop, nz), log_conf.dtype)]
+    scratch = [pltpu.SemaphoreType.DMA((comps,))]
+    if second:
+        shapes.append(jax.ShapeDtypeStruct((comps, rows, 2, nz), jnp.float32))
+        scratch += [pltpu.VMEM((comps, rows, 16, nz), log_conf.dtype), pltpu.SemaphoreType.DMA]
     return pl.pallas_call(
-        pack_kernel,
+        functools.partial(pack_kernel, second),
         in_specs=[pl.BlockSpec(memory_space=pltpu.HBM)],
-        out_specs=[anywhere, anywhere, pl.BlockSpec(memory_space=pltpu.VMEM)],
-        out_shape=[sent, sent, jax.ShapeDtypeStruct((comps, rows, 2, nz), jnp.float32)],
-        scratch_shapes=[
-            pltpu.VMEM((comps, rows, 16, nz), log_conf.dtype),
-            pltpu.SemaphoreType.DMA((2 * comps + 1,)),
-        ],
-        compiler_params=pltpu.CompilerParams(vmem_limit_bytes=8 * 2**20),
+        out_specs=[pl.BlockSpec(memory_space=pltpu.VMEM)] * len(shapes),
+        out_shape=shapes,
+        scratch_shapes=scratch,
+        compiler_params=pltpu.CompilerParams(vmem_limit_bytes=4 * 2**20),
         name="pack",
     )(pltpu.with_memory_space_constraint(log_conf, pltpu.HBM))
 
 
-def begin_kernel(f_ref, b_ref, r_ref, cols_ref, ty_ref, tz_ref, out_ref, first_ref, second_ref):
+def begin_kernel(
+    f_ref, b_ref, r_ref, cols_ref, k_ref, out_ref, first_ref, second_ref, w_ref, pick_ref, ty_ref, tz_ref
+):
     rows, ny = f_ref.shape[1], f_ref.shape[2]
     odd, gy = position()
     step = 64
+
+    @pl.when(pl.program_id(0) == 0)
+    def _():
+        nz = f_ref.shape[3]
+        ty_ref[...] = band(ny)
+        tz_ref[...] = band(nz)
+        planes = pick_ref.shape[0]
+        z = lax.broadcasted_iota(jnp.int32, (planes, nz), 1)
+        k = lax.broadcasted_iota(jnp.int32, (planes, nz), 0)
+        for piece, chosen in enumerate((lax.shift_right_logical(z + 2, 2) == k, z == 4 * k + 2)):
+            value = jnp.where(chosen, 1.0, 0.0).astype(jnp.bfloat16)
+            pick_ref[:, piece * nz : (piece + 1) * nz] = value
+            pick_ref[:, (piece + 2) * nz : (piece + 3) * nz] = value
+        tap = (lax.broadcasted_iota(jnp.int32, (NC, nz), 1) + 2) & 3
+        for a in range(5):
+            for b in range(5):
+                taps = k_ref[a, b]
+                near = jnp.broadcast_to(taps[:, 0:1], (NC, nz))
+                for e in range(1, 4):
+                    near = jnp.where(tap == e, taps[:, e : e + 1], near)
+                w_ref[a, b, 0] = near
+                w_ref[a, b, 1] = jnp.broadcast_to(taps[:, 4:5], (NC, nz))
+
     late = first_ref.shape[2]
     first_ref[0] = f_ref[0, pl.ds(2 - 2 * odd, 2), ny - late : ny]
     second_ref[0] = f_ref[0, pl.ds(2 * odd, 2), ny - late : ny]
@@ -106,7 +136,7 @@
             out_ref[0, x, ny - 8 : ny] += STENCIL * extra
 
 
-def begin(log_conf, brownian, relax_rate, cols, late):
+def begin(log_conf, brownian, relax_rate, cols, kernel, late):
     comps, rows, ny, nz = log_conf.shape
     whole = lambda *shape: pl.BlockSpec(shape, lambda c: (0,) * len(shape))
     block = pl.BlockSpec((1, rows, ny, nz), lambda c: (c, 0, 0, 0))
@@ -119,21 +149,23 @@
             block,
             whole(rows, ny, nz),
             pl.BlockSpec((1, rows, 2, nz), lambda c: (c, 0, 0, 0)),
-            whole(ny, ny),
-            whole(nz, nz),
+            whole(5, 5, comps, 5),
         ],
-        out_specs=[block, sent, sent],
+        out_specs=[block, sent, sent, whole(5, 5, 2, comps, nz), whole(nz // 4, 4 * nz)],
         out_shape=[
             jax.ShapeDtypeStruct((comps, rows, ny, nz), jnp.float32),
             jax.ShapeDtypeStruct((comps, 2, late, nz), log_conf.dtype),
             jax.ShapeDtypeStruct((comps, 2, late, nz), log_conf.dtype),
+            jax.ShapeDtypeStruct((5, 5, 2, comps, nz), jnp.float32),
+            jax.ShapeDtypeStruct((nz // 4, 4 * nz), jnp.bfloat16),
         ],
+        scratch_shapes=[pltpu.VMEM((ny, ny), jnp.bfloat16), pltpu.VMEM((nz, nz), jnp.bfloat16)],
         compiler_params=pltpu.CompilerParams(vmem_limit_bytes=16 * 2**20),
         cost_estimate=pl.CostEstimate(
             flops=30 * comps * rows * ny * nz, bytes_accessed=10 * comps * rows * ny * nz, transcendentals=0
         ),
         name="begin",
-    )(log_conf, brownian, relax_rate, cols, band(ny), band(nz))
+    )(log_conf, brownian, relax_rate, cols, jnp.transpose(kernel, (1, 2, 0, 3)))
 
 
 def finish_kernel(start, stop, has_base, u_ref, first_ref, second_ref, w_ref, pick_ref, *refs):
@@ -190,7 +222,7 @@
             for row, a in taps[t]:
                 for b in range(5):
                     for k in range(2):
-                        weight[row, b, k] = w_ref[c, a, 2 * b + k : 2 * b + k + 1]
+                        weight[row, b, k] = w_ref[a, b, k, c : c + 1]
             for jb in range(own_j // 8 + 1):
                 total = [None, None]
                 for b in range(5 if jb < own_j // 8 else 2):
@@ -286,19 +318,12 @@
     swap_first = [(i, i ^ 1) for i in range(width_gx)]
     swap_second = [(i, ((i + 1) ^ 1) - 1) for i in range(1, width_gx - 1)]
     early = 3 * ny // 4
-    first, second, cols = pack(log_conf, early)
+    (first,) = pack(log_conf, early, False)
+    second, cols = pack(log_conf, early, True)
     halo_early = [lax.ppermute(first, "gx", swap_first), lax.ppermute(second, "gx", swap_second)]
     cols = lax.ppermute(cols, "gy", [(0, 1), (1, 0)])
-    begun, first, second = begin(log_conf, brownian, relax_rate, cols, ny - early)
+    begun, first, second, weights, pick = begin(log_conf, brownian, relax_rate, cols, kernel, ny - early)
     halo_late = [lax.ppermute(first, "gx", swap_first), lax.ppermute(second, "gx", swap_second)]
-
-    near = jnp.tile(jnp.roll(kernel[..., :4], -2, axis=-1), (1, 1, 1, nz // 4))
-    last = jnp.broadcast_to(kernel[..., 4:], near.shape)
-    weights = jnp.stack([near, last], axis=3).reshape(comps, 5, 10, nz)
-    weights = jnp.pad(weights, ((0, 0), (0, 1), (0, 6), (0, 0)))
-    z = lax.broadcasted_iota(jnp.int32, (planes, nz), 1)
-    k = lax.broadcasted_iota(jnp.int32, (planes, nz), 0)
-    pick = jnp.concatenate([(z + 2) // 4 == k, z == 4 * k + 2] * 2, axis=1).astype(jnp.bfloat16)
 
     part = finish(0, early, begun, halo_early, weights, pick, None)
     part = finish(early, ny, begun, halo_late, weights, pick, part)

time: 91.8 us -> 54.6 us (0.59)
  Pallas kernels: 48.5 us -> 12 us
  waiting for transfers between devices: 8.03 us -> 18.8 us
  local copies, waits for them, and re-layouts: 9.69 us -> 0.01 us
  other arithmetic: 1.57 us -> 0 us
    pallas_call x1 -> x2, Pallas kernels: 37.6 us -> 2.59 us  [pack(): pl.pallas_call(functools.partial(pack_kernel, second), in_specs=[pl.Block...]
    ppermute x2, waiting for transfers between devices: 8.02 us -> 17.6 us  [local(): lax.ppermute(first, 'gx', swap_first)]
    another operation x4 -> x0, local copies, waits for them, and re-layouts: 6.76 us -> none  [the longest x2 6.67 us: local(): near = jnp.tile(jnp.roll(kernel[..., :4], -2, axis=-1), (1, 1, 1, nz // 4))]
    slice x3 -> x0, local copies, waits for them, and re-layouts: 2.09 us -> none  [the longest x1 1.06 us: local(): near = jnp.tile(jnp.roll(kernel[..., :4], -2, axis=-1), (1, 1, 1, nz // 4))]
    ppermute x2, starting transfers between devices: 6.06 us -> 7.28 us  [local(): lax.ppermute(first, 'gx', swap_first)]
    pallas_call x2, Pallas kernels: 3.87 us -> 2.66 us  [finish(): pl.pallas_call(functools.partial(finish_kernel, start, stop, base is not...]
    ppermute x1, waiting for transfers between devices: 0.01 us -> 1.18 us  [local(): cols = lax.ppermute(cols, 'gy', [(0, 1), (1, 0)])]
  transfers between devices with their start and end apart: 5 -> 5, of which waited for: 2 -> 3; matrix products, arithmetic and copies ran while one was open for 11% -> 0% of each run, Pallas kernels for 10% -> 17%
where the time goes in v3:
time: 54.6 us; the launch traced here: 54.4 us
  waiting for transfers between devices  18.8 us (34%)
  blocking collectives  14.9 us (27%)
  Pallas kernels  12 us (22%)
  starting transfers between devices  8.71 us (16%)
    ppermute x2, waiting for transfers between devices, local(): lax.ppermute(first, 'gx', swap_first)  17.6 us
    all_to_all x1, blocking collectives, local(): lax.all_to_all(part.reshape(planes, 8, ny // 2), ('gx', 'gy'), 0, 0, tile...  14.9 us
    ppermute x2, starting transfers between devices, local(): lax.ppermute(first, 'gx', swap_first)  7.28 us
    pallas_call x1, Pallas kernels, begin(): pl.pallas_call(begin_kernel, grid=(comps,), in_specs=[block, block, whole...  5.98 us
    pallas_call x2, Pallas kernels, finish(): pl.pallas_call(functools.partial(finish_kernel, start, stop, base is not...  2.66 us
    pallas_call x2, Pallas kernels, pack(): pl.pallas_call(functools.partial(pack_kernel, second), in_specs=[pl.Block...  2.59 us
    ppermute x2, starting transfers between devices, local(): lax.ppermute(second, 'gx', swap_second)  1.36 us
    ppermute x1, waiting for transfers between devices, local(): cols = lax.ppermute(cols, 'gy', [(0, 1), (1, 0)])  1.18 us
  transfers between devices with their start and end apart: 5, of which 3 were waited for; matrix products, arithmetic and copies ran while one was open for 0% of the time, Pallas kernels for 17%

profile of v3, /device:TPU:0, one launch (start us, length us, event | category | flops | bytes accessed | tf_op | source)
XLA Modules:
  0.0 54.4 jit_solution(12914872185640248329)
XLA Ops:
  0.0 0.0 copy-start
  0.0 0.0 copy-start.3
  0.0 0.0 copy-start.2
  0.0 0.0 copy-start.1
  0.0 1.3 %pack.3 = bf16[6,2,192,128]{3,2,1,0:T(8,128)(2,1)S(1)} custom-call(bf16[6,4,256,128]{3,2,1,0:T(8,128)(2,1)} %f_ref.5), custom_call_target="tpu_custom_call" | custom-call | tf_op jit(solution)/shard_map/pack/pallas_call | solution.py:64
  1.4 3.0 %collective-permute-start.3 = (bf16[6,2,192,128]{3,2,1,0:T(8,128)(2,1)S(1)}, bf16[6,2,192,128]{3,2,1,0:T(8,128)(2,1)S(1)}, u32[]{:S(2)}, u32[]{:S(2)}) collective-permute-start(bf16[6,2,192,128]{3,2,1,0:T(8,128)(2,1)S(1)} %pack.3), channel_id=1, source_target_pairs={{0,2},{2,0},{4,6},{6,4},{8,10},{10,8},{12,14},{14,12},{16,18},{18,... | collective-permute-start | bytes 1769480 | tf_op jit(solution)/shard_map/ppermute | solution.py:323
  4.4 1.3 %pack.2 = (bf16[6,2,192,128]{3,2,1,0:T(8,128)(2,1)S(1)}, f32[6,4,2,128]{3,2,1,0:T(2,128)S(1)}) custom-call(bf16[6,4,256,128]{3,2,1,0:T(8,128)(2,1)} %f_ref.5), custom_call_target="tpu_custom_call" | custom-call | tf_op jit(solution)/shard_map/pack/pallas_call | solution.py:64
  5.6 0.7 %collective-permute-start.4 = (bf16[6,2,192,128]{3,2,1,0:T(8,128)(2,1)S(1)}, bf16[6,2,192,128]{3,2,1,0:T(8,128)(2,1)S(1)}, u32[]{:S(2)}, u32[]{:S(2)}) collective-permute-start(bf16[6,2,192,128]{3,2,1,0:T(8,128)(2,1)S(1)} %get-tuple-element.18), channel_id=1, source_target_pairs={{2,4},{4,2},{6,8},{8,6},{10,12},{12,10},{14,16},{16,14},{18,20},{2... | collective-permute-start | bytes 1769480 | tf_op jit(solution)/shard_map/ppermute | solution.py:323
  6.3 0.1 collective-permute-start
  6.4 1.2 %collective-permute-done.cols_ref = f32[6,4,2,128]{3,2,1,0:T(2,128)S(1)} collective-permute-done((f32[6,4,2,128]{3,2,1,0:T(2,128)S(1)}, f32[6,4,2,128]{3,2,1,0:T(2,128)S(1)}, u32[]{:S(2)}, u32[]{:S(2)}) %collective-permute-start) | collective-permute-done | bytes 24608 | tf_op jit(solution)/shard_map/ppermute | solution.py:324
  7.6 0.0 copy-done
  7.6 0.0 copy-done.3
  7.6 0.0 copy-done.2
  7.6 0.0 copy-done.1
  7.6 6.0 %begin.1 = (f32[6,4,256,128]{3,2,1,0:T(8,128)S(1)}, bf16[6,2,64,128]{3,2,1,0:T(8,128)(2,1)S(1)}, bf16[6,2,64,128]{3,2,1,0:T(8,128)(2,1)S(1)}, f32[5,5,2,6,128]{4,3,2,1,0:T(8,128)S(1)}, bf16[32,512]{1,0:T(8,128)(2,1)S(1)}) custom-call(bf16[6,4,256,128]{3,2,1,0:T(8,128)(2,1)S(1)} %copy-done, bf16[6,4,256,128]{3,2,1,0:T(8,128)(2,1)S(1)} %copy-done.1, ...), custom_call_target="tpu_custom_call" | custom-call | flops 23592960 | bytes 7864320 | tf_op jit(solution)/shard_map/begin/pallas_call | solution.py:144
  13.6 4.3 %collective-permute-start.1 = (bf16[6,2,64,128]{3,2,1,0:T(8,128)(2,1)S(1)}, bf16[6,2,64,128]{3,2,1,0:T(8,128)(2,1)S(1)}, u32[]{:S(2)}, u32[]{:S(2)}) collective-permute-start(bf16[6,2,64,128]{3,2,1,0:T(8,128)(2,1)S(1)} %get-tuple-element.14), channel_id=1, source_target_pairs={{0,2},{2,0},{4,6},{6,4},{8,10},{10,8},{12,14},{14,12},{16,18},{18,... | collective-permute-start | bytes 589832 | tf_op jit(solution)/shard_map/ppermute | solution.py:326
  17.9 0.7 %collective-permute-start.2 = (bf16[6,2,64,128]{3,2,1,0:T(8,128)(2,1)S(1)}, bf16[6,2,64,128]{3,2,1,0:T(8,128)(2,1)S(1)}, u32[]{:S(2)}, u32[]{:S(2)}) collective-permute-start(bf16[6,2,64,128]{3,2,1,0:T(8,128)(2,1)S(1)} %get-tuple-element.15), channel_id=1, source_target_pairs={{2,4},{4,2},{6,8},{8,6},{10,12},{12,10},{14,16},{16,14},{18,20},{2... | collective-permute-start | bytes 589832 | tf_op jit(solution)/shard_map/ppermute | solution.py:326
  18.5 16.4 %collective-permute-done.3.first_ref = bf16[6,2,192,128]{3,2,1,0:T(8,128)(2,1)S(1)} collective-permute-done((bf16[6,2,192,128]{3,2,1,0:T(8,128)(2,1)S(1)}, bf16[6,2,192,128]{3,2,1,0:T(8,128)(2,1)S(1)}, u32[]{:S(2)}, u32[]{:S(2)}) %collective-permute-start.3) | collective-permute-done | bytes 589856 | tf_op jit(solution)/shard_map/ppermute | solution.py:323
  35.0 0.0 collective-permute-done.4.second_ref
  35.0 1.9 %finish.2.refs_0_ = f32[256,128]{1,0:T(8,128)S(1)} custom-call(f32[6,4,256,128]{3,2,1,0:T(8,128)S(1)} %get-tuple-element.13.u_ref, bf16[6,2,192,128]{3,2,1,0:T(8,128)(2,1)S(1)} %collective-permute-done.3.first_ref, bf16[6,2,192,128]{3,2,1,0:T(8,128)(2,1)S(1)} %collective-permute-done.4.second_ref, f32[5,5,2,6,128]{4,3,2,1,0:T(8,128)S(1)} %get-tuple-element.16.w_ref, ...), custom_call_target="tpu_custom_call" | custom-call | flops 11796480 | bytes 4718592 | tf_op jit(solution)/shard_map/finish/pallas_call | solution.py:277
  36.8 1.2 %collective-permute-done.1.first_ref = bf16[6,2,64,128]{3,2,1,0:T(8,128)(2,1)S(1)} collective-permute-done((bf16[6,2,64,128]{3,2,1,0:T(8,128)(2,1)S(1)}, bf16[6,2,64,128]{3,2,1,0:T(8,128)(2,1)S(1)}, u32[]{:S(2)}, u32[]{:S(2)}) %collective-permute-start.1) | collective-permute-done | bytes 196640 | tf_op jit(solution)/shard_map/ppermute | solution.py:326
  38.0 0.0 collective-permute-done.2.second_ref
  38.0 0.8 %finish.3 = f32[256,128]{1,0:T(8,128)S(1)} custom-call(f32[6,4,256,128]{3,2,1,0:T(8,128)S(1)} %get-tuple-element.13.u_ref, bf16[6,2,64,128]{3,2,1,0:T(8,128)(2,1)S(1)} %collective-permute-done.1.first_ref, bf16[6,2,64,128]{3,2,1,0:T(8,128)(2,1)S(1)} %collective-permute-done.2.second_ref, f32[5,5,2,6,128]{4,3,2,1,0:T(8,128)S(1)} %get-tuple-element.16.w_ref, ...), custom_call_target="tpu_custom_call" | custom-call | flops 3932160 | bytes 1572864 | tf_op jit(solution)/shard_map/finish/pallas_call | solution.py:277
  38.8 14.9 %all_to_all.5 = f32[32,8,128]{2,1,0:T(8,128)S(1)} all-to-all(f32[32,8,128]{2,1,0:T(8,128)S(1)} %bitcast.3), channel_id=1, replica_groups=mesh['grp'=1,'gx'=16,'gy'=2] {'gx','gy'}, dimensions={0} | all-to-all | bytes 262144 | tf_op jit(solution)/shard_map/all_to_all | solution.py:330
  53.7 0.7 %gather.1 = f32[6,1,16,128]{3,2,1,0:T(8,128)} custom-call(f32[256,128]{1,0:T(8,128)S(1)} %bitcast.4), custom_call_target="tpu_custom_call" | custom-call | tf_op jit(solution)/shard_map/gather/pallas_call | solution.py:331
Async XLA Ops:
  0.0 7.6 %copy-start = (bf16[6,4,256,128]{3,2,1,0:T(8,128)(2,1)S(1)}, bf16[6,4,256,128]{3,2,1,0:T(8,128)(2,1)}, u32[]{:S(2)}) copy-start(bf16[6,4,256,128]{3,2,1,0:T(8,128)(2,1)} %f_ref.5) | copy-start | bytes 4718596
  0.0 7.6 %copy-start.3 = (f32[6,5,5,5]{3,0,2,1:T(8,128)S(1)}, f32[6,5,5,5]{3,0,2,1:T(8,128)}, u32[]{:S(2)}) copy-start(f32[6,5,5,5]{3,0,2,1:T(8,128)} %param.7) | copy-start | bytes 9004
  0.0 7.6 %copy-start.2 = (bf16[4,256,128]{2,1,0:T(8,128)(2,1)S(1)}, bf16[4,256,128]{2,1,0:T(8,128)(2,1)}, u32[]{:S(2)}) copy-start(bf16[4,256,128]{2,1,0:T(8,128)(2,1)} %r_ref.1) | copy-start | bytes 786436
  0.0 7.6 %copy-start.1 = (bf16[6,4,256,128]{3,2,1,0:T(8,128)(2,1)S(1)}, bf16[6,4,256,128]{3,2,1,0:T(8,128)(2,1)}, u32[]{:S(2)}) copy-start(bf16[6,4,256,128]{3,2,1,0:T(8,128)(2,1)} %b_ref.1) | copy-start | bytes 4718596
  1.4 33.6 %collective-permute-start.3 = (bf16[6,2,192,128]{3,2,1,0:T(8,128)(2,1)S(1)}, bf16[6,2,192,128]{3,2,1,0:T(8,128)(2,1)S(1)}, u32[]{:S(2)}, u32[]{:S(2)}) collective-permute-start(bf16[6,2,192,128]{3,2,1,0:T(8,128)(2,1)S(1)} %pack.3), channel_id=1, source_target_pairs={{0,2},{2,0},{4,6},{6,4},{8,10},{10,8},{12,14},{14,12},{16,18},{18,... | collective-permute-start | bytes 1769480 | tf_op jit(solution)/shard_map/ppermute | solution.py:323
  5.6 29.3 %collective-permute-start.4 = (bf16[6,2,192,128]{3,2,1,0:T(8,128)(2,1)S(1)}, bf16[6,2,192,128]{3,2,1,0:T(8,128)(2,1)S(1)}, u32[]{:S(2)}, u32[]{:S(2)}) collective-permute-start(bf16[6,2,192,128]{3,2,1,0:T(8,128)(2,1)S(1)} %get-tuple-element.18), channel_id=1, source_target_pairs={{2,4},{4,2},{6,8},{8,6},{10,12},{12,10},{14,16},{16,14},{18,20},{2... | collective-permute-start | bytes 1769480 | tf_op jit(solution)/shard_map/ppermute | solution.py:323
  6.3 1.3 %collective-permute-start = (f32[6,4,2,128]{3,2,1,0:T(2,128)S(1)}, f32[6,4,2,128]{3,2,1,0:T(2,128)S(1)}, u32[]{:S(2)}, u32[]{:S(2)}) collective-permute-start(f32[6,4,2,128]{3,2,1,0:T(2,128)S(1)} %get-tuple-element.12), channel_id=1, source_target_pairs={{0,1},{1,0},{2,3},{3,2},{4,5},{5,4},{6,7},{7,6},{8,9},{9,8},{10,11... | collective-permute-start | bytes 73736 | tf_op jit(solution)/shard_map/ppermute | solution.py:324
  13.6 24.4 %collective-permute-start.1 = (bf16[6,2,64,128]{3,2,1,0:T(8,128)(2,1)S(1)}, bf16[6,2,64,128]{3,2,1,0:T(8,128)(2,1)S(1)}, u32[]{:S(2)}, u32[]{:S(2)}) collective-permute-start(bf16[6,2,64,128]{3,2,1,0:T(8,128)(2,1)S(1)} %get-tuple-element.14), channel_id=1, source_target_pairs={{0,2},{2,0},{4,6},{6,4},{8,10},{10,8},{12,14},{14,12},{16,18},{18,... | collective-permute-start | bytes 589832 | tf_op jit(solution)/shard_map/ppermute | solution.py:326
  17.9 20.2 %collective-permute-start.2 = (bf16[6,2,64,128]{3,2,1,0:T(8,128)(2,1)S(1)}, bf16[6,2,64,128]{3,2,1,0:T(8,128)(2,1)S(1)}, u32[]{:S(2)}, u32[]{:S(2)}) collective-permute-start(bf16[6,2,64,128]{3,2,1,0:T(8,128)(2,1)S(1)} %get-tuple-element.15), channel_id=1, source_target_pairs={{2,4},{4,2},{6,8},{8,6},{10,12},{12,10},{14,16},{16,14},{18,20},{2... | collective-permute-start | bytes 589832 | tf_op jit(solution)/shard_map/ppermute | solution.py:326

commit v4 on v3

--- a/solution.py
+++ b/solution.py
@@ -73,10 +73,11 @@
 
 
 def begin_kernel(
-    f_ref, b_ref, r_ref, cols_ref, k_ref, out_ref, first_ref, second_ref, w_ref, pick_ref, ty_ref, tz_ref
+    cuts, f_ref, b_ref, r_ref, cols_ref, k_ref, out_ref, w_ref, pick_ref, *refs
 ):
     rows, ny = f_ref.shape[1], f_ref.shape[2]
     odd, gy = position()
+    ty_ref, tz_ref = refs[-2:]
     step = 64
 
     @pl.when(pl.program_id(0) == 0)
@@ -101,9 +102,9 @@
                 w_ref[a, b, 0] = near
                 w_ref[a, b, 1] = jnp.broadcast_to(taps[:, 4:5], (NC, nz))
 
-    late = first_ref.shape[2]
-    first_ref[0] = f_ref[0, pl.ds(2 - 2 * odd, 2), ny - late : ny]
-    second_ref[0] = f_ref[0, pl.ds(2 * odd, 2), ny - late : ny]
+    for (start, stop), first_ref, second_ref in zip(cuts, refs[0:-2:2], refs[1:-2:2]):
+        first_ref[0] = f_ref[0, pl.ds(2 - 2 * odd, 2), start:stop]
+        second_ref[0] = f_ref[0, pl.ds(2 * odd, 2), start:stop]
     for x in range(rows):
         plane = f_ref[0, x]
         for y in range(0, ny, step):
@@ -136,13 +137,13 @@
             out_ref[0, x, ny - 8 : ny] += STENCIL * extra
 
 
-def begin(log_conf, brownian, relax_rate, cols, kernel, late):
+def begin(log_conf, brownian, relax_rate, cols, kernel, cuts):
     comps, rows, ny, nz = log_conf.shape
     whole = lambda *shape: pl.BlockSpec(shape, lambda c: (0,) * len(shape))
     block = pl.BlockSpec((1, rows, ny, nz), lambda c: (c, 0, 0, 0))
-    sent = pl.BlockSpec((1, 2, late, nz), lambda c: (c, 0, 0, 0))
+    heights = [stop - start for start, stop in cuts for _ in range(2)]
     return pl.pallas_call(
-        begin_kernel,
+        functools.partial(begin_kernel, cuts),
         grid=(comps,),
         in_specs=[
             block,
@@ -151,21 +152,21 @@
             pl.BlockSpec((1, rows, 2, nz), lambda c: (c, 0, 0, 0)),
             whole(5, 5, comps, 5),
         ],
-        out_specs=[block, sent, sent, whole(5, 5, 2, comps, nz), whole(nz // 4, 4 * nz)],
+        out_specs=[block, whole(5, 5, 2, comps, nz), whole(nz // 4, 4 * nz)]
+        + [pl.BlockSpec((1, 2, height, nz), lambda c: (c, 0, 0, 0)) for height in heights],
         out_shape=[
             jax.ShapeDtypeStruct((comps, rows, ny, nz), jnp.float32),
-            jax.ShapeDtypeStruct((comps, 2, late, nz), log_conf.dtype),
-            jax.ShapeDtypeStruct((comps, 2, late, nz), log_conf.dtype),
             jax.ShapeDtypeStruct((5, 5, 2, comps, nz), jnp.float32),
             jax.ShapeDtypeStruct((nz // 4, 4 * nz), jnp.bfloat16),
-        ],
+        ]
+        + [jax.ShapeDtypeStruct((comps, 2, height, nz), log_conf.dtype) for height in heights],
         scratch_shapes=[pltpu.VMEM((ny, ny), jnp.bfloat16), pltpu.VMEM((nz, nz), jnp.bfloat16)],
         compiler_params=pltpu.CompilerParams(vmem_limit_bytes=16 * 2**20),
         cost_estimate=pl.CostEstimate(
             flops=30 * comps * rows * ny * nz, bytes_accessed=10 * comps * rows * ny * nz, transcendentals=0
         ),
         name="begin",
-    )(log_conf, brownian, relax_rate, cols, jnp.transpose(kernel, (1, 2, 0, 3)))
+    )(*(pltpu.with_memory_space_constraint(x, pltpu.HBM) for x in (log_conf, brownian, relax_rate)), cols, jnp.transpose(kernel, (1, 2, 0, 3)))
 
 
 def finish_kernel(start, stop, has_base, u_ref, first_ref, second_ref, w_ref, pick_ref, *refs):
@@ -177,6 +178,10 @@
     width, nj = stop - start, ny // 4
     own_j, planes, pieces = width // 4, out_ref.shape[0] // 8, nz // LANES
     odd, _ = position()
+    compact = len(sums.shape) == 2
+    if compact:
+        for t in range(2):
+            sums[t * nj + 8 * NC : (t + 1) * nj] = jnp.zeros((nj - 8 * NC, 2 * nz), jnp.float32)
     for c in range(NC):
         for r in range(rows):
             for piece in range(pieces):
@@ -233,7 +238,14 @@
                             term = value * weight[row, b, k]
                             total[k] = term if total[k] is None else total[k] + term
                 for k in range(2):
-                    sums[c, t, 8 * jb : 8 * jb + 8, k * nz : (k + 1) * nz] = total[k]
+                    lanes = slice(k * nz, (k + 1) * nz)
+                    if not compact:
+                        sums[c, t, 8 * jb : 8 * jb + 8, lanes] = total[k]
+                    elif jb == 0:
+                        sums[t * nj + 8 * c : t * nj + 8 * c + 8, lanes] = total[k]
+                    else:
+                        at = t * nj + 8 * NC + c
+                        sums[at : at + 1, lanes] = total[k][0:1]
 
     def reduced(values):
         high = values.astype(jnp.bfloat16)
@@ -248,6 +260,16 @@
         if has_base:
             value = value + base_ref[at, :]
         out_ref[at, :] = value
+
+    if compact:
+        lane = lax.broadcasted_iota(jnp.int32, (planes, 2 * nj), 1)
+        spread = reduced(sums[...])
+        for c in range(NC):
+            moved = pltpu.roll(spread, nj - 8 - 8 * c, 1)
+            put(c, jnp.where((lane & (nj - 1)) >= nj - 8, moved, 0.0))
+        out_ref[pl.ds(NC, planes, stride=8), :] = spread
+        out_ref[pl.ds(7, planes, stride=8), :] = jnp.zeros((planes, 2 * nj), jnp.float32)
+        return
 
     first_j = start // 4
     held = min(own_j + 8, nj - first_j)
@@ -260,18 +282,14 @@
             if first_j + held < nj:
                 parts.append(jnp.zeros((nj - first_j - held, 2 * nz), jnp.float32))
         put(c, reduced(jnp.concatenate(parts, axis=0)))
-    if stop == ny:
-        beyond = [sums[c, t, own_j : own_j + 1] for c in range(NC) for t in range(2)]
-        beyond.append(jnp.zeros((2 * nj - 2 * NC, 2 * nz), jnp.float32))
-        put(NC, reduced(jnp.concatenate(beyond, axis=0)))
-    else:
-        out_ref[pl.ds(NC, planes, stride=8), :] = jnp.zeros((planes, 2 * nj), jnp.float32)
-    out_ref[pl.ds(7, planes, stride=8), :] = jnp.zeros((planes, 2 * nj), jnp.float32)
+    for place in (NC, 7):
+        out_ref[pl.ds(place, planes, stride=8), :] = jnp.zeros((planes, 2 * nj), jnp.float32)
 
 
 def finish(start, stop, begun, halos, weights, pick, base):
     comps, rows, ny, nz = begun.shape
     planes, nj = nz // 4, ny // 4
+    places = (2 * nj, 2 * nz) if stop == ny else (comps, 2, (stop - start) // 4 + 8, 2 * nz)
     operands = [begun, *halos, weights, pick] + ([] if base is None else [base])
     operands = [pltpu.with_memory_space_constraint(x, pltpu.VMEM) for x in operands]
     return pl.pallas_call(
@@ -281,7 +299,7 @@
         out_shape=jax.ShapeDtypeStruct((planes * 8, 2 * nj), jnp.float32),
         scratch_shapes=[
             pltpu.VMEM((comps, rows, nz // LANES, LEAD + stop - start + TAIL, LANES), jnp.float32),
-            pltpu.VMEM((comps, 2, (stop - start) // 4 + 8, 2 * nz), jnp.float32),
+            pltpu.VMEM(places, jnp.float32),
         ],
         compiler_params=pltpu.CompilerParams(vmem_limit_bytes=16 * 2**20),
         cost_estimate=pl.CostEstimate(
@@ -302,9 +320,9 @@
         first = in_ref[pl.ds(c, count, stride=16), :]
         second = in_ref[pl.ds(8 + c, count, stride=16), :]
         own = jnp.where(low, first, pltpu.roll(second, half, 1))
-        own += jnp.where(lane == half, pltpu.roll(beyond, half - 2 * c, 1), 0.0)
+        own += jnp.where(lane == half, pltpu.roll(beyond, half - 8 * NC - c, 1), 0.0)
         after = jnp.where(low, pltpu.roll(first, half, 1), second)
-        after += jnp.where(lane == half, pltpu.roll(beyond, half - 2 * c - 1, 1), 0.0)
+        after += jnp.where(lane == half, pltpu.roll(beyond, lanes - 8 * NC - c, 1), 0.0)
         out_ref[c, 0] = own + jnp.where(row > 0, pltpu.roll(after, 1, 0), 0.0)
 
 
@@ -313,20 +331,23 @@
     width_gx, width_gy = lax.axis_size("gx"), lax.axis_size("gy")
     planes = nz // 4
     assert comps == NC and rows == 4 and width_gy == 2 and width_gx % 2 == 0
-    assert planes == width_gx * width_gy
+    assert planes == width_gx * width_gy and ny == 256
 
     swap_first = [(i, i ^ 1) for i in range(width_gx)]
     swap_second = [(i, ((i + 1) ^ 1) - 1) for i in range(1, width_gx - 1)]
-    early = 3 * ny // 4
+    cuts = [(0, ny // 2), (ny // 2, 7 * ny // 8), (7 * ny // 8, ny)]
+    early = cuts[0][1]
     (first,) = pack(log_conf, early, False)
     second, cols = pack(log_conf, early, True)
-    halo_early = [lax.ppermute(first, "gx", swap_first), lax.ppermute(second, "gx", swap_second)]
+    halos = [[lax.ppermute(first, "gx", swap_first), lax.ppermute(second, "gx", swap_second)]]
     cols = lax.ppermute(cols, "gy", [(0, 1), (1, 0)])
-    begun, first, second, weights, pick = begin(log_conf, brownian, relax_rate, cols, kernel, ny - early)
-    halo_late = [lax.ppermute(first, "gx", swap_first), lax.ppermute(second, "gx", swap_second)]
-
-    part = finish(0, early, begun, halo_early, weights, pick, None)
-    part = finish(early, ny, begun, halo_late, weights, pick, part)
+    begun, weights, pick, *sent = begin(log_conf, brownian, relax_rate, cols, kernel, cuts[1:])
+    for first, second in zip(sent[0::2], sent[1::2]):
+        halos.append([lax.ppermute(first, "gx", swap_first), lax.ppermute(second, "gx", swap_second)])
+
+    part = None
+    for (start, stop), pair in zip(cuts, halos):
+        part = finish(start, stop, begun, pair, weights, pick, part)
     moved = lax.all_to_all(part.reshape(planes, 8, ny // 2), ("gx", "gy"), 0, 0, tiled=True)
     return pl.pallas_call(
         gather_kernel,

time: 54.6 us -> 54.3 us (level)
  waiting for transfers between devices: 18.8 us -> 12.1 us
  starting transfers between devices: 8.71 us -> 13.6 us
  Pallas kernels: 12 us -> 13.3 us
    ppermute x2 -> x3, waiting for transfers between devices: 17.6 us -> 10.9 us  [local(): lax.ppermute(first, 'gx', swap_first)]
    ppermute x2 -> x3, starting transfers between devices: 7.28 us -> 11.5 us  [local(): lax.ppermute(first, 'gx', swap_first)]
    pallas_call x1, Pallas kernels: 5.98 us -> 7.3 us  [begin(): pl.pallas_call(functools.partial(begin_kernel, cuts), grid=(comps,), in_s...]
    ppermute x2 -> x3, starting transfers between devices: 1.36 us -> 2.01 us  [local(): lax.ppermute(second, 'gx', swap_second)]
    pallas_call x2 -> x3, Pallas kernels: 2.66 us -> 2.99 us  [finish(): pl.pallas_call(functools.partial(finish_kernel, start, stop, base is not...]
  transfers between devices with their start and end apart: 5 -> 7, of which waited for: 3 -> 2; matrix products, arithmetic and copies ran while one was open for 0% -> 0% of each run, Pallas kernels for 17% -> 20%
where the time goes in v4:
time: 54.3 us; the launch traced here: 53.9 us
  blocking collectives  14.8 us (27%)
  starting transfers between devices  13.6 us (25%)
  Pallas kernels  13.3 us (24%)
  waiting for transfers between devices  12.1 us (22%)
    all_to_all x1, blocking collectives, local(): lax.all_to_all(part.reshape(planes, 8, ny // 2), ('gx', 'gy'), 0, 0, tile...  14.8 us
    ppermute x3, starting transfers between devices, local(): lax.ppermute(first, 'gx', swap_first)  11.5 us
    ppermute x3, waiting for transfers between devices, local(): lax.ppermute(first, 'gx', swap_first)  10.9 us
    pallas_call x1, Pallas kernels, begin(): pl.pallas_call(functools.partial(begin_kernel, cuts), grid=(comps,), in_s...  7.3 us
    pallas_call x3, Pallas kernels, finish(): pl.pallas_call(functools.partial(finish_kernel, start, stop, base is not...  2.99 us
    pallas_call x2, Pallas kernels, pack(): pl.pallas_call(functools.partial(pack_kernel, second), in_specs=[pl.Block...  2.25 us
    ppermute x3, starting transfers between devices, local(): lax.ppermute(second, 'gx', swap_second)  2.01 us
    ppermute x1, waiting for transfers between devices, local(): cols = lax.ppermute(cols, 'gy', [(0, 1), (1, 0)])  1.18 us
  transfers between devices with their start and end apart: 7, of which 2 were waited for; matrix products, arithmetic and copies ran while one was open for 0% of the time, Pallas kernels for 20%

profile of v4, /device:TPU:0, one launch (start us, length us, event | category | flops | bytes accessed | tf_op | source)
XLA Modules:
  0.0 53.9 jit_solution(16632860246461400276)
XLA Ops:
  0.0 0.0 copy-start
  0.0 1.1 %pack.3 = bf16[6,2,128,128]{3,2,1,0:T(8,128)(2,1)S(1)} custom-call(bf16[6,4,256,128]{3,2,1,0:T(8,128)(2,1)} %f_ref.5), custom_call_target="tpu_custom_call" | custom-call | tf_op jit(solution)/shard_map/pack/pallas_call | solution.py:64
  1.1 3.0 %collective-permute-start.5 = (bf16[6,2,128,128]{3,2,1,0:T(8,128)(2,1)S(1)}, bf16[6,2,128,128]{3,2,1,0:T(8,128)(2,1)S(1)}, u32[]{:S(2)}, u32[]{:S(2)}) collective-permute-start(bf16[6,2,128,128]{3,2,1,0:T(8,128)(2,1)S(1)} %pack.3), channel_id=1, source_target_pairs={{0,2},{2,0},{4,6},{6,4},{8,10},{10,8},{12,14},{14,12},{16,18},{18,... | collective-permute-start | bytes 1179656 | tf_op jit(solution)/shard_map/ppermute | solution.py:342
  4.1 1.2 %pack.2 = (bf16[6,2,128,128]{3,2,1,0:T(8,128)(2,1)S(1)}, f32[6,4,2,128]{3,2,1,0:T(2,128)S(1)}) custom-call(bf16[6,4,256,128]{3,2,1,0:T(8,128)(2,1)} %f_ref.5), custom_call_target="tpu_custom_call" | custom-call | tf_op jit(solution)/shard_map/pack/pallas_call | solution.py:64
  5.3 0.7 %collective-permute-start.6 = (bf16[6,2,128,128]{3,2,1,0:T(8,128)(2,1)S(1)}, bf16[6,2,128,128]{3,2,1,0:T(8,128)(2,1)S(1)}, u32[]{:S(2)}, u32[]{:S(2)}) collective-permute-start(bf16[6,2,128,128]{3,2,1,0:T(8,128)(2,1)S(1)} %get-tuple-element.22), channel_id=1, source_target_pairs={{2,4},{4,2},{6,8},{8,6},{10,12},{12,10},{14,16},{16,14},{18,20},{2... | collective-permute-start | bytes 1179656 | tf_op jit(solution)/shard_map/ppermute | solution.py:342
  6.0 0.1 collective-permute-start
  6.0 1.2 %collective-permute-done.cols_ref = f32[6,4,2,128]{3,2,1,0:T(2,128)S(1)} collective-permute-done((f32[6,4,2,128]{3,2,1,0:T(2,128)S(1)}, f32[6,4,2,128]{3,2,1,0:T(2,128)S(1)}, u32[]{:S(2)}, u32[]{:S(2)}) %collective-permute-start) | collective-permute-done | bytes 24608 | tf_op jit(solution)/shard_map/ppermute | solution.py:343
  7.2 0.0 copy-done
  7.2 7.3 %begin.1 = (f32[6,4,256,128]{3,2,1,0:T(8,128)S(1)}, f32[5,5,2,6,128]{4,3,2,1,0:T(8,128)S(1)}, bf16[32,512]{1,0:T(8,128)(2,1)S(1)}, bf16[6,2,96,128]{3,2,1,0:T(8,...) custom-call(bf16[6,4,256,128]{3,2,1,0:T(8,128)(2,1)} %f_ref.5, ...), custom_call_target="tpu_custom_call" | custom-call | flops 23592960 | bytes 7864320 | tf_op jit(solution)/shard_map/begin/pallas_call | solution.py:145
  14.5 4.3 %collective-permute-start.3 = (bf16[6,2,96,128]{3,2,1,0:T(8,128)(2,1)S(1)}, bf16[6,2,96,128]{3,2,1,0:T(8,128)(2,1)S(1)}, u32[]{:S(2)}, u32[]{:S(2)}) collective-permute-start(bf16[6,2,96,128]{3,2,1,0:T(8,128)(2,1)S(1)} %get-tuple-element.20), channel_id=1, source_target_pairs={{0,2},{2,0},{4,6},{6,4},{8,10},{10,8},{12,14},{14,12},{16,18},{18,... | collective-permute-start | bytes 884744 | tf_op jit(solution)/shard_map/ppermute | solution.py:346
  18.8 0.7 %collective-permute-start.4 = (bf16[6,2,96,128]{3,2,1,0:T(8,128)(2,1)S(1)}, bf16[6,2,96,128]{3,2,1,0:T(8,128)(2,1)S(1)}, u32[]{:S(2)}, u32[]{:S(2)}) collective-permute-start(bf16[6,2,96,128]{3,2,1,0:T(8,128)(2,1)S(1)} %get-tuple-element.21), channel_id=1, source_target_pairs={{2,4},{4,2},{6,8},{8,6},{10,12},{12,10},{14,16},{16,14},{18,20},{2... | collective-permute-start | bytes 884744 | tf_op jit(solution)/shard_map/ppermute | solution.py:346
  19.5 4.3 %collective-permute-start.1 = (bf16[6,2,32,128]{3,2,1,0:T(8,128)(2,1)S(1)}, bf16[6,2,32,128]{3,2,1,0:T(8,128)(2,1)S(1)}, u32[]{:S(2)}, u32[]{:S(2)}) collective-permute-start(bf16[6,2,32,128]{3,2,1,0:T(8,128)(2,1)S(1)} %get-tuple-element.16), channel_id=1, source_target_pairs={{0,2},{2,0},{4,6},{6,4},{8,10},{10,8},{12,14},{14,12},{16,18},{18,... | collective-permute-start | bytes 294920 | tf_op jit(solution)/shard_map/ppermute | solution.py:346
  23.7 0.0 collective-permute-done.5.first_ref
  23.8 0.7 %collective-permute-start.2 = (bf16[6,2,32,128]{3,2,1,0:T(8,128)(2,1)S(1)}, bf16[6,2,32,128]{3,2,1,0:T(8,128)(2,1)S(1)}, u32[]{:S(2)}, u32[]{:S(2)}) collective-permute-start(bf16[6,2,32,128]{3,2,1,0:T(8,128)(2,1)S(1)} %get-tuple-element.17), channel_id=1, source_target_pairs={{2,4},{4,2},{6,8},{8,6},{10,12},{12,10},{14,16},{16,14},{18,20},{2... | collective-permute-start | bytes 294920 | tf_op jit(solution)/shard_map/ppermute | solution.py:346
  24.4 0.0 collective-permute-done.6.second_ref
  24.4 1.3 %finish.3.refs_0_ = f32[256,128]{1,0:T(8,128)S(1)} custom-call(f32[6,4,256,128]{3,2,1,0:T(8,128)S(1)} %get-tuple-element.15.u_ref, bf16[6,2,128,128]{3,2,1,0:T(8,128)(2,1)S(1)} %collective-permute-done.5.first_ref, bf16[6,2,128,128]{3,2,1,0:T(8,128)(2,1)S(1)} %collective-permute-done.6.second_ref, f32[5,5,2,6,128]{4,3,2,1,0:T(8,128)S(1)} %get-tuple-element.18.w_ref, ...), custom_call_target="tpu_custom_call" | custom-call | flops 7864320 | bytes 3145728 | tf_op jit(solution)/shard_map/finish/pallas_call | solution.py:295
  25.8 10.9 %collective-permute-done.3.first_ref = bf16[6,2,96,128]{3,2,1,0:T(8,128)(2,1)S(1)} collective-permute-done((bf16[6,2,96,128]{3,2,1,0:T(8,128)(2,1)S(1)}, bf16[6,2,96,128]{3,2,1,0:T(8,128)(2,1)S(1)}, u32[]{:S(2)}, u32[]{:S(2)}) %collective-permute-start.3) | collective-permute-done | bytes 294944 | tf_op jit(solution)/shard_map/ppermute | solution.py:346
  36.7 0.0 collective-permute-done.4.second_ref
  36.7 1.1 %finish.4.refs_0_ = f32[256,128]{1,0:T(8,128)S(1)} custom-call(f32[6,4,256,128]{3,2,1,0:T(8,128)S(1)} %get-tuple-element.15.u_ref, bf16[6,2,96,128]{3,2,1,0:T(8,128)(2,1)S(1)} %collective-permute-done.3.first_ref, bf16[6,2,96,128]{3,2,1,0:T(8,128)(2,1)S(1)} %collective-permute-done.4.second_ref, f32[5,5,2,6,128]{4,3,2,1,0:T(8,128)S(1)} %get-tuple-element.18.w_ref, ...), custom_call_target="tpu_custom_call" | custom-call | flops 5898240 | bytes 2359296 | tf_op jit(solution)/shard_map/finish/pallas_call | solution.py:295
  37.8 0.0 collective-permute-done.1.first_ref
  37.8 0.0 collective-permute-done.2.second_ref
  37.8 0.6 %finish.5 = f32[256,128]{1,0:T(8,128)S(1)} custom-call(f32[6,4,256,128]{3,2,1,0:T(8,128)S(1)} %get-tuple-element.15.u_ref, bf16[6,2,32,128]{3,2,1,0:T(8,128)(2,1)S(1)} %collective-permute-done.1.first_ref, bf16[6,2,32,128]{3,2,1,0:T(8,128)(2,1)S(1)} %collective-permute-done.2.second_ref, f32[5,5,2,6,128]{4,3,2,1,0:T(8,128)S(1)} %get-tuple-element.18.w_ref, ...), custom_call_target="tpu_custom_call" | custom-call | flops 1966080 | bytes 786432 | tf_op jit(solution)/shard_map/finish/pallas_call | solution.py:295
  38.4 14.8 %all_to_all.5 = f32[32,8,128]{2,1,0:T(8,128)S(1)} all-to-all(f32[32,8,128]{2,1,0:T(8,128)S(1)} %bitcast.4), channel_id=1, replica_groups=mesh['grp'=1,'gx'=16,'gy'=2] {'gx','gy'}, dimensions={0} | all-to-all | bytes 262144 | tf_op jit(solution)/shard_map/all_to_all | solution.py:351
  53.2 0.7 %gather.1 = f32[6,1,16,128]{3,2,1,0:T(8,128)} custom-call(f32[256,128]{1,0:T(8,128)S(1)} %bitcast.3), custom_call_target="tpu_custom_call" | custom-call | tf_op jit(solution)/shard_map/gather/pallas_call | solution.py:352
Async XLA Ops:
  0.0 7.2 %copy-start = (f32[6,5,5,5]{3,0,2,1:T(8,128)S(1)}, f32[6,5,5,5]{3,0,2,1:T(8,128)}, u32[]{:S(2)}) copy-start(f32[6,5,5,5]{3,0,2,1:T(8,128)} %param.7) | copy-start | bytes 9004
  1.1 22.7 %collective-permute-start.5 = (bf16[6,2,128,128]{3,2,1,0:T(8,128)(2,1)S(1)}, bf16[6,2,128,128]{3,2,1,0:T(8,128)(2,1)S(1)}, u32[]{:S(2)}, u32[]{:S(2)}) collective-permute-start(bf16[6,2,128,128]{3,2,1,0:T(8,128)(2,1)S(1)} %pack.3), channel_id=1, source_target_pairs={{0,2},{2,0},{4,6},{6,4},{8,10},{10,8},{12,14},{14,12},{16,18},{18,... | collective-permute-start | bytes 1179656 | tf_op jit(solution)/shard_map/ppermute | solution.py:342
  5.3 19.2 %collective-permute-start.6 = (bf16[6,2,128,128]{3,2,1,0:T(8,128)(2,1)S(1)}, bf16[6,2,128,128]{3,2,1,0:T(8,128)(2,1)S(1)}, u32[]{:S(2)}, u32[]{:S(2)}) collective-permute-start(bf16[6,2,128,128]{3,2,1,0:T(8,128)(2,1)S(1)} %get-tuple-element.22), channel_id=1, source_target_pairs={{2,4},{4,2},{6,8},{8,6},{10,12},{12,10},{14,16},{16,14},{18,20},{2... | collective-permute-start | bytes 1179656 | tf_op jit(solution)/shard_map/ppermute | solution.py:342
  6.0 1.3 %collective-permute-start = (f32[6,4,2,128]{3,2,1,0:T(2,128)S(1)}, f32[6,4,2,128]{3,2,1,0:T(2,128)S(1)}, u32[]{:S(2)}, u32[]{:S(2)}) collective-permute-start(f32[6,4,2,128]{3,2,1,0:T(2,128)S(1)} %get-tuple-element.14), channel_id=1, source_target_pairs={{0,1},{1,0},{2,3},{3,2},{4,5},{5,4},{6,7},{7,6},{8,9},{9,8},{10,11... | collective-permute-start | bytes 73736 | tf_op jit(solution)/shard_map/ppermute | solution.py:343
  14.5 22.2 %collective-permute-start.3 = (bf16[6,2,96,128]{3,2,1,0:T(8,128)(2,1)S(1)}, bf16[6,2,96,128]{3,2,1,0:T(8,128)(2,1)S(1)}, u32[]{:S(2)}, u32[]{:S(2)}) collective-permute-start(bf16[6,2,96,128]{3,2,1,0:T(8,128)(2,1)S(1)} %get-tuple-element.20), channel_id=1, source_target_pairs={{0,2},{2,0},{4,6},{6,4},{8,10},{10,8},{12,14},{14,12},{16,18},{18,... | collective-permute-start | bytes 884744 | tf_op jit(solution)/shard_map/ppermute | solution.py:346
  18.8 17.9 %collective-permute-start.4 = (bf16[6,2,96,128]{3,2,1,0:T(8,128)(2,1)S(1)}, bf16[6,2,96,128]{3,2,1,0:T(8,128)(2,1)S(1)}, u32[]{:S(2)}, u32[]{:S(2)}) collective-permute-start(bf16[6,2,96,128]{3,2,1,0:T(8,128)(2,1)S(1)} %get-tuple-element.21), channel_id=1, source_target_pairs={{2,4},{4,2},{6,8},{8,6},{10,12},{12,10},{14,16},{16,14},{18,20},{2... | collective-permute-start | bytes 884744 | tf_op jit(solution)/shard_map/ppermute | solution.py:346
  19.5 18.3 %collective-permute-start.1 = (bf16[6,2,32,128]{3,2,1,0:T(8,128)(2,1)S(1)}, bf16[6,2,32,128]{3,2,1,0:T(8,128)(2,1)S(1)}, u32[]{:S(2)}, u32[]{:S(2)}) collective-permute-start(bf16[6,2,32,128]{3,2,1,0:T(8,128)(2,1)S(1)} %get-tuple-element.16), channel_id=1, source_target_pairs={{0,2},{2,0},{4,6},{6,4},{8,10},{10,8},{12,14},{14,12},{16,18},{18,... | collective-permute-start | bytes 294920 | tf_op jit(solution)/shard_map/ppermute | solution.py:346
  23.8 14.0 %collective-permute-start.2 = (bf16[6,2,32,128]{3,2,1,0:T(8,128)(2,1)S(1)}, bf16[6,2,32,128]{3,2,1,0:T(8,128)(2,1)S(1)}, u32[]{:S(2)}, u32[]{:S(2)}) collective-permute-start(bf16[6,2,32,128]{3,2,1,0:T(8,128)(2,1)S(1)} %get-tuple-element.17), channel_id=1, source_target_pairs={{2,4},{4,2},{6,8},{8,6},{10,12},{12,10},{14,16},{16,14},{18,20},{2... | collective-permute-start | bytes 294920 | tf_op jit(solution)/shard_map/ppermute | solution.py:346

commit v5 on v4

--- a/solution.py
+++ b/solution.py
@@ -12,6 +12,7 @@
 NOISE_AMP = 0.3
 NC = 6
 LANES = 128
+ROWS = NC + 1
 LEAD = 8
 TAIL = 32
 
@@ -37,9 +38,7 @@
         out_ref, sems = refs
     row = 2 * odd if second else 2 - 2 * odd
     copies = []
-    for c in range(comps):
-        source = f_ref.at[c, pl.ds(row, 2), pl.ds(0, out_ref.shape[2])]
-        copies.append(pltpu.make_async_copy(source, out_ref.at[c], sems.at[c]))
+    copies.append(pltpu.make_async_copy(f_ref.at[:, pl.ds(row, 2), pl.ds(0, out_ref.shape[2])], out_ref, sems))
     if second:
         at = pl.multiple_of((1 - gy) * (ny - 16), 16)
         copies.append(pltpu.make_async_copy(f_ref.at[:, :, pl.ds(at, 16)], edges, edge_sem))
@@ -57,7 +56,7 @@
 def pack(log_conf, stop, second):
     comps, rows, ny, nz = log_conf.shape
     shapes = [jax.ShapeDtypeStruct((comps, 2, stop, nz), log_conf.dtype)]
-    scratch = [pltpu.SemaphoreType.DMA((comps,))]
+    scratch = [pltpu.SemaphoreType.DMA]
     if second:
         shapes.append(jax.ShapeDtypeStruct((comps, rows, 2, nz), jnp.float32))
         scratch += [pltpu.VMEM((comps, rows, 16, nz), log_conf.dtype), pltpu.SemaphoreType.DMA]
@@ -176,7 +175,7 @@
         out_ref, stress, sums = refs
     rows, ny, nz = u_ref.shape[1:]
     width, nj = stop - start, ny // 4
-    own_j, planes, pieces = width // 4, out_ref.shape[0] // 8, nz // LANES
+    own_j, planes, pieces = width // 4, out_ref.shape[0] // ROWS, nz // LANES
     odd, _ = position()
     compact = len(sums.shape) == 2
     if compact:
@@ -256,7 +255,7 @@
         )
 
     def put(place, value):
-        at = pl.ds(place, planes, stride=8)
+        at = pl.ds(place, planes, stride=ROWS)
         if has_base:
             value = value + base_ref[at, :]
         out_ref[at, :] = value
@@ -267,8 +266,7 @@
         for c in range(NC):
             moved = pltpu.roll(spread, nj - 8 - 8 * c, 1)
             put(c, jnp.where((lane & (nj - 1)) >= nj - 8, moved, 0.0))
-        out_ref[pl.ds(NC, planes, stride=8), :] = spread
-        out_ref[pl.ds(7, planes, stride=8), :] = jnp.zeros((planes, 2 * nj), jnp.float32)
+        out_ref[pl.ds(NC, planes, stride=ROWS), :] = spread
         return
 
     first_j = start // 4
@@ -282,8 +280,7 @@
             if first_j + held < nj:
                 parts.append(jnp.zeros((nj - first_j - held, 2 * nz), jnp.float32))
         put(c, reduced(jnp.concatenate(parts, axis=0)))
-    for place in (NC, 7):
-        out_ref[pl.ds(place, planes, stride=8), :] = jnp.zeros((planes, 2 * nj), jnp.float32)
+    out_ref[pl.ds(NC, planes, stride=ROWS), :] = jnp.zeros((planes, 2 * nj), jnp.float32)
 
 
 def finish(start, stop, begun, halos, weights, pick, base):
@@ -296,7 +293,7 @@
         functools.partial(finish_kernel, start, stop, base is not None),
         in_specs=[pl.BlockSpec(memory_space=pltpu.VMEM)] * len(operands),
         out_specs=pl.BlockSpec(memory_space=pltpu.VMEM),
-        out_shape=jax.ShapeDtypeStruct((planes * 8, 2 * nj), jnp.float32),
+        out_shape=jax.ShapeDtypeStruct((planes * ROWS, 2 * nj), jnp.float32),
         scratch_shapes=[
             pltpu.VMEM((comps, rows, nz // LANES, LEAD + stop - start + TAIL, LANES), jnp.float32),
             pltpu.VMEM(places, jnp.float32),
@@ -315,10 +312,10 @@
     lane = lax.broadcasted_iota(jnp.int32, (count, lanes), 1)
     row = lax.broadcasted_iota(jnp.int32, (count, lanes), 0)
     low = lane < half
-    beyond = in_ref[pl.ds(NC, count, stride=16), :]
+    beyond = in_ref[pl.ds(NC, count, stride=2 * ROWS), :]
     for c in range(NC):
-        first = in_ref[pl.ds(c, count, stride=16), :]
-        second = in_ref[pl.ds(8 + c, count, stride=16), :]
+        first = in_ref[pl.ds(c, count, stride=2 * ROWS), :]
+        second = in_ref[pl.ds(ROWS + c, count, stride=2 * ROWS), :]
         own = jnp.where(low, first, pltpu.roll(second, half, 1))
         own += jnp.where(lane == half, pltpu.roll(beyond, half - 8 * NC - c, 1), 0.0)
         after = jnp.where(low, pltpu.roll(first, half, 1), second)
@@ -348,14 +345,14 @@
     part = None
     for (start, stop), pair in zip(cuts, halos):
         part = finish(start, stop, begun, pair, weights, pick, part)
-    moved = lax.all_to_all(part.reshape(planes, 8, ny // 2), ("gx", "gy"), 0, 0, tiled=True)
+    moved = lax.all_to_all(part.reshape(planes, 1, ROWS * ny // 2), ("gx", "gy"), 0, 0, tiled=True)
     return pl.pallas_call(
         gather_kernel,
         out_shape=jax.ShapeDtypeStruct((comps, 1, width_gx, ny // 2), jnp.float32),
         in_specs=[pl.BlockSpec(memory_space=pltpu.VMEM)],
         compiler_params=pltpu.CompilerParams(vmem_limit_bytes=4 * 2**20),
         name="gather",
-    )(pltpu.with_memory_space_constraint(moved.reshape(planes * 8, ny // 2), pltpu.VMEM))
+    )(pltpu.with_memory_space_constraint(moved.reshape(planes * ROWS, ny // 2), pltpu.VMEM))
 
 
 def solution(mesh):

time: 54.3 us -> 54 us (level)
  no operation moved by 1% of the time
where the time goes in v5:
time: 54 us; the launch traced here: 53.7 us
  blocking collectives  14.6 us (27%)
  starting transfers between devices  13.6 us (25%)
  Pallas kernels  13.1 us (24%)
  waiting for transfers between devices  12.3 us (23%)
    all_to_all x1, blocking collectives, local(): lax.all_to_all(part.reshape(planes, 1, ROWS * ny // 2), ('gx', 'gy'), 0,...  14.6 us
    ppermute x3, starting transfers between devices, local(): lax.ppermute(first, 'gx', swap_first)  11.6 us
    ppermute x3, waiting for transfers between devices, local(): lax.ppermute(first, 'gx', swap_first)  11.1 us
    pallas_call x1, Pallas kernels, begin(): pl.pallas_call(functools.partial(begin_kernel, cuts), grid=(comps,), in_s...  7.29 us
    pallas_call x3, Pallas kernels, finish(): pl.pallas_call(functools.partial(finish_kernel, start, stop, base is not...  2.98 us
    pallas_call x2, Pallas kernels, pack(): pl.pallas_call(functools.partial(pack_kernel, second), in_specs=[pl.Block...  2.08 us
    ppermute x3, starting transfers between devices, local(): lax.ppermute(second, 'gx', swap_second)  2.01 us
    ppermute x1, waiting for transfers between devices, local(): cols = lax.ppermute(cols, 'gy', [(0, 1), (1, 0)])  1.18 us
  transfers between devices with their start and end apart: 7, of which 2 were waited for; matrix products, arithmetic and copies ran while one was open for 0% of the time, Pallas kernels for 20%

profile of v5, /device:TPU:0, one launch (start us, length us, event | category | flops | bytes accessed | tf_op | source)
XLA Modules:
  0.0 53.7 jit_solution(9852864757941935954)
XLA Ops:
  0.0 0.0 copy-start
  0.0 1.0 %pack.3 = bf16[6,2,128,128]{3,2,1,0:T(8,128)(2,1)S(1)} custom-call(bf16[6,4,256,128]{3,2,1,0:T(8,128)(2,1)} %f_ref.5), custom_call_target="tpu_custom_call" | custom-call | tf_op jit(solution)/shard_map/pack/pallas_call | solution.py:63
  1.0 3.0 %collective-permute-start.5 = (bf16[6,2,128,128]{3,2,1,0:T(8,128)(2,1)S(1)}, bf16[6,2,128,128]{3,2,1,0:T(8,128)(2,1)S(1)}, u32[]{:S(2)}, u32[]{:S(2)}) collective-permute-start(bf16[6,2,128,128]{3,2,1,0:T(8,128)(2,1)S(1)} %pack.3), channel_id=1, source_target_pairs={{0,2},{2,0},{4,6},{6,4},{8,10},{10,8},{12,14},{14,12},{16,18},{18,... | collective-permute-start | bytes 1179656 | tf_op jit(solution)/shard_map/ppermute | solution.py:339
  4.1 1.0 %pack.2 = (bf16[6,2,128,128]{3,2,1,0:T(8,128)(2,1)S(1)}, f32[6,4,2,128]{3,2,1,0:T(2,128)S(1)}) custom-call(bf16[6,4,256,128]{3,2,1,0:T(8,128)(2,1)} %f_ref.5), custom_call_target="tpu_custom_call" | custom-call | tf_op jit(solution)/shard_map/pack/pallas_call | solution.py:63
  5.1 0.7 %collective-permute-start.6 = (bf16[6,2,128,128]{3,2,1,0:T(8,128)(2,1)S(1)}, bf16[6,2,128,128]{3,2,1,0:T(8,128)(2,1)S(1)}, u32[]{:S(2)}, u32[]{:S(2)}) collective-permute-start(bf16[6,2,128,128]{3,2,1,0:T(8,128)(2,1)S(1)} %get-tuple-element.22), channel_id=1, source_target_pairs={{2,4},{4,2},{6,8},{8,6},{10,12},{12,10},{14,16},{16,14},{18,20},{2... | collective-permute-start | bytes 1179656 | tf_op jit(solution)/shard_map/ppermute | solution.py:339
  5.8 0.1 collective-permute-start
  5.9 1.2 %collective-permute-done.cols_ref = f32[6,4,2,128]{3,2,1,0:T(2,128)S(1)} collective-permute-done((f32[6,4,2,128]{3,2,1,0:T(2,128)S(1)}, f32[6,4,2,128]{3,2,1,0:T(2,128)S(1)}, u32[]{:S(2)}, u32[]{:S(2)}) %collective-permute-start) | collective-permute-done | bytes 24608 | tf_op jit(solution)/shard_map/ppermute | solution.py:340
  7.1 0.0 copy-done
  7.1 7.3 %begin.1 = (f32[6,4,256,128]{3,2,1,0:T(8,128)S(1)}, f32[5,5,2,6,128]{4,3,2,1,0:T(8,128)S(1)}, bf16[32,512]{1,0:T(8,128)(2,1)S(1)}, bf16[6,2,96,128]{3,2,1,0:T(8,...) custom-call(bf16[6,4,256,128]{3,2,1,0:T(8,128)(2,1)} %f_ref.5, ...), custom_call_target="tpu_custom_call" | custom-call | flops 23592960 | bytes 7864320 | tf_op jit(solution)/shard_map/begin/pallas_call | solution.py:144
  14.4 4.3 %collective-permute-start.3 = (bf16[6,2,96,128]{3,2,1,0:T(8,128)(2,1)S(1)}, bf16[6,2,96,128]{3,2,1,0:T(8,128)(2,1)S(1)}, u32[]{:S(2)}, u32[]{:S(2)}) collective-permute-start(bf16[6,2,96,128]{3,2,1,0:T(8,128)(2,1)S(1)} %get-tuple-element.20), channel_id=1, source_target_pairs={{0,2},{2,0},{4,6},{6,4},{8,10},{10,8},{12,14},{14,12},{16,18},{18,... | collective-permute-start | bytes 884744 | tf_op jit(solution)/shard_map/ppermute | solution.py:343
  18.6 0.7 %collective-permute-start.4 = (bf16[6,2,96,128]{3,2,1,0:T(8,128)(2,1)S(1)}, bf16[6,2,96,128]{3,2,1,0:T(8,128)(2,1)S(1)}, u32[]{:S(2)}, u32[]{:S(2)}) collective-permute-start(bf16[6,2,96,128]{3,2,1,0:T(8,128)(2,1)S(1)} %get-tuple-element.21), channel_id=1, source_target_pairs={{2,4},{4,2},{6,8},{8,6},{10,12},{12,10},{14,16},{16,14},{18,20},{2... | collective-permute-start | bytes 884744 | tf_op jit(solution)/shard_map/ppermute | solution.py:343
  19.3 4.3 %collective-permute-start.1 = (bf16[6,2,32,128]{3,2,1,0:T(8,128)(2,1)S(1)}, bf16[6,2,32,128]{3,2,1,0:T(8,128)(2,1)S(1)}, u32[]{:S(2)}, u32[]{:S(2)}) collective-permute-start(bf16[6,2,32,128]{3,2,1,0:T(8,128)(2,1)S(1)} %get-tuple-element.16), channel_id=1, source_target_pairs={{0,2},{2,0},{4,6},{6,4},{8,10},{10,8},{12,14},{14,12},{16,18},{18,... | collective-permute-start | bytes 294920 | tf_op jit(solution)/shard_map/ppermute | solution.py:343
  23.6 0.0 collective-permute-done.5.first_ref
  23.6 0.7 %collective-permute-start.2 = (bf16[6,2,32,128]{3,2,1,0:T(8,128)(2,1)S(1)}, bf16[6,2,32,128]{3,2,1,0:T(8,128)(2,1)S(1)}, u32[]{:S(2)}, u32[]{:S(2)}) collective-permute-start(bf16[6,2,32,128]{3,2,1,0:T(8,128)(2,1)S(1)} %get-tuple-element.17), channel_id=1, source_target_pairs={{2,4},{4,2},{6,8},{8,6},{10,12},{12,10},{14,16},{16,14},{18,20},{2... | collective-permute-start | bytes 294920 | tf_op jit(solution)/shard_map/ppermute | solution.py:343
  24.3 0.0 collective-permute-done.6.second_ref
  24.3 1.3 %finish.3.refs_0_ = f32[224,128]{1,0:T(8,128)S(1)} custom-call(f32[6,4,256,128]{3,2,1,0:T(8,128)S(1)} %get-tuple-element.15.u_ref, bf16[6,2,128,128]{3,2,1,0:T(8,128)(2,1)S(1)} %collective-permute-done.5.first_ref, bf16[6,2,128,128]{3,2,1,0:T(8,128)(2,1)S(1)} %collective-permute-done.6.second_ref, f32[5,5,2,6,128]{4,3,2,1,0:T(8,128)S(1)} %get-tuple-element.18.w_ref, ...), custom_call_target="tpu_custom_call" | custom-call | flops 7864320 | bytes 3145728 | tf_op jit(solution)/shard_map/finish/pallas_call | solution.py:292
  25.6 11.0 %collective-permute-done.3.first_ref = bf16[6,2,96,128]{3,2,1,0:T(8,128)(2,1)S(1)} collective-permute-done((bf16[6,2,96,128]{3,2,1,0:T(8,128)(2,1)S(1)}, bf16[6,2,96,128]{3,2,1,0:T(8,128)(2,1)S(1)}, u32[]{:S(2)}, u32[]{:S(2)}) %collective-permute-start.3) | collective-permute-done | bytes 294944 | tf_op jit(solution)/shard_map/ppermute | solution.py:343
  36.7 0.0 collective-permute-done.4.second_ref
  36.7 1.1 %finish.4.refs_0_ = f32[224,128]{1,0:T(8,128)S(1)} custom-call(f32[6,4,256,128]{3,2,1,0:T(8,128)S(1)} %get-tuple-element.15.u_ref, bf16[6,2,96,128]{3,2,1,0:T(8,128)(2,1)S(1)} %collective-permute-done.3.first_ref, bf16[6,2,96,128]{3,2,1,0:T(8,128)(2,1)S(1)} %collective-permute-done.4.second_ref, f32[5,5,2,6,128]{4,3,2,1,0:T(8,128)S(1)} %get-tuple-element.18.w_ref, ...), custom_call_target="tpu_custom_call" | custom-call | flops 5898240 | bytes 2359296 | tf_op jit(solution)/shard_map/finish/pallas_call | solution.py:292
  37.7 0.0 collective-permute-done.1.first_ref
  37.8 0.0 collective-permute-done.2.second_ref
  37.8 0.6 %finish.5 = f32[224,128]{1,0:T(8,128)S(1)} custom-call(f32[6,4,256,128]{3,2,1,0:T(8,128)S(1)} %get-tuple-element.15.u_ref, bf16[6,2,32,128]{3,2,1,0:T(8,128)(2,1)S(1)} %collective-permute-done.1.first_ref, bf16[6,2,32,128]{3,2,1,0:T(8,128)(2,1)S(1)} %collective-permute-done.2.second_ref, f32[5,5,2,6,128]{4,3,2,1,0:T(8,128)S(1)} %get-tuple-element.18.w_ref, ...), custom_call_target="tpu_custom_call" | custom-call | flops 1966080 | bytes 786432 | tf_op jit(solution)/shard_map/finish/pallas_call | solution.py:292
  38.3 14.6 %all_to_all.5 = f32[32,1,896]{2,1,0:T(1,128)S(1)} all-to-all(f32[32,1,896]{2,1,0:T(1,128)S(1)} %bitcast.4), channel_id=1, replica_groups=mesh['grp'=1,'gx'=16,'gy'=2] {'gx','gy'}, dimensions={0} | all-to-all | bytes 229376 | tf_op jit(solution)/shard_map/all_to_all | solution.py:348
  52.9 0.7 %gather.1 = f32[6,1,16,128]{3,2,1,0:T(8,128)} custom-call(f32[224,128]{1,0:T(8,128)S(1)} %bitcast.3), custom_call_target="tpu_custom_call" | custom-call | tf_op jit(solution)/shard_map/gather/pallas_call | solution.py:349
Async XLA Ops:
  0.0 7.1 %copy-start = (f32[6,5,5,5]{3,0,2,1:T(8,128)S(1)}, f32[6,5,5,5]{3,0,2,1:T(8,128)}, u32[]{:S(2)}) copy-start(f32[6,5,5,5]{3,0,2,1:T(8,128)} %param.7) | copy-start | bytes 9004
  1.0 22.5 %collective-permute-start.5 = (bf16[6,2,128,128]{3,2,1,0:T(8,128)(2,1)S(1)}, bf16[6,2,128,128]{3,2,1,0:T(8,128)(2,1)S(1)}, u32[]{:S(2)}, u32[]{:S(2)}) collective-permute-start(bf16[6,2,128,128]{3,2,1,0:T(8,128)(2,1)S(1)} %pack.3), channel_id=1, source_target_pairs={{0,2},{2,0},{4,6},{6,4},{8,10},{10,8},{12,14},{14,12},{16,18},{18,... | collective-permute-start | bytes 1179656 | tf_op jit(solution)/shard_map/ppermute | solution.py:339
  5.1 19.2 %collective-permute-start.6 = (bf16[6,2,128,128]{3,2,1,0:T(8,128)(2,1)S(1)}, bf16[6,2,128,128]{3,2,1,0:T(8,128)(2,1)S(1)}, u32[]{:S(2)}, u32[]{:S(2)}) collective-permute-start(bf16[6,2,128,128]{3,2,1,0:T(8,128)(2,1)S(1)} %get-tuple-element.22), channel_id=1, source_target_pairs={{2,4},{4,2},{6,8},{8,6},{10,12},{12,10},{14,16},{16,14},{18,20},{2... | collective-permute-start | bytes 1179656 | tf_op jit(solution)/shard_map/ppermute | solution.py:339
  5.8 1.3 %collective-permute-start = (f32[6,4,2,128]{3,2,1,0:T(2,128)S(1)}, f32[6,4,2,128]{3,2,1,0:T(2,128)S(1)}, u32[]{:S(2)}, u32[]{:S(2)}) collective-permute-start(f32[6,4,2,128]{3,2,1,0:T(2,128)S(1)} %get-tuple-element.14), channel_id=1, source_target_pairs={{0,1},{1,0},{2,3},{3,2},{4,5},{5,4},{6,7},{7,6},{8,9},{9,8},{10,11... | collective-permute-start | bytes 73736 | tf_op jit(solution)/shard_map/ppermute | solution.py:340
  14.4 22.3 %collective-permute-start.3 = (bf16[6,2,96,128]{3,2,1,0:T(8,128)(2,1)S(1)}, bf16[6,2,96,128]{3,2,1,0:T(8,128)(2,1)S(1)}, u32[]{:S(2)}, u32[]{:S(2)}) collective-permute-start(bf16[6,2,96,128]{3,2,1,0:T(8,128)(2,1)S(1)} %get-tuple-element.20), channel_id=1, source_target_pairs={{0,2},{2,0},{4,6},{6,4},{8,10},{10,8},{12,14},{14,12},{16,18},{18,... | collective-permute-start | bytes 884744 | tf_op jit(solution)/shard_map/ppermute | solution.py:343
  18.6 18.0 %collective-permute-start.4 = (bf16[6,2,96,128]{3,2,1,0:T(8,128)(2,1)S(1)}, bf16[6,2,96,128]{3,2,1,0:T(8,128)(2,1)S(1)}, u32[]{:S(2)}, u32[]{:S(2)}) collective-permute-start(bf16[6,2,96,128]{3,2,1,0:T(8,128)(2,1)S(1)} %get-tuple-element.21), channel_id=1, source_target_pairs={{2,4},{4,2},{6,8},{8,6},{10,12},{12,10},{14,16},{16,14},{18,20},{2... | collective-permute-start | bytes 884744 | tf_op jit(solution)/shard_map/ppermute | solution.py:343
  19.3 18.4 %collective-permute-start.1 = (bf16[6,2,32,128]{3,2,1,0:T(8,128)(2,1)S(1)}, bf16[6,2,32,128]{3,2,1,0:T(8,128)(2,1)S(1)}, u32[]{:S(2)}, u32[]{:S(2)}) collective-permute-start(bf16[6,2,32,128]{3,2,1,0:T(8,128)(2,1)S(1)} %get-tuple-element.16), channel_id=1, source_target_pairs={{0,2},{2,0},{4,6},{6,4},{8,10},{10,8},{12,14},{14,12},{16,18},{18,... | collective-permute-start | bytes 294920 | tf_op jit(solution)/shard_map/ppermute | solution.py:343
  23.6 14.2 %collective-permute-start.2 = (bf16[6,2,32,128]{3,2,1,0:T(8,128)(2,1)S(1)}, bf16[6,2,32,128]{3,2,1,0:T(8,128)(2,1)S(1)}, u32[]{:S(2)}, u32[]{:S(2)}) collective-permute-start(bf16[6,2,32,128]{3,2,1,0:T(8,128)(2,1)S(1)} %get-tuple-element.17), channel_id=1, source_target_pairs={{2,4},{4,2},{6,8},{8,6},{10,12},{12,10},{14,16},{16,14},{18,20},{2... | collective-permute-start | bytes 294920 | tf_op jit(solution)/shard_map/ppermute | solution.py:343

commit v6 on v5

--- a/solution.py
+++ b/solution.py
@@ -168,7 +168,7 @@
     )(*(pltpu.with_memory_space_constraint(x, pltpu.HBM) for x in (log_conf, brownian, relax_rate)), cols, jnp.transpose(kernel, (1, 2, 0, 3)))
 
 
-def finish_kernel(start, stop, has_base, u_ref, first_ref, second_ref, w_ref, pick_ref, *refs):
+def finish_kernel(start, stop, has_base, u_ref, a_ref, b_ref, w_ref, pick_ref, *refs):
     if has_base:
         base_ref, out_ref, stress, sums = refs
     else:
@@ -176,6 +176,7 @@
     rows, ny, nz = u_ref.shape[1:]
     width, nj = stop - start, ny // 4
     own_j, planes, pieces = width // 4, out_ref.shape[0] // ROWS, nz // LANES
+    first_ref, second_ref = (b_ref, a_ref) if start > 3 * u_ref.shape[2] // 4 else (a_ref, b_ref)
     odd, _ = position()
     compact = len(sums.shape) == 2
     if compact:
@@ -185,7 +186,8 @@
         for r in range(rows):
             for piece in range(pieces):
                 stress[c, r, piece, 0:LEAD] = jnp.zeros((LEAD, LANES), jnp.float32)
-                stress[c, r, piece, LEAD + width :] = jnp.zeros((TAIL, LANES), jnp.float32)
+                if not compact:
+                    stress[c, r, piece, LEAD + width :] = jnp.zeros((TAIL, LANES), jnp.float32)
 
     for side, halo_ref in enumerate((first_ref, second_ref)):
         upper = (odd == side).astype(jnp.int32)
@@ -287,7 +289,7 @@
     comps, rows, ny, nz = begun.shape
     planes, nj = nz // 4, ny // 4
     places = (2 * nj, 2 * nz) if stop == ny else (comps, 2, (stop - start) // 4 + 8, 2 * nz)
-    operands = [begun, *halos, weights, pick] + ([] if base is None else [base])
+    operands = [begun, *(halos[::-1] if start > 3 * begun.shape[2] // 4 else halos), weights, pick] + ([] if base is None else [base])
     operands = [pltpu.with_memory_space_constraint(x, pltpu.VMEM) for x in operands]
     return pl.pallas_call(
         functools.partial(finish_kernel, start, stop, base is not None),
@@ -332,7 +334,7 @@
 
     swap_first = [(i, i ^ 1) for i in range(width_gx)]
     swap_second = [(i, ((i + 1) ^ 1) - 1) for i in range(1, width_gx - 1)]
-    cuts = [(0, ny // 2), (ny // 2, 7 * ny // 8), (7 * ny // 8, ny)]
+    cuts = [(0, 5 * ny // 8), (5 * ny // 8, 7 * ny // 8), (7 * ny // 8, ny)]
     early = cuts[0][1]
     (first,) = pack(log_conf, early, False)
     second, cols = pack(log_conf, early, True)

time: 54 us -> 54 us (level)
  waiting for transfers between devices: 12.3 us -> 14.8 us
  starting transfers between devices: 13.6 us -> 11.8 us
  blocking collectives: 14.6 us -> 13.9 us
    ppermute x3, waiting for transfers between devices: 11.1 us -> 13.5 us  [local(): lax.ppermute(first, 'gx', swap_first)]
    ppermute x3, starting transfers between devices: 11.6 us -> 9.75 us  [local(): lax.ppermute(first, 'gx', swap_first)]
    all_to_all x1, blocking collectives: 14.6 us -> 13.9 us  [local(): lax.all_to_all(part.reshape(planes, 1, ROWS * ny // 2), ('gx', 'gy'), 0,...]
  transfers between devices with their start and end apart: 7 -> 7, of which waited for: 2 -> 4; matrix products, arithmetic and copies ran while one was open for 0% -> 0% of each run, Pallas kernels for 20% -> 20%
where the time goes in v6:
time: 54 us; the launch traced here: 53.7 us
  waiting for transfers between devices  14.8 us (27%)
  blocking collectives  13.9 us (26%)
  Pallas kernels  13.1 us (24%)
  starting transfers between devices  11.8 us (22%)
    all_to_all x1, blocking collectives, local(): lax.all_to_all(part.reshape(planes, 1, ROWS * ny // 2), ('gx', 'gy'), 0,...  13.9 us
    ppermute x3, waiting for transfers between devices, local(): lax.ppermute(first, 'gx', swap_first)  13.5 us
    ppermute x3, starting transfers between devices, local(): lax.ppermute(first, 'gx', swap_first)  9.75 us
    pallas_call x1, Pallas kernels, begin(): pl.pallas_call(functools.partial(begin_kernel, cuts), grid=(comps,), in_s...  7.29 us
    pallas_call x3, Pallas kernels, finish(): pl.pallas_call(functools.partial(finish_kernel, start, stop, base is not...  2.93 us
    pallas_call x2, Pallas kernels, pack(): pl.pallas_call(functools.partial(pack_kernel, second), in_specs=[pl.Block...  2.15 us
    ppermute x3, starting transfers between devices, local(): lax.ppermute(second, 'gx', swap_second)  2.02 us
    ppermute x1, waiting for transfers between devices, local(): cols = lax.ppermute(cols, 'gy', [(0, 1), (1, 0)])  1.18 us
  transfers between devices with their start and end apart: 7, of which 4 were waited for; matrix products, arithmetic and copies ran while one was open for 0% of the time, Pallas kernels for 20%

profile of v6, /device:TPU:0, one launch (start us, length us, event | category | flops | bytes accessed | tf_op | source)
XLA Modules:
  0.0 53.7 jit_solution(15575641766525127858)
XLA Ops:
  0.0 0.0 copy-start
  0.0 1.1 %pack.3 = bf16[6,2,160,128]{3,2,1,0:T(8,128)(2,1)S(1)} custom-call(bf16[6,4,256,128]{3,2,1,0:T(8,128)(2,1)} %f_ref.5), custom_call_target="tpu_custom_call" | custom-call | tf_op jit(solution)/shard_map/pack/pallas_call | solution.py:63
  1.1 3.0 %collective-permute-start.5 = (bf16[6,2,160,128]{3,2,1,0:T(8,128)(2,1)S(1)}, bf16[6,2,160,128]{3,2,1,0:T(8,128)(2,1)S(1)}, u32[]{:S(2)}, u32[]{:S(2)}) collective-permute-start(bf16[6,2,160,128]{3,2,1,0:T(8,128)(2,1)S(1)} %pack.3), channel_id=1, source_target_pairs={{0,2},{2,0},{4,6},{6,4},{8,10},{10,8},{12,14},{14,12},{16,18},{18,... | collective-permute-start | bytes 1474568 | tf_op jit(solution)/shard_map/ppermute | solution.py:341
  4.1 1.1 %pack.2 = (bf16[6,2,160,128]{3,2,1,0:T(8,128)(2,1)S(1)}, f32[6,4,2,128]{3,2,1,0:T(2,128)S(1)}) custom-call(bf16[6,4,256,128]{3,2,1,0:T(8,128)(2,1)} %f_ref.5), custom_call_target="tpu_custom_call" | custom-call | tf_op jit(solution)/shard_map/pack/pallas_call | solution.py:63
  5.2 0.7 %collective-permute-start.6 = (bf16[6,2,160,128]{3,2,1,0:T(8,128)(2,1)S(1)}, bf16[6,2,160,128]{3,2,1,0:T(8,128)(2,1)S(1)}, u32[]{:S(2)}, u32[]{:S(2)}) collective-permute-start(bf16[6,2,160,128]{3,2,1,0:T(8,128)(2,1)S(1)} %get-tuple-element.22), channel_id=1, source_target_pairs={{2,4},{4,2},{6,8},{8,6},{10,12},{12,10},{14,16},{16,14},{18,20},{2... | collective-permute-start | bytes 1474568 | tf_op jit(solution)/shard_map/ppermute | solution.py:341
  5.9 0.1 collective-permute-start
  5.9 1.2 %collective-permute-done.cols_ref = f32[6,4,2,128]{3,2,1,0:T(2,128)S(1)} collective-permute-done((f32[6,4,2,128]{3,2,1,0:T(2,128)S(1)}, f32[6,4,2,128]{3,2,1,0:T(2,128)S(1)}, u32[]{:S(2)}, u32[]{:S(2)}) %collective-permute-start) | collective-permute-done | bytes 24608 | tf_op jit(solution)/shard_map/ppermute | solution.py:342
  7.1 0.0 copy-done
  7.1 7.3 %begin.1 = (f32[6,4,256,128]{3,2,1,0:T(8,128)S(1)}, f32[5,5,2,6,128]{4,3,2,1,0:T(8,128)S(1)}, bf16[32,512]{1,0:T(8,128)(2,1)S(1)}, bf16[6,2,64,128]{3,2,1,0:T(8,...) custom-call(bf16[6,4,256,128]{3,2,1,0:T(8,128)(2,1)} %f_ref.5, ...), custom_call_target="tpu_custom_call" | custom-call | flops 23592960 | bytes 7864320 | tf_op jit(solution)/shard_map/begin/pallas_call | solution.py:144
  14.4 4.3 %collective-permute-start.3 = (bf16[6,2,64,128]{3,2,1,0:T(8,128)(2,1)S(1)}, bf16[6,2,64,128]{3,2,1,0:T(8,128)(2,1)S(1)}, u32[]{:S(2)}, u32[]{:S(2)}) collective-permute-start(bf16[6,2,64,128]{3,2,1,0:T(8,128)(2,1)S(1)} %get-tuple-element.20), channel_id=1, source_target_pairs={{0,2},{2,0},{4,6},{6,4},{8,10},{10,8},{12,14},{14,12},{16,18},{18,... | collective-permute-start | bytes 589832 | tf_op jit(solution)/shard_map/ppermute | solution.py:345
  18.7 0.7 %collective-permute-start.4 = (bf16[6,2,64,128]{3,2,1,0:T(8,128)(2,1)S(1)}, bf16[6,2,64,128]{3,2,1,0:T(8,128)(2,1)S(1)}, u32[]{:S(2)}, u32[]{:S(2)}) collective-permute-start(bf16[6,2,64,128]{3,2,1,0:T(8,128)(2,1)S(1)} %get-tuple-element.21), channel_id=1, source_target_pairs={{2,4},{4,2},{6,8},{8,6},{10,12},{12,10},{14,16},{16,14},{18,20},{2... | collective-permute-start | bytes 589832 | tf_op jit(solution)/shard_map/ppermute | solution.py:345
  19.4 0.7 %collective-permute-start.1 = (bf16[6,2,32,128]{3,2,1,0:T(8,128)(2,1)S(1)}, bf16[6,2,32,128]{3,2,1,0:T(8,128)(2,1)S(1)}, u32[]{:S(2)}, u32[]{:S(2)}) collective-permute-start(bf16[6,2,32,128]{3,2,1,0:T(8,128)(2,1)S(1)} %get-tuple-element.16), channel_id=1, source_target_pairs={{2,4},{4,2},{6,8},{8,6},{10,12},{12,10},{14,16},{16,14},{18,20},{2... | collective-permute-start | bytes 294920 | tf_op jit(solution)/shard_map/ppermute | solution.py:345
  20.0 12.5 %collective-permute-done.5.a_ref = bf16[6,2,160,128]{3,2,1,0:T(8,128)(2,1)S(1)} collective-permute-done((bf16[6,2,160,128]{3,2,1,0:T(8,128)(2,1)S(1)}, bf16[6,2,160,128]{3,2,1,0:T(8,128)(2,1)S(1)}, u32[]{:S(2)}, u32[]{:S(2)}) %collective-permute-start.5) | collective-permute-done | bytes 491552 | tf_op jit(solution)/shard_map/ppermute | solution.py:341
  32.6 2.5 %collective-permute-start.2 = (bf16[6,2,32,128]{3,2,1,0:T(8,128)(2,1)S(1)}, bf16[6,2,32,128]{3,2,1,0:T(8,128)(2,1)S(1)}, u32[]{:S(2)}, u32[]{:S(2)}) collective-permute-start(bf16[6,2,32,128]{3,2,1,0:T(8,128)(2,1)S(1)} %get-tuple-element.17), channel_id=1, source_target_pairs={{0,2},{2,0},{4,6},{6,4},{8,10},{10,8},{12,14},{14,12},{16,18},{18,... | collective-permute-start | bytes 294920 | tf_op jit(solution)/shard_map/ppermute | solution.py:345
  35.0 0.0 collective-permute-done.6.b_ref
  35.1 1.6 %finish.3.refs_0_ = f32[224,128]{1,0:T(8,128)S(1)} custom-call(f32[6,4,256,128]{3,2,1,0:T(8,128)S(1)} %get-tuple-element.15.u_ref, bf16[6,2,160,128]{3,2,1,0:T(8,128)(2,1)S(1)} %collective-permute-done.5.a_ref, bf16[6,2,160,128]{3,2,1,0:T(8,128)(2,1)S(1)} %collective-permute-done.6.b_ref, f32[5,5,2,6,128]{4,3,2,1,0:T(8,128)S(1)} %get-tuple-element.18.w_ref, ...), custom_call_target="tpu_custom_call" | custom-call | flops 9830400 | bytes 3932160 | tf_op jit(solution)/shard_map/finish/pallas_call | solution.py:294
  36.6 0.1 collective-permute-done.3.a_ref
  36.7 0.0 collective-permute-done.4.b_ref
  36.7 0.8 %finish.4.refs_0_ = f32[224,128]{1,0:T(8,128)S(1)} custom-call(f32[6,4,256,128]{3,2,1,0:T(8,128)S(1)} %get-tuple-element.15.u_ref, bf16[6,2,64,128]{3,2,1,0:T(8,128)(2,1)S(1)} %collective-permute-done.3.a_ref, bf16[6,2,64,128]{3,2,1,0:T(8,128)(2,1)S(1)} %collective-permute-done.4.b_ref, f32[5,5,2,6,128]{4,3,2,1,0:T(8,128)S(1)} %get-tuple-element.18.w_ref, ...), custom_call_target="tpu_custom_call" | custom-call | flops 3932160 | bytes 1572864 | tf_op jit(solution)/shard_map/finish/pallas_call | solution.py:294
  37.5 0.0 collective-permute-done.1.a_ref
  37.5 1.0 %collective-permute-done.2.b_ref = bf16[6,2,32,128]{3,2,1,0:T(8,128)(2,1)S(1)} collective-permute-done((bf16[6,2,32,128]{3,2,1,0:T(8,128)(2,1)S(1)}, bf16[6,2,32,128]{3,2,1,0:T(8,128)(2,1)S(1)}, u32[]{:S(2)}, u32[]{:S(2)}) %collective-permute-start.2) | collective-permute-done | bytes 98336 | tf_op jit(solution)/shard_map/ppermute | solution.py:345
  38.5 0.5 %finish.5 = f32[224,128]{1,0:T(8,128)S(1)} custom-call(f32[6,4,256,128]{3,2,1,0:T(8,128)S(1)} %get-tuple-element.15.u_ref, bf16[6,2,32,128]{3,2,1,0:T(8,128)(2,1)S(1)} %collective-permute-done.1.a_ref, bf16[6,2,32,128]{3,2,1,0:T(8,128)(2,1)S(1)} %collective-permute-done.2.b_ref, f32[5,5,2,6,128]{4,3,2,1,0:T(8,128)S(1)} %get-tuple-element.18.w_ref, ...), custom_call_target="tpu_custom_call" | custom-call | flops 1966080 | bytes 786432 | tf_op jit(solution)/shard_map/finish/pallas_call | solution.py:294
  39.0 13.9 %all_to_all.5 = f32[32,1,896]{2,1,0:T(1,128)S(1)} all-to-all(f32[32,1,896]{2,1,0:T(1,128)S(1)} %bitcast.4), channel_id=1, replica_groups=mesh['grp'=1,'gx'=16,'gy'=2] {'gx','gy'}, dimensions={0} | all-to-all | bytes 229376 | tf_op jit(solution)/shard_map/all_to_all | solution.py:350
  53.0 0.7 %gather.1 = f32[6,1,16,128]{3,2,1,0:T(8,128)} custom-call(f32[224,128]{1,0:T(8,128)S(1)} %bitcast.3), custom_call_target="tpu_custom_call" | custom-call | tf_op jit(solution)/shard_map/gather/pallas_call | solution.py:351
Async XLA Ops:
  0.0 7.1 %copy-start = (f32[6,5,5,5]{3,0,2,1:T(8,128)S(1)}, f32[6,5,5,5]{3,0,2,1:T(8,128)}, u32[]{:S(2)}) copy-start(f32[6,5,5,5]{3,0,2,1:T(8,128)} %param.7) | copy-start | bytes 9004
  1.1 31.5 %collective-permute-start.5 = (bf16[6,2,160,128]{3,2,1,0:T(8,128)(2,1)S(1)}, bf16[6,2,160,128]{3,2,1,0:T(8,128)(2,1)S(1)}, u32[]{:S(2)}, u32[]{:S(2)}) collective-permute-start(bf16[6,2,160,128]{3,2,1,0:T(8,128)(2,1)S(1)} %pack.3), channel_id=1, source_target_pairs={{0,2},{2,0},{4,6},{6,4},{8,10},{10,8},{12,14},{14,12},{16,18},{18,... | collective-permute-start | bytes 1474568 | tf_op jit(solution)/shard_map/ppermute | solution.py:341
  5.2 29.9 %collective-permute-start.6 = (bf16[6,2,160,128]{3,2,1,0:T(8,128)(2,1)S(1)}, bf16[6,2,160,128]{3,2,1,0:T(8,128)(2,1)S(1)}, u32[]{:S(2)}, u32[]{:S(2)}) collective-permute-start(bf16[6,2,160,128]{3,2,1,0:T(8,128)(2,1)S(1)} %get-tuple-element.22), channel_id=1, source_target_pairs={{2,4},{4,2},{6,8},{8,6},{10,12},{12,10},{14,16},{16,14},{18,20},{2... | collective-permute-start | bytes 1474568 | tf_op jit(solution)/shard_map/ppermute | solution.py:341
  5.9 1.3 %collective-permute-start = (f32[6,4,2,128]{3,2,1,0:T(2,128)S(1)}, f32[6,4,2,128]{3,2,1,0:T(2,128)S(1)}, u32[]{:S(2)}, u32[]{:S(2)}) collective-permute-start(f32[6,4,2,128]{3,2,1,0:T(2,128)S(1)} %get-tuple-element.14), channel_id=1, source_target_pairs={{0,1},{1,0},{2,3},{3,2},{4,5},{5,4},{6,7},{7,6},{8,9},{9,8},{10,11... | collective-permute-start | bytes 73736 | tf_op jit(solution)/shard_map/ppermute | solution.py:342
  14.4 22.3 %collective-permute-start.3 = (bf16[6,2,64,128]{3,2,1,0:T(8,128)(2,1)S(1)}, bf16[6,2,64,128]{3,2,1,0:T(8,128)(2,1)S(1)}, u32[]{:S(2)}, u32[]{:S(2)}) collective-permute-start(bf16[6,2,64,128]{3,2,1,0:T(8,128)(2,1)S(1)} %get-tuple-element.20), channel_id=1, source_target_pairs={{0,2},{2,0},{4,6},{6,4},{8,10},{10,8},{12,14},{14,12},{16,18},{18,... | collective-permute-start | bytes 589832 | tf_op jit(solution)/shard_map/ppermute | solution.py:345
  18.7 18.0 %collective-permute-start.4 = (bf16[6,2,64,128]{3,2,1,0:T(8,128)(2,1)S(1)}, bf16[6,2,64,128]{3,2,1,0:T(8,128)(2,1)S(1)}, u32[]{:S(2)}, u32[]{:S(2)}) collective-permute-start(bf16[6,2,64,128]{3,2,1,0:T(8,128)(2,1)S(1)} %get-tuple-element.21), channel_id=1, source_target_pairs={{2,4},{4,2},{6,8},{8,6},{10,12},{12,10},{14,16},{16,14},{18,20},{2... | collective-permute-start | bytes 589832 | tf_op jit(solution)/shard_map/ppermute | solution.py:345
  19.4 18.2 %collective-permute-start.1 = (bf16[6,2,32,128]{3,2,1,0:T(8,128)(2,1)S(1)}, bf16[6,2,32,128]{3,2,1,0:T(8,128)(2,1)S(1)}, u32[]{:S(2)}, u32[]{:S(2)}) collective-permute-start(bf16[6,2,32,128]{3,2,1,0:T(8,128)(2,1)S(1)} %get-tuple-element.16), channel_id=1, source_target_pairs={{2,4},{4,2},{6,8},{8,6},{10,12},{12,10},{14,16},{16,14},{18,20},{2... | collective-permute-start | bytes 294920 | tf_op jit(solution)/shard_map/ppermute | solution.py:345
  32.6 5.9 %collective-permute-start.2 = (bf16[6,2,32,128]{3,2,1,0:T(8,128)(2,1)S(1)}, bf16[6,2,32,128]{3,2,1,0:T(8,128)(2,1)S(1)}, u32[]{:S(2)}, u32[]{:S(2)}) collective-permute-start(bf16[6,2,32,128]{3,2,1,0:T(8,128)(2,1)S(1)} %get-tuple-element.17), channel_id=1, source_target_pairs={{0,2},{2,0},{4,6},{6,4},{8,10},{10,8},{12,14},{14,12},{16,18},{18,... | collective-permute-start | bytes 294920 | tf_op jit(solution)/shard_map/ppermute | solution.py:345

commit v7 on v6

--- a/solution.py
+++ b/solution.py
@@ -223,30 +223,33 @@
 
     taps = {0: ((0, 2), (1, 3), (2, 4)), 1: ((2, 0), (3, 1))}
     for c in range(NC):
+        weight = {}
         for t in range(2):
-            weight = {}
             for row, a in taps[t]:
                 for b in range(5):
                     for k in range(2):
-                        weight[row, b, k] = w_ref[a, b, k, c : c + 1]
-            for jb in range(own_j // 8 + 1):
-                total = [None, None]
-                for b in range(5 if jb < own_j // 8 else 2):
-                    at = pl.ds(LEAD + 32 * jb + b - 2, 8, stride=4)
-                    for row, _ in taps[t]:
-                        value = jnp.concatenate([stress[c, row, piece, at] for piece in range(pieces)], axis=1)
+                        weight[t, row, b, k] = w_ref[a, b, k, c : c + 1]
+        for jb in range(own_j // 8 + 1):
+            total = {}
+            for b in range(5 if jb < own_j // 8 else 2):
+                at = pl.ds(LEAD + 32 * jb + b - 2, 8, stride=4)
+                for row in range(rows):
+                    value = jnp.concatenate([stress[c, row, piece, at] for piece in range(pieces)], axis=1)
+                    for t in range(2):
                         for k in range(2):
-                            term = value * weight[row, b, k]
-                            total[k] = term if total[k] is None else total[k] + term
+                            if (t, row, b, k) in weight:
+                                term = value * weight[t, row, b, k]
+                                total[t, k] = total[t, k] + term if (t, k) in total else term
+            for t in range(2):
                 for k in range(2):
                     lanes = slice(k * nz, (k + 1) * nz)
                     if not compact:
-                        sums[c, t, 8 * jb : 8 * jb + 8, lanes] = total[k]
+                        sums[c, t, 8 * jb : 8 * jb + 8, lanes] = total[t, k]
                     elif jb == 0:
-                        sums[t * nj + 8 * c : t * nj + 8 * c + 8, lanes] = total[k]
+                        sums[t * nj + 8 * c : t * nj + 8 * c + 8, lanes] = total[t, k]
                     else:
                         at = t * nj + 8 * NC + c
-                        sums[at : at + 1, lanes] = total[k][0:1]
+                        sums[at : at + 1, lanes] = total[t, k][0:1]
 
     def reduced(values):
         high = values.astype(jnp.bfloat16)

time: 54 us -> 54 us (level)
  no operation moved by 1% of the time
where the time goes in v7:
time: 54 us; the launch traced here: 53.7 us
  waiting for transfers between devices  14.8 us (27%)
  blocking collectives  13.9 us (26%)
  Pallas kernels  13.1 us (24%)
  starting transfers between devices  11.8 us (22%)
    all_to_all x1, blocking collectives, local(): lax.all_to_all(part.reshape(planes, 1, ROWS * ny // 2), ('gx', 'gy'), 0,...  13.9 us
    ppermute x3, waiting for transfers between devices, local(): lax.ppermute(first, 'gx', swap_first)  13.6 us
    ppermute x3, starting transfers between devices, local(): lax.ppermute(first, 'gx', swap_first)  9.75 us
    pallas_call x1, Pallas kernels, begin(): pl.pallas_call(functools.partial(begin_kernel, cuts), grid=(comps,), in_s...  7.29 us
    pallas_call x3, Pallas kernels, finish(): pl.pallas_call(functools.partial(finish_kernel, start, stop, base is not...  2.9 us
    pallas_call x2, Pallas kernels, pack(): pl.pallas_call(functools.partial(pack_kernel, second), in_specs=[pl.Block...  2.15 us
    ppermute x3, starting transfers between devices, local(): lax.ppermute(second, 'gx', swap_second)  2.02 us
    ppermute x1, waiting for transfers between devices, local(): cols = lax.ppermute(cols, 'gy', [(0, 1), (1, 0)])  1.18 us
  transfers between devices with their start and end apart: 7, of which 4 were waited for; matrix products, arithmetic and copies ran while one was open for 0% of the time, Pallas kernels for 20%

profile of v7, /device:TPU:0, one launch (start us, length us, event | category | flops | bytes accessed | tf_op | source)
XLA Modules:
  0.0 53.7 jit_solution(15926086564292871874)
XLA Ops:
  0.0 0.0 copy-start
  0.0 1.1 %pack.3 = bf16[6,2,160,128]{3,2,1,0:T(8,128)(2,1)S(1)} custom-call(bf16[6,4,256,128]{3,2,1,0:T(8,128)(2,1)} %f_ref.5), custom_call_target="tpu_custom_call" | custom-call | tf_op jit(solution)/shard_map/pack/pallas_call | solution.py:63
  1.1 3.0 %collective-permute-start.5 = (bf16[6,2,160,128]{3,2,1,0:T(8,128)(2,1)S(1)}, bf16[6,2,160,128]{3,2,1,0:T(8,128)(2,1)S(1)}, u32[]{:S(2)}, u32[]{:S(2)}) collective-permute-start(bf16[6,2,160,128]{3,2,1,0:T(8,128)(2,1)S(1)} %pack.3), channel_id=1, source_target_pairs={{0,2},{2,0},{4,6},{6,4},{8,10},{10,8},{12,14},{14,12},{16,18},{18,... | collective-permute-start | bytes 1474568 | tf_op jit(solution)/shard_map/ppermute | solution.py:344
  4.1 1.1 %pack.2 = (bf16[6,2,160,128]{3,2,1,0:T(8,128)(2,1)S(1)}, f32[6,4,2,128]{3,2,1,0:T(2,128)S(1)}) custom-call(bf16[6,4,256,128]{3,2,1,0:T(8,128)(2,1)} %f_ref.5), custom_call_target="tpu_custom_call" | custom-call | tf_op jit(solution)/shard_map/pack/pallas_call | solution.py:63
  5.2 0.7 %collective-permute-start.6 = (bf16[6,2,160,128]{3,2,1,0:T(8,128)(2,1)S(1)}, bf16[6,2,160,128]{3,2,1,0:T(8,128)(2,1)S(1)}, u32[]{:S(2)}, u32[]{:S(2)}) collective-permute-start(bf16[6,2,160,128]{3,2,1,0:T(8,128)(2,1)S(1)} %get-tuple-element.22), channel_id=1, source_target_pairs={{2,4},{4,2},{6,8},{8,6},{10,12},{12,10},{14,16},{16,14},{18,20},{2... | collective-permute-start | bytes 1474568 | tf_op jit(solution)/shard_map/ppermute | solution.py:344
  5.9 0.1 collective-permute-start
  5.9 1.2 %collective-permute-done.cols_ref = f32[6,4,2,128]{3,2,1,0:T(2,128)S(1)} collective-permute-done((f32[6,4,2,128]{3,2,1,0:T(2,128)S(1)}, f32[6,4,2,128]{3,2,1,0:T(2,128)S(1)}, u32[]{:S(2)}, u32[]{:S(2)}) %collective-permute-start) | collective-permute-done | bytes 24608 | tf_op jit(solution)/shard_map/ppermute | solution.py:345
  7.1 0.0 copy-done
  7.1 7.3 %begin.1 = (f32[6,4,256,128]{3,2,1,0:T(8,128)S(1)}, f32[5,5,2,6,128]{4,3,2,1,0:T(8,128)S(1)}, bf16[32,512]{1,0:T(8,128)(2,1)S(1)}, bf16[6,2,64,128]{3,2,1,0:T(8,...) custom-call(bf16[6,4,256,128]{3,2,1,0:T(8,128)(2,1)} %f_ref.5, ...), custom_call_target="tpu_custom_call" | custom-call | flops 23592960 | bytes 7864320 | tf_op jit(solution)/shard_map/begin/pallas_call | solution.py:144
  14.4 4.3 %collective-permute-start.3 = (bf16[6,2,64,128]{3,2,1,0:T(8,128)(2,1)S(1)}, bf16[6,2,64,128]{3,2,1,0:T(8,128)(2,1)S(1)}, u32[]{:S(2)}, u32[]{:S(2)}) collective-permute-start(bf16[6,2,64,128]{3,2,1,0:T(8,128)(2,1)S(1)} %get-tuple-element.20), channel_id=1, source_target_pairs={{0,2},{2,0},{4,6},{6,4},{8,10},{10,8},{12,14},{14,12},{16,18},{18,... | collective-permute-start | bytes 589832 | tf_op jit(solution)/shard_map/ppermute | solution.py:348
  18.7 0.7 %collective-permute-start.4 = (bf16[6,2,64,128]{3,2,1,0:T(8,128)(2,1)S(1)}, bf16[6,2,64,128]{3,2,1,0:T(8,128)(2,1)S(1)}, u32[]{:S(2)}, u32[]{:S(2)}) collective-permute-start(bf16[6,2,64,128]{3,2,1,0:T(8,128)(2,1)S(1)} %get-tuple-element.21), channel_id=1, source_target_pairs={{2,4},{4,2},{6,8},{8,6},{10,12},{12,10},{14,16},{16,14},{18,20},{2... | collective-permute-start | bytes 589832 | tf_op jit(solution)/shard_map/ppermute | solution.py:348
  19.4 0.7 %collective-permute-start.1 = (bf16[6,2,32,128]{3,2,1,0:T(8,128)(2,1)S(1)}, bf16[6,2,32,128]{3,2,1,0:T(8,128)(2,1)S(1)}, u32[]{:S(2)}, u32[]{:S(2)}) collective-permute-start(bf16[6,2,32,128]{3,2,1,0:T(8,128)(2,1)S(1)} %get-tuple-element.16), channel_id=1, source_target_pairs={{2,4},{4,2},{6,8},{8,6},{10,12},{12,10},{14,16},{16,14},{18,20},{2... | collective-permute-start | bytes 294920 | tf_op jit(solution)/shard_map/ppermute | solution.py:348
  20.0 12.5 %collective-permute-done.5.a_ref = bf16[6,2,160,128]{3,2,1,0:T(8,128)(2,1)S(1)} collective-permute-done((bf16[6,2,160,128]{3,2,1,0:T(8,128)(2,1)S(1)}, bf16[6,2,160,128]{3,2,1,0:T(8,128)(2,1)S(1)}, u32[]{:S(2)}, u32[]{:S(2)}) %collective-permute-start.5) | collective-permute-done | bytes 491552 | tf_op jit(solution)/shard_map/ppermute | solution.py:344
  32.6 2.5 %collective-permute-start.2 = (bf16[6,2,32,128]{3,2,1,0:T(8,128)(2,1)S(1)}, bf16[6,2,32,128]{3,2,1,0:T(8,128)(2,1)S(1)}, u32[]{:S(2)}, u32[]{:S(2)}) collective-permute-start(bf16[6,2,32,128]{3,2,1,0:T(8,128)(2,1)S(1)} %get-tuple-element.17), channel_id=1, source_target_pairs={{0,2},{2,0},{4,6},{6,4},{8,10},{10,8},{12,14},{14,12},{16,18},{18,... | collective-permute-start | bytes 294920 | tf_op jit(solution)/shard_map/ppermute | solution.py:348
  35.0 0.0 collective-permute-done.6.b_ref
  35.1 1.6 %finish.3.refs_0_ = f32[224,128]{1,0:T(8,128)S(1)} custom-call(f32[6,4,256,128]{3,2,1,0:T(8,128)S(1)} %get-tuple-element.15.u_ref, bf16[6,2,160,128]{3,2,1,0:T(8,128)(2,1)S(1)} %collective-permute-done.5.a_ref, bf16[6,2,160,128]{3,2,1,0:T(8,128)(2,1)S(1)} %collective-permute-done.6.b_ref, f32[5,5,2,6,128]{4,3,2,1,0:T(8,128)S(1)} %get-tuple-element.18.w_ref, ...), custom_call_target="tpu_custom_call" | custom-call | flops 9830400 | bytes 3932160 | tf_op jit(solution)/shard_map/finish/pallas_call | solution.py:297
  36.6 0.1 collective-permute-done.3.a_ref
  36.7 0.0 collective-permute-done.4.b_ref
  36.7 0.8 %finish.4.refs_0_ = f32[224,128]{1,0:T(8,128)S(1)} custom-call(f32[6,4,256,128]{3,2,1,0:T(8,128)S(1)} %get-tuple-element.15.u_ref, bf16[6,2,64,128]{3,2,1,0:T(8,128)(2,1)S(1)} %collective-permute-done.3.a_ref, bf16[6,2,64,128]{3,2,1,0:T(8,128)(2,1)S(1)} %collective-permute-done.4.b_ref, f32[5,5,2,6,128]{4,3,2,1,0:T(8,128)S(1)} %get-tuple-element.18.w_ref, ...), custom_call_target="tpu_custom_call" | custom-call | flops 3932160 | bytes 1572864 | tf_op jit(solution)/shard_map/finish/pallas_call | solution.py:297
  37.5 0.0 collective-permute-done.1.a_ref
  37.5 1.0 %collective-permute-done.2.b_ref = bf16[6,2,32,128]{3,2,1,0:T(8,128)(2,1)S(1)} collective-permute-done((bf16[6,2,32,128]{3,2,1,0:T(8,128)(2,1)S(1)}, bf16[6,2,32,128]{3,2,1,0:T(8,128)(2,1)S(1)}, u32[]{:S(2)}, u32[]{:S(2)}) %collective-permute-start.2) | collective-permute-done | bytes 98336 | tf_op jit(solution)/shard_map/ppermute | solution.py:348
  38.5 0.5 %finish.5 = f32[224,128]{1,0:T(8,128)S(1)} custom-call(f32[6,4,256,128]{3,2,1,0:T(8,128)S(1)} %get-tuple-element.15.u_ref, bf16[6,2,32,128]{3,2,1,0:T(8,128)(2,1)S(1)} %collective-permute-done.1.a_ref, bf16[6,2,32,128]{3,2,1,0:T(8,128)(2,1)S(1)} %collective-permute-done.2.b_ref, f32[5,5,2,6,128]{4,3,2,1,0:T(8,128)S(1)} %get-tuple-element.18.w_ref, ...), custom_call_target="tpu_custom_call" | custom-call | flops 1966080 | bytes 786432 | tf_op jit(solution)/shard_map/finish/pallas_call | solution.py:297
  39.0 13.9 %all_to_all.5 = f32[32,1,896]{2,1,0:T(1,128)S(1)} all-to-all(f32[32,1,896]{2,1,0:T(1,128)S(1)} %bitcast.4), channel_id=1, replica_groups=mesh['grp'=1,'gx'=16,'gy'=2] {'gx','gy'}, dimensions={0} | all-to-all | bytes 229376 | tf_op jit(solution)/shard_map/all_to_all | solution.py:353
  53.0 0.7 %gather.1 = f32[6,1,16,128]{3,2,1,0:T(8,128)} custom-call(f32[224,128]{1,0:T(8,128)S(1)} %bitcast.3), custom_call_target="tpu_custom_call" | custom-call | tf_op jit(solution)/shard_map/gather/pallas_call | solution.py:354
Async XLA Ops:
  0.0 7.1 %copy-start = (f32[6,5,5,5]{3,0,2,1:T(8,128)S(1)}, f32[6,5,5,5]{3,0,2,1:T(8,128)}, u32[]{:S(2)}) copy-start(f32[6,5,5,5]{3,0,2,1:T(8,128)} %param.7) | copy-start | bytes 9004
  1.1 31.5 %collective-permute-start.5 = (bf16[6,2,160,128]{3,2,1,0:T(8,128)(2,1)S(1)}, bf16[6,2,160,128]{3,2,1,0:T(8,128)(2,1)S(1)}, u32[]{:S(2)}, u32[]{:S(2)}) collective-permute-start(bf16[6,2,160,128]{3,2,1,0:T(8,128)(2,1)S(1)} %pack.3), channel_id=1, source_target_pairs={{0,2},{2,0},{4,6},{6,4},{8,10},{10,8},{12,14},{14,12},{16,18},{18,... | collective-permute-start | bytes 1474568 | tf_op jit(solution)/shard_map/ppermute | solution.py:344
  5.2 29.9 %collective-permute-start.6 = (bf16[6,2,160,128]{3,2,1,0:T(8,128)(2,1)S(1)}, bf16[6,2,160,128]{3,2,1,0:T(8,128)(2,1)S(1)}, u32[]{:S(2)}, u32[]{:S(2)}) collective-permute-start(bf16[6,2,160,128]{3,2,1,0:T(8,128)(2,1)S(1)} %get-tuple-element.22), channel_id=1, source_target_pairs={{2,4},{4,2},{6,8},{8,6},{10,12},{12,10},{14,16},{16,14},{18,20},{2... | collective-permute-start | bytes 1474568 | tf_op jit(solution)/shard_map/ppermute | solution.py:344
  5.9 1.3 %collective-permute-start = (f32[6,4,2,128]{3,2,1,0:T(2,128)S(1)}, f32[6,4,2,128]{3,2,1,0:T(2,128)S(1)}, u32[]{:S(2)}, u32[]{:S(2)}) collective-permute-start(f32[6,4,2,128]{3,2,1,0:T(2,128)S(1)} %get-tuple-element.14), channel_id=1, source_target_pairs={{0,1},{1,0},{2,3},{3,2},{4,5},{5,4},{6,7},{7,6},{8,9},{9,8},{10,11... | collective-permute-start | bytes 73736 | tf_op jit(solution)/shard_map/ppermute | solution.py:345
  14.4 22.3 %collective-permute-start.3 = (bf16[6,2,64,128]{3,2,1,0:T(8,128)(2,1)S(1)}, bf16[6,2,64,128]{3,2,1,0:T(8,128)(2,1)S(1)}, u32[]{:S(2)}, u32[]{:S(2)}) collective-permute-start(bf16[6,2,64,128]{3,2,1,0:T(8,128)(2,1)S(1)} %get-tuple-element.20), channel_id=1, source_target_pairs={{0,2},{2,0},{4,6},{6,4},{8,10},{10,8},{12,14},{14,12},{16,18},{18,... | collective-permute-start | bytes 589832 | tf_op jit(solution)/shard_map/ppermute | solution.py:348
  18.7 18.0 %collective-permute-start.4 = (bf16[6,2,64,128]{3,2,1,0:T(8,128)(2,1)S(1)}, bf16[6,2,64,128]{3,2,1,0:T(8,128)(2,1)S(1)}, u32[]{:S(2)}, u32[]{:S(2)}) collective-permute-start(bf16[6,2,64,128]{3,2,1,0:T(8,128)(2,1)S(1)} %get-tuple-element.21), channel_id=1, source_target_pairs={{2,4},{4,2},{6,8},{8,6},{10,12},{12,10},{14,16},{16,14},{18,20},{2... | collective-permute-start | bytes 589832 | tf_op jit(solution)/shard_map/ppermute | solution.py:348
  19.4 18.2 %collective-permute-start.1 = (bf16[6,2,32,128]{3,2,1,0:T(8,128)(2,1)S(1)}, bf16[6,2,32,128]{3,2,1,0:T(8,128)(2,1)S(1)}, u32[]{:S(2)}, u32[]{:S(2)}) collective-permute-start(bf16[6,2,32,128]{3,2,1,0:T(8,128)(2,1)S(1)} %get-tuple-element.16), channel_id=1, source_target_pairs={{2,4},{4,2},{6,8},{8,6},{10,12},{12,10},{14,16},{16,14},{18,20},{2... | collective-permute-start | bytes 294920 | tf_op jit(solution)/shard_map/ppermute | solution.py:348
  32.6 5.9 %collective-permute-start.2 = (bf16[6,2,32,128]{3,2,1,0:T(8,128)(2,1)S(1)}, bf16[6,2,32,128]{3,2,1,0:T(8,128)(2,1)S(1)}, u32[]{:S(2)}, u32[]{:S(2)}) collective-permute-start(bf16[6,2,32,128]{3,2,1,0:T(8,128)(2,1)S(1)} %get-tuple-element.17), channel_id=1, source_target_pairs={{0,2},{2,0},{4,6},{6,4},{8,10},{10,8},{12,14},{14,12},{16,18},{18,... | collective-permute-start | bytes 294920 | tf_op jit(solution)/shard_map/ppermute | solution.py:348

commit v8 on v6

--- a/solution.py
+++ b/solution.py
@@ -176,7 +176,7 @@
     rows, ny, nz = u_ref.shape[1:]
     width, nj = stop - start, ny // 4
     own_j, planes, pieces = width // 4, out_ref.shape[0] // ROWS, nz // LANES
-    first_ref, second_ref = (b_ref, a_ref) if start > 3 * u_ref.shape[2] // 4 else (a_ref, b_ref)
+    first_ref, second_ref = (b_ref, a_ref) if 0 < start < 3 * u_ref.shape[2] // 4 else (a_ref, b_ref)
     odd, _ = position()
     compact = len(sums.shape) == 2
     if compact:
@@ -186,8 +186,7 @@
         for r in range(rows):
             for piece in range(pieces):
                 stress[c, r, piece, 0:LEAD] = jnp.zeros((LEAD, LANES), jnp.float32)
-                if not compact:
-                    stress[c, r, piece, LEAD + width :] = jnp.zeros((TAIL, LANES), jnp.float32)
+                stress[c, r, piece, LEAD + width :] = jnp.zeros((TAIL, LANES), jnp.float32)
 
     for side, halo_ref in enumerate((first_ref, second_ref)):
         upper = (odd == side).astype(jnp.int32)
@@ -289,7 +288,7 @@
     comps, rows, ny, nz = begun.shape
     planes, nj = nz // 4, ny // 4
     places = (2 * nj, 2 * nz) if stop == ny else (comps, 2, (stop - start) // 4 + 8, 2 * nz)
-    operands = [begun, *(halos[::-1] if start > 3 * begun.shape[2] // 4 else halos), weights, pick] + ([] if base is None else [base])
+    operands = [begun, *(halos[::-1] if 0 < start < 3 * begun.shape[2] // 4 else halos), weights, pick] + ([] if base is None else [base])
     operands = [pltpu.with_memory_space_constraint(x, pltpu.VMEM) for x in operands]
     return pl.pallas_call(
         functools.partial(finish_kernel, start, stop, base is not None),

time: 54 us -> 54 us (level)
  starting transfers between devices: 11.8 us -> 10.7 us
  blocking collectives: 13.9 us -> 14.7 us
    ppermute x3, starting transfers between devices: 9.75 us -> 8.6 us  [local(): lax.ppermute(first, 'gx', swap_first)]
    all_to_all x1, blocking collectives: 13.9 us -> 14.7 us  [local(): lax.all_to_all(part.reshape(planes, 1, ROWS * ny // 2), ('gx', 'gy'), 0,...]
where the time goes in v8:
time: 54 us; the launch traced here: 53.7 us
  waiting for transfers between devices  15.2 us (28%)
  blocking collectives  14.7 us (27%)
  Pallas kernels  13.1 us (24%)
  starting transfers between devices  10.7 us (20%)
    all_to_all x1, blocking collectives, local(): lax.all_to_all(part.reshape(planes, 1, ROWS * ny // 2), ('gx', 'gy'), 0,...  14.7 us
    ppermute x3, waiting for transfers between devices, local(): lax.ppermute(first, 'gx', swap_first)  14 us
    ppermute x3, starting transfers between devices, local(): lax.ppermute(first, 'gx', swap_first)  8.6 us
    pallas_call x1, Pallas kernels, begin(): pl.pallas_call(functools.partial(begin_kernel, cuts), grid=(comps,), in_s...  7.29 us
    pallas_call x3, Pallas kernels, finish(): pl.pallas_call(functools.partial(finish_kernel, start, stop, base is not...  2.96 us
    pallas_call x2, Pallas kernels, pack(): pl.pallas_call(functools.partial(pack_kernel, second), in_specs=[pl.Block...  2.15 us
    ppermute x3, starting transfers between devices, local(): lax.ppermute(second, 'gx', swap_second)  2.02 us
    ppermute x1, waiting for transfers between devices, local(): cols = lax.ppermute(cols, 'gy', [(0, 1), (1, 0)])  1.18 us
  transfers between devices with their start and end apart: 7, of which 4 were waited for; matrix products, arithmetic and copies ran while one was open for 0% of the time, Pallas kernels for 20%

profile of v8, /device:TPU:0, one launch (start us, length us, event | category | flops | bytes accessed | tf_op | source)
XLA Modules:
  0.0 53.7 jit_solution(14748623396994566393)
XLA Ops:
  0.0 0.0 copy-start
  0.0 1.1 %pack.3 = bf16[6,2,160,128]{3,2,1,0:T(8,128)(2,1)S(1)} custom-call(bf16[6,4,256,128]{3,2,1,0:T(8,128)(2,1)} %f_ref.5), custom_call_target="tpu_custom_call" | custom-call | tf_op jit(solution)/shard_map/pack/pallas_call | solution.py:63
  1.1 3.0 %collective-permute-start.5 = (bf16[6,2,160,128]{3,2,1,0:T(8,128)(2,1)S(1)}, bf16[6,2,160,128]{3,2,1,0:T(8,128)(2,1)S(1)}, u32[]{:S(2)}, u32[]{:S(2)}) collective-permute-start(bf16[6,2,160,128]{3,2,1,0:T(8,128)(2,1)S(1)} %pack.3), channel_id=1, source_target_pairs={{0,2},{2,0},{4,6},{6,4},{8,10},{10,8},{12,14},{14,12},{16,18},{18,... | collective-permute-start | bytes 1474568 | tf_op jit(solution)/shard_map/ppermute | solution.py:340
  4.1 1.1 %pack.2 = (bf16[6,2,160,128]{3,2,1,0:T(8,128)(2,1)S(1)}, f32[6,4,2,128]{3,2,1,0:T(2,128)S(1)}) custom-call(bf16[6,4,256,128]{3,2,1,0:T(8,128)(2,1)} %f_ref.5), custom_call_target="tpu_custom_call" | custom-call | tf_op jit(solution)/shard_map/pack/pallas_call | solution.py:63
  5.2 0.7 %collective-permute-start.6 = (bf16[6,2,160,128]{3,2,1,0:T(8,128)(2,1)S(1)}, bf16[6,2,160,128]{3,2,1,0:T(8,128)(2,1)S(1)}, u32[]{:S(2)}, u32[]{:S(2)}) collective-permute-start(bf16[6,2,160,128]{3,2,1,0:T(8,128)(2,1)S(1)} %get-tuple-element.22), channel_id=1, source_target_pairs={{2,4},{4,2},{6,8},{8,6},{10,12},{12,10},{14,16},{16,14},{18,20},{2... | collective-permute-start | bytes 1474568 | tf_op jit(solution)/shard_map/ppermute | solution.py:340
  5.9 0.1 collective-permute-start
  5.9 1.2 %collective-permute-done.cols_ref = f32[6,4,2,128]{3,2,1,0:T(2,128)S(1)} collective-permute-done((f32[6,4,2,128]{3,2,1,0:T(2,128)S(1)}, f32[6,4,2,128]{3,2,1,0:T(2,128)S(1)}, u32[]{:S(2)}, u32[]{:S(2)}) %collective-permute-start) | collective-permute-done | bytes 24608 | tf_op jit(solution)/shard_map/ppermute | solution.py:341
  7.1 0.0 copy-done
  7.1 7.3 %begin.1 = (f32[6,4,256,128]{3,2,1,0:T(8,128)S(1)}, f32[5,5,2,6,128]{4,3,2,1,0:T(8,128)S(1)}, bf16[32,512]{1,0:T(8,128)(2,1)S(1)}, bf16[6,2,64,128]{3,2,1,0:T(8,...) custom-call(bf16[6,4,256,128]{3,2,1,0:T(8,128)(2,1)} %f_ref.5, ...), custom_call_target="tpu_custom_call" | custom-call | flops 23592960 | bytes 7864320 | tf_op jit(solution)/shard_map/begin/pallas_call | solution.py:144
  14.4 0.7 %collective-permute-start.3 = (bf16[6,2,64,128]{3,2,1,0:T(8,128)(2,1)S(1)}, bf16[6,2,64,128]{3,2,1,0:T(8,128)(2,1)S(1)}, u32[]{:S(2)}, u32[]{:S(2)}) collective-permute-start(bf16[6,2,64,128]{3,2,1,0:T(8,128)(2,1)S(1)} %get-tuple-element.20), channel_id=1, source_target_pairs={{2,4},{4,2},{6,8},{8,6},{10,12},{12,10},{14,16},{16,14},{18,20},{2... | collective-permute-start | bytes 589832 | tf_op jit(solution)/shard_map/ppermute | solution.py:344
  15.1 5.5 %collective-permute-start.4 = (bf16[6,2,64,128]{3,2,1,0:T(8,128)(2,1)S(1)}, bf16[6,2,64,128]{3,2,1,0:T(8,128)(2,1)S(1)}, u32[]{:S(2)}, u32[]{:S(2)}) collective-permute-start(bf16[6,2,64,128]{3,2,1,0:T(8,128)(2,1)S(1)} %get-tuple-element.21), channel_id=1, source_target_pairs={{0,2},{2,0},{4,6},{6,4},{8,10},{10,8},{12,14},{14,12},{16,18},{18,... | collective-permute-start | bytes 589832 | tf_op jit(solution)/shard_map/ppermute | solution.py:344
  20.6 0.1 collective-permute-start.1
  20.7 9.8 %collective-permute-done.5.a_ref = bf16[6,2,160,128]{3,2,1,0:T(8,128)(2,1)S(1)} collective-permute-done((bf16[6,2,160,128]{3,2,1,0:T(8,128)(2,1)S(1)}, bf16[6,2,160,128]{3,2,1,0:T(8,128)(2,1)S(1)}, u32[]{:S(2)}, u32[]{:S(2)}) %collective-permute-start.5) | collective-permute-done | bytes 491552 | tf_op jit(solution)/shard_map/ppermute | solution.py:340
  30.5 0.7 %collective-permute-start.2 = (bf16[6,2,32,128]{3,2,1,0:T(8,128)(2,1)S(1)}, bf16[6,2,32,128]{3,2,1,0:T(8,128)(2,1)S(1)}, u32[]{:S(2)}, u32[]{:S(2)}) collective-permute-start(bf16[6,2,32,128]{3,2,1,0:T(8,128)(2,1)S(1)} %get-tuple-element.17), channel_id=1, source_target_pairs={{2,4},{4,2},{6,8},{8,6},{10,12},{12,10},{14,16},{16,14},{18,20},{2... | collective-permute-start | bytes 294920 | tf_op jit(solution)/shard_map/ppermute | solution.py:344
  31.1 0.0 collective-permute-done.6.b_ref
  31.1 1.6 %finish.3.refs_0_ = f32[224,128]{1,0:T(8,128)S(1)} custom-call(f32[6,4,256,128]{3,2,1,0:T(8,128)S(1)} %get-tuple-element.15.u_ref, bf16[6,2,160,128]{3,2,1,0:T(8,128)(2,1)S(1)} %collective-permute-done.5.a_ref, bf16[6,2,160,128]{3,2,1,0:T(8,128)(2,1)S(1)} %collective-permute-done.6.b_ref, f32[5,5,2,6,128]{4,3,2,1,0:T(8,128)S(1)} %get-tuple-element.18.w_ref, ...), custom_call_target="tpu_custom_call" | custom-call | flops 9830400 | bytes 3932160 | tf_op jit(solution)/shard_map/finish/pallas_call | solution.py:293
  32.7 0.0 collective-permute-done.3.a_ref
  32.7 4.0 %collective-permute-done.4.b_ref = bf16[6,2,64,128]{3,2,1,0:T(8,128)(2,1)S(1)} collective-permute-done((bf16[6,2,64,128]{3,2,1,0:T(8,128)(2,1)S(1)}, bf16[6,2,64,128]{3,2,1,0:T(8,128)(2,1)S(1)}, u32[]{:S(2)}, u32[]{:S(2)}) %collective-permute-start.4) | collective-permute-done | bytes 196640 | tf_op jit(solution)/shard_map/ppermute | solution.py:344
  36.7 0.8 %finish.4.refs_0_ = f32[224,128]{1,0:T(8,128)S(1)} custom-call(f32[6,4,256,128]{3,2,1,0:T(8,128)S(1)} %get-tuple-element.15.u_ref, bf16[6,2,64,128]{3,2,1,0:T(8,128)(2,1)S(1)} %collective-permute-done.3.a_ref, bf16[6,2,64,128]{3,2,1,0:T(8,128)(2,1)S(1)} %collective-permute-done.4.b_ref, f32[5,5,2,6,128]{4,3,2,1,0:T(8,128)S(1)} %get-tuple-element.18.w_ref, ...), custom_call_target="tpu_custom_call" | custom-call | flops 3932160 | bytes 1572864 | tf_op jit(solution)/shard_map/finish/pallas_call | solution.py:293
  37.5 0.2 collective-permute-done.1.a_ref
  37.7 0.0 collective-permute-done.2.b_ref
  37.7 0.6 %finish.5 = f32[224,128]{1,0:T(8,128)S(1)} custom-call(f32[6,4,256,128]{3,2,1,0:T(8,128)S(1)} %get-tuple-element.15.u_ref, bf16[6,2,32,128]{3,2,1,0:T(8,128)(2,1)S(1)} %collective-permute-done.1.a_ref, bf16[6,2,32,128]{3,2,1,0:T(8,128)(2,1)S(1)} %collective-permute-done.2.b_ref, f32[5,5,2,6,128]{4,3,2,1,0:T(8,128)S(1)} %get-tuple-element.18.w_ref, ...), custom_call_target="tpu_custom_call" | custom-call | flops 1966080 | bytes 786432 | tf_op jit(solution)/shard_map/finish/pallas_call | solution.py:293
  38.3 14.7 %all_to_all.5 = f32[32,1,896]{2,1,0:T(1,128)S(1)} all-to-all(f32[32,1,896]{2,1,0:T(1,128)S(1)} %bitcast.4), channel_id=1, replica_groups=mesh['grp'=1,'gx'=16,'gy'=2] {'gx','gy'}, dimensions={0} | all-to-all | bytes 229376 | tf_op jit(solution)/shard_map/all_to_all | solution.py:349
  53.0 0.7 %gather.1 = f32[6,1,16,128]{3,2,1,0:T(8,128)} custom-call(f32[224,128]{1,0:T(8,128)S(1)} %bitcast.3), custom_call_target="tpu_custom_call" | custom-call | tf_op jit(solution)/shard_map/gather/pallas_call | solution.py:350
Async XLA Ops:
  0.0 7.1 %copy-start = (f32[6,5,5,5]{3,0,2,1:T(8,128)S(1)}, f32[6,5,5,5]{3,0,2,1:T(8,128)}, u32[]{:S(2)}) copy-start(f32[6,5,5,5]{3,0,2,1:T(8,128)} %param.7) | copy-start | bytes 9004
  1.1 29.4 %collective-permute-start.5 = (bf16[6,2,160,128]{3,2,1,0:T(8,128)(2,1)S(1)}, bf16[6,2,160,128]{3,2,1,0:T(8,128)(2,1)S(1)}, u32[]{:S(2)}, u32[]{:S(2)}) collective-permute-start(bf16[6,2,160,128]{3,2,1,0:T(8,128)(2,1)S(1)} %pack.3), channel_id=1, source_target_pairs={{0,2},{2,0},{4,6},{6,4},{8,10},{10,8},{12,14},{14,12},{16,18},{18,... | collective-permute-start | bytes 1474568 | tf_op jit(solution)/shard_map/ppermute | solution.py:340
  5.2 26.0 %collective-permute-start.6 = (bf16[6,2,160,128]{3,2,1,0:T(8,128)(2,1)S(1)}, bf16[6,2,160,128]{3,2,1,0:T(8,128)(2,1)S(1)}, u32[]{:S(2)}, u32[]{:S(2)}) collective-permute-start(bf16[6,2,160,128]{3,2,1,0:T(8,128)(2,1)S(1)} %get-tuple-element.22), channel_id=1, source_target_pairs={{2,4},{4,2},{6,8},{8,6},{10,12},{12,10},{14,16},{16,14},{18,20},{2... | collective-permute-start | bytes 1474568 | tf_op jit(solution)/shard_map/ppermute | solution.py:340
  5.9 1.3 %collective-permute-start = (f32[6,4,2,128]{3,2,1,0:T(2,128)S(1)}, f32[6,4,2,128]{3,2,1,0:T(2,128)S(1)}, u32[]{:S(2)}, u32[]{:S(2)}) collective-permute-start(f32[6,4,2,128]{3,2,1,0:T(2,128)S(1)} %get-tuple-element.14), channel_id=1, source_target_pairs={{0,1},{1,0},{2,3},{3,2},{4,5},{5,4},{6,7},{7,6},{8,9},{9,8},{10,11... | collective-permute-start | bytes 73736 | tf_op jit(solution)/shard_map/ppermute | solution.py:341
  14.4 18.3 %collective-permute-start.3 = (bf16[6,2,64,128]{3,2,1,0:T(8,128)(2,1)S(1)}, bf16[6,2,64,128]{3,2,1,0:T(8,128)(2,1)S(1)}, u32[]{:S(2)}, u32[]{:S(2)}) collective-permute-start(bf16[6,2,64,128]{3,2,1,0:T(8,128)(2,1)S(1)} %get-tuple-element.20), channel_id=1, source_target_pairs={{2,4},{4,2},{6,8},{8,6},{10,12},{12,10},{14,16},{16,14},{18,20},{2... | collective-permute-start | bytes 589832 | tf_op jit(solution)/shard_map/ppermute | solution.py:344
  15.1 21.6 %collective-permute-start.4 = (bf16[6,2,64,128]{3,2,1,0:T(8,128)(2,1)S(1)}, bf16[6,2,64,128]{3,2,1,0:T(8,128)(2,1)S(1)}, u32[]{:S(2)}, u32[]{:S(2)}) collective-permute-start(bf16[6,2,64,128]{3,2,1,0:T(8,128)(2,1)S(1)} %get-tuple-element.21), channel_id=1, source_target_pairs={{0,2},{2,0},{4,6},{6,4},{8,10},{10,8},{12,14},{14,12},{16,18},{18,... | collective-permute-start | bytes 589832 | tf_op jit(solution)/shard_map/ppermute | solution.py:344
  20.6 17.1 %collective-permute-start.1 = (bf16[6,2,32,128]{3,2,1,0:T(8,128)(2,1)S(1)}, bf16[6,2,32,128]{3,2,1,0:T(8,128)(2,1)S(1)}, u32[]{:S(2)}, u32[]{:S(2)}) collective-permute-start(bf16[6,2,32,128]{3,2,1,0:T(8,128)(2,1)S(1)} %get-tuple-element.16), channel_id=1, source_target_pairs={{0,2},{2,0},{4,6},{6,4},{8,10},{10,8},{12,14},{14,12},{16,18},{18,... | collective-permute-start | bytes 294920 | tf_op jit(solution)/shard_map/ppermute | solution.py:344
  30.5 7.3 %collective-permute-start.2 = (bf16[6,2,32,128]{3,2,1,0:T(8,128)(2,1)S(1)}, bf16[6,2,32,128]{3,2,1,0:T(8,128)(2,1)S(1)}, u32[]{:S(2)}, u32[]{:S(2)}) collective-permute-start(bf16[6,2,32,128]{3,2,1,0:T(8,128)(2,1)S(1)} %get-tuple-element.17), channel_id=1, source_target_pairs={{2,4},{4,2},{6,8},{8,6},{10,12},{12,10},{14,16},{16,14},{18,20},{2... | collective-permute-start | bytes 294920 | tf_op jit(solution)/shard_map/ppermute | solution.py:344
